TPU v7x, 256 devices: a whole 4x4x8 slice. The times are simulated.
256 devices in a mesh: wide: 32 (over z, x_lo, core), narrow: 8 (over y, x_hi).
Axes of the slice: x: 4 (x_hi: 2, x_lo: 2; x = x_hi * 2 + x_lo), y: 4, z: 8, core: 2. Of those that a mesh axis runs over, the one named last changes fastest.
Arguments:
- resp_q: bfloat16 [8, 512, 4096], P(None, 'wide', 'narrow'), may hold values from -6 to 6
- resp_k: bfloat16 [8, 512, 4096], P(None, 'wide', 'narrow'), may hold values from -6 to 6
- resp_v: bfloat16 [8, 512, 4096], P(None, 'wide', 'narrow'), may hold values from -6 to 6
- resp_dout: bfloat16 [8, 512, 4096], P(None, 'wide', 'narrow'), may hold values from -6 to 6
- advantage: float32 [8], replicated, may hold values from -4 to 4
- resp_len: int32 [8], replicated, may hold values from 1 to 512, as said below
- prompt_k: bfloat16 [2048, 4096], P(('wide', 'narrow')), may hold values from -6 to 6
- prompt_v: bfloat16 [2048, 4096], P(('wide', 'narrow')), may hold values from -6 to 6
Outputs:
- grad_query: bfloat16 [8, 512, 4096], P(None, 'wide', 'narrow')
- grad_key: bfloat16 [8, 512, 4096], P(None, 'wide', 'narrow')
- grad_value: bfloat16 [8, 512, 4096], P(None, 'wide', 'narrow')
- prompt_grad_key: bfloat16 [2048, 4096], P(('wide', 'narrow'))
- prompt_grad_value: bfloat16 [2048, 4096], P(('wide', 'narrow'))
Inputs may be any that keep to these rules, and one draw needn't show every extreme that they name: `resp_len`: in every draw some response has the full length 512.
All inputs are finite; a program needn't handle non-finite values.
Results may differ from a plain program's by a relative error of at most 0.03.
Values may be sent and summed in bfloat16 or wider, within the bound.
No kernel may reach another device: no remote copies, remote signals or barrier semaphores. Data moves between devices by JAX's collectives and lax.ppermute only.
A program may use at most 256 MiB of HBM per device.

v0:
```python
import jax
import jax.numpy as jnp
from jax import lax
from jax.sharding import PartitionSpec as P

HEADS = 32
HDIM = 128


def backward_local(queries, keys, values, cotangent, weight, query_pos, key_pos, slopes, from_key):
    rows = queries.shape[0]
    total = keys.shape[0]
    heads_here = queries.shape[1] // HDIM
    factor = HDIM ** (-0.5)
    query_heads = queries.reshape(rows, heads_here, HDIM)
    key_heads = keys.reshape(total, heads_here, HDIM)
    value_heads = values.reshape(total, heads_here, HDIM)
    scores = (
        jnp.einsum("qhd,khd->hqk", query_heads, key_heads, preferred_element_type=jnp.float32)
        * factor
    )
    distance = (query_pos[:, None] - key_pos[None, :]).astype(jnp.float32)
    visible = key_pos[None, :] <= query_pos[:, None]
    scores = scores - slopes[:, None, None] * distance[None]
    masked = jnp.where(visible[None], scores, -jnp.inf)
    top = jnp.max(masked, axis=-1, keepdims=True)
    expo = jnp.exp(masked - top)
    summed = jnp.sum(expo, axis=-1, keepdims=True)
    probs = expo / summed
    probs_b = probs.astype(jnp.bfloat16)
    grad_b = (cotangent.astype(jnp.float32) * weight[:, None]).astype(jnp.bfloat16)
    grad_heads = grad_b.reshape(rows, heads_here, HDIM)
    output = jnp.einsum("hqk,khd->qhd", probs_b, value_heads, preferred_element_type=jnp.float32)
    delta = jnp.sum(grad_heads.astype(jnp.float32) * output, axis=-1)
    dprob = jnp.einsum("qhd,khd->hqk", grad_heads, value_heads, preferred_element_type=jnp.float32)
    dscore = (probs * (dprob - delta.T[:, :, None]) * factor).astype(jnp.bfloat16)
    dquery = (
        jnp.einsum("hqk,khd->qhd", dscore, key_heads, preferred_element_type=jnp.float32)
        .reshape(rows, heads_here * HDIM)
        .astype(jnp.bfloat16)
    )
    kept = total - from_key
    dkey = jnp.einsum(
        "hqk,qhd->khd", dscore, query_heads, preferred_element_type=jnp.float32
    ).reshape(kept, heads_here * HDIM)
    dvalue = jnp.einsum(
        "hqk,qhd->khd", probs_b, grad_heads, preferred_element_type=jnp.float32
    ).reshape(kept, heads_here * HDIM)
    return (dquery, dkey, dvalue, top[:, :, 0].T, summed[:, :, 0].T, delta, grad_b)


def body(resp_q, resp_k, resp_v, resp_dout, advantage, resp_len, prompt_k, prompt_v):
    own_pk, own_pv = (
        lax.all_to_all(prompt_k, "narrow", split_axis=1, concat_axis=0, tiled=True),
        lax.all_to_all(prompt_v, "narrow", split_axis=1, concat_axis=0, tiled=True),
    )
    full_pk, full_pv = (
        lax.all_gather(own_pk, "wide", axis=0, tiled=True),
        lax.all_gather(own_pv, "wide", axis=0, tiled=True),
    )
    full_rk, full_rv = (
        lax.all_gather(resp_k, "wide", axis=1, tiled=True),
        lax.all_gather(resp_v, "wide", axis=1, tiled=True),
    )
    prompt_len = full_pk.shape[0]
    resp_total = full_rk.shape[1]
    local_rows = resp_q.shape[1]
    width = resp_q.shape[2]
    head_dev = width // HDIM
    reach = 128.0 / (prompt_len + resp_total)
    head_ids = lax.axis_index("narrow") * head_dev + jnp.arange(head_dev, dtype=jnp.int32)
    slopes = 2.0 ** (-8.0 * (head_ids.astype(jnp.float32) + 1.0) / HEADS) * reach
    first_row = lax.axis_index("wide") * local_rows
    key_pos = jnp.concatenate(
        [
            jnp.arange(prompt_len, dtype=jnp.int32) - prompt_len,
            jnp.arange(resp_total, dtype=jnp.int32),
        ]
    )
    query_pos = first_row + jnp.arange(local_rows, dtype=jnp.int32)
    from_key = 0
    dqueries = []
    terms_k = []
    terms_v = []
    tops = []
    totals = []
    deltas = []
    grads = []
    prompt_terms_k = jnp.zeros((prompt_len, width), jnp.float32)
    prompt_terms_v = jnp.zeros((prompt_len, width), jnp.float32)
    for which in range(resp_q.shape[0]):
        weight = advantage[which] * (query_pos < resp_len[which]).astype(jnp.float32)
        all_keys = jnp.concatenate([full_pk, full_rk[which]], axis=0)
        all_values = jnp.concatenate([full_pv, full_rv[which]], axis=0)
        dquery, dkey, dvalue, top, summed, delta, grad_b = backward_local(
            resp_q[which],
            all_keys,
            all_values,
            resp_dout[which],
            weight,
            query_pos,
            key_pos,
            slopes,
            from_key,
        )
        dqueries.append(dquery)
        terms_k.append(dkey[prompt_len - from_key :])
        terms_v.append(dvalue[prompt_len - from_key :])
        tops.append(top)
        totals.append(summed)
        deltas.append(delta)
        grads.append(grad_b)
        prompt_terms_k = prompt_terms_k + dkey[:prompt_len]
        prompt_terms_v = prompt_terms_v + dvalue[:prompt_len]
    owned_rk, owned_rv = (
        lax.psum_scatter(
            jnp.stack(terms_k).astype(jnp.bfloat16), "wide", scatter_dimension=1, tiled=True
        ).astype(jnp.float32),
        lax.psum_scatter(
            jnp.stack(terms_v).astype(jnp.bfloat16), "wide", scatter_dimension=1, tiled=True
        ).astype(jnp.float32),
    )
    owned_k, owned_v = (
        lax.psum_scatter(
            prompt_terms_k.astype(jnp.bfloat16), "wide", scatter_dimension=0, tiled=True
        ).astype(jnp.float32),
        lax.psum_scatter(
            prompt_terms_v.astype(jnp.bfloat16), "wide", scatter_dimension=0, tiled=True
        ).astype(jnp.float32),
    )
    back_k, back_v = (
        lax.all_to_all(
            owned_k.astype(jnp.bfloat16), "narrow", split_axis=0, concat_axis=1, tiled=True
        ),
        lax.all_to_all(
            owned_v.astype(jnp.bfloat16), "narrow", split_axis=0, concat_axis=1, tiled=True
        ),
    )
    return (
        jnp.stack(dqueries),
        owned_rk.astype(jnp.bfloat16),
        owned_rv.astype(jnp.bfloat16),
        back_k,
        back_v,
    )


def solution(mesh):
    placed = (
        P(None, "wide", "narrow"),
        P(None, "wide", "narrow"),
        P(None, "wide", "narrow"),
        P(None, "wide", "narrow"),
        P(),
        P(),
        P(("wide", "narrow"), None),
        P(("wide", "narrow"), None),
    )
    return jax.shard_map(
        body,
        mesh=mesh,
        in_specs=placed,
        out_specs=(
            P(None, "wide", "narrow"),
            P(None, "wide", "narrow"),
            P(None, "wide", "narrow"),
            P(("wide", "narrow"), None),
            P(("wide", "narrow"), None),
        ),
        check_vma=False,
    )
```

profile of v0, /device:TPU:8, one launch (start us, length us, event | category | flops | bytes accessed | tf_op | source)
XLA Modules:
  0.0 944.2 jit_solution(10547915646876274458)
XLA Ops:
  7.2 13.9 %all_to_all.76 = bf16[8,8,512]{2,0,1:T(8,128)(2,1)} all-to-all(bf16[8,8,512]{2,0,1:T(8,128)(2,1)} %bitcast.316), channel_id=1, replica_groups=mesh['wide'=32,'narrow'=8] {'narrow'}, dimensions={1} | all-to-all | bytes 131072 | tf_op jit(solution)/shard_map/all_to_all | solution.py:54
  21.2 11.8 %all_to_all.77 = bf16[8,8,512]{2,0,1:T(8,128)(2,1)} all-to-all(bf16[8,8,512]{2,0,1:T(8,128)(2,1)} %bitcast.317), channel_id=1, replica_groups=mesh['wide'=32,'narrow'=8] {'narrow'}, dimensions={1} | all-to-all | bytes 131072 | tf_op jit(solution)/shard_map/all_to_all | solution.py:55
  47.2 2.6 compare_select_fusion
  49.8 2.5 compare_select_fusion.2
  52.2 2.4 compare_select_fusion.4
  54.7 2.5 compare_select_fusion.6
  59.2 26.5 %all-gather.5.cloned.1.call-done = bf16[2048,512]{1,0:T(8,128)(2,1)} async-done(((bf16[64,512]{1,0:T(8,128)(2,1)}), bf16[2048,512]{1,0:T(8,128)(2,1)}) %all-gather.5.cloned.1.call-update) | async-done | bytes 2097168 | tf_op jit(solution)/shard_map/all_gather | solution.py:58
  85.8 2.9 copy.203
  88.7 2.5 copy.206
  91.2 60.6 %all-gather.9.cloned.1.call-done = bf16[2048,512]{1,0:T(8,128)(2,1)} async-done(((bf16[64,512]{1,0:T(8,128)(2,1)}), bf16[2048,512]{1,0:T(8,128)(2,1)}) %all-gather.9.cloned.1.call-update) | async-done | bytes 2097168 | tf_op jit(solution)/shard_map/all_gather | solution.py:59
  151.8 2.9 copy.210
  154.7 2.5 copy.213
  157.3 63.6 %all-gather.11.cloned.1.call-done = bf16[8,512,512]{2,0,1:T(8,128)(2,1)} async-done(((bf16[8,16,512]{2,0,1:T(8,128)(2,1)}), bf16[8,512,512]{2,0,1:T(8,128)(2,1)}) %all-gather.11.cloned.1.call-update) | async-done | bytes 4194320 | tf_op jit(solution)/shard_map/all_gather | solution.py:63
  220.8 21.7 %fusion.211 = (bf16[1,512,512]{2,0,1:T(2,128)(2,1)}, bf16[1,512,512]{2,0,1:T(2,128)(2,1)}, bf16[1,512,512]{2,0,1:T(2,128)(2,1)}, bf16[1,512,512]{2,0,1:T(2,128)(...) fusion(bf16[8,512,512]{2,0,1:T(8,128)(2,1)} %all-gather.11.clon, ...), kind=kLoop, calls=%fused_computation.335 | loop fusion | bytes 8388608 | tf_op jit(solution)/shard_map/slice | solution.py:94
  242.5 3.5 copy.320
  248.0 3.5 copy.318
  253.5 3.5 copy.316
  259.1 3.5 copy.314
  264.6 3.5 copy.312
  270.2 2.3 copy.310
  279.1 10.5 %all-gather.7.cloned.1.call-done = bf16[8,512,512]{2,0,1:T(8,128)(2,1)} async-done(((bf16[8,16,512]{2,0,1:T(8,128)(2,1)}), bf16[8,512,512]{2,0,1:T(8,128)(2,1)}) %all-gather.7.cloned.1.call-update) | async-done | bytes 4194320 | tf_op jit(solution)/shard_map/all_gather | solution.py:62
  289.6 21.6 %fusion.210 = (bf16[1,512,512]{2,0,1:T(2,128)(2,1)}, bf16[1,512,512]{2,0,1:T(2,128)(2,1)}, bf16[1,512,512]{2,0,1:T(2,128)(2,1)}, bf16[1,512,512]{2,0,1:T(2,128)(...) fusion(bf16[8,512,512]{2,0,1:T(8,128)(2,1)} %all-gather.7.clone, ...), kind=kLoop, calls=%fused_computation.334 | loop fusion | bytes 8388608 | tf_op jit(solution)/shard_map/slice | solution.py:93
  311.2 3.5 copy.319
  316.7 3.5 copy.317
  322.2 3.5 copy.315
  327.7 3.5 copy.313
  333.2 3.5 copy.311
  338.8 2.3 copy.309
  348.1 2.5 fusion.57
  354.6 3.2 convolution_bitcast_fusion
  357.9 3.0 fusion.114
  360.9 3.3 convolution_bitcast_fusion.1
  364.2 2.8 fusion.115
  370.5 3.2 convolution_bitcast_fusion.2
  373.6 3.1 fusion.116
  379.9 3.3 convolution_bitcast_fusion.3
  383.2 3.0 fusion.117
  389.4 3.3 convolution_bitcast_fusion.4
  392.7 3.0 fusion.118
  399.0 3.2 convolution_bitcast_fusion.5
  402.2 3.0 fusion.119
  405.2 13.5 %fusion.39 = f32[4,16,2560]{2,1,0:T(8,128)S(1)} fusion(bf16[512,4,128]{2,0,1:T(8,128)(2,1)S(1)} %copy-done.20, bf16[2048,4,128]{2,0,1:T(8,128)(2,1)S(1)} %copy-done.3, f32[16,2560]{1,0:T(8,128)S(1)} %copy-done.50, f32[4]{0:T(128)} %power_multiply_fusion, pred[16,2560]{1,0:T(8,128)(4,1)} %broadcast_compare_fusion, bf16[16,4,128]{2,1,0:T(4,128)(2,1)} %reshape_squeeze.25), kind=kOutput, calls=%fused_computation.85 | convolution fusion | flops 47841280 | bytes 3498000 | tf_op jit(solution)/shard_map/qhd,khd->hqk/dot_general | solution.py:19
  419.5 3.2 convolution_bitcast_fusion.6
  422.7 3.0 fusion.120
  429.2 4.0 convolution_bitcast_fusion.7
  433.2 2.3 fusion.121
  435.5 12.2 %fusion.8 = bf16[2048,4,128]{0,2,1:T(8,128)(2,1)S(1)} fusion(f32[2560,4,128]{0,2,1:T(8,128)} %convolution_bitcast_fusion, f32[2560,4,128]{0,2,1:T(8,128)} %convolution_bitcast_fusion.1, f32[2560,4,128]{0,2,1:T(8,128)} %convolution_bitcast_fusion.2, f32[2560,4,128]{0,2,1:T(8,128)} %convolution_bitcast_fusion.3, f32[2560,4,128]{0,2,1:T(8,128)} %convolution_bitcast_fusion.4, ...), kind=kLoop, calls=%fused_computation.25 | loop fusion | flops 8388608 | bytes 35651584 | tf_op jit(solution)/shard_map/convert_element_type | solution.py:128
  447.7 2.5 copy.304
  450.3 2.6 fusion.66
  465.3 3.6 convolution_bitcast_fusion.12
  468.9 3.2 convolution_bitcast_fusion.11
  472.1 3.3 convolution_bitcast_fusion.10
  475.4 3.2 convolution_bitcast_fusion.9
  478.6 3.2 convolution_bitcast_fusion.8
  481.8 8.7 fusion.9
  490.5 2.5 copy.303
  532.1 2.1 slice.510
  560.9 7.8 reduce-scatter.11.cloned.1.call-done
  568.7 6.9 all-to-all-start.3
  575.7 112.1 %reduce-scatter.9.cloned.1.call-done = bf16[64,512]{1,0:T(8,128)(2,1)} async-done(((bf16[2048,512]{1,0:T(8,128)(2,1)}), bf16[64,512]{1,0:T(8,128)(2,1)}) %reduce-scatter.9.cloned.1.call-update) | async-done | bytes 65552 | tf_op jit(solution)/shard_map/reduce_scatter | solution.py:124
  687.8 7.0 all-to-all-start.2
  694.8 6.4 all-to-all-done.2
  701.2 110.3 %reduce-scatter.7.cloned.1.call-done = bf16[8,16,512]{2,1,0:T(8,128)(2,1)} async-done(((bf16[8,512,512]{2,1,0:T(8,128)(2,1)}), bf16[8,16,512]{2,1,0:T(8,128)(2,1)}) %reduce-scatter.7.cloned.1.call-update) | async-done | bytes 131088 | tf_op jit(solution)/shard_map/reduce_scatter | solution.py:119
  811.6 124.2 %reduce-scatter.5.cloned.1.call-done = bf16[8,16,512]{2,1,0:T(8,128)(2,1)} async-done(((bf16[8,512,512]{2,1,0:T(8,128)(2,1)}), bf16[8,16,512]{2,1,0:T(8,128)(2,1)}) %reduce-scatter.5.cloned.1.call-update) | async-done | bytes 131088 | tf_op jit(solution)/shard_map/reduce_scatter | solution.py:116
  (349 shorter events, 150.6 us)
Async XLA Ops:
  7.2 78.6 %all-gather.5.cloned.1.call-start = ((), (), s32[]{:S(2)}) async-start(), calls=%async_computation.8 | async-start | bytes 2162688 | tf_op jit(solution)/shard_map/all_gather | solution.py:58
  21.1 130.7 %all-gather.9.cloned.1.call-start = ((), (), s32[]{:S(2)}) async-start(), calls=%async_computation.10 | async-start | bytes 2162688 | tf_op jit(solution)/shard_map/all_gather | solution.py:59
  33.0 187.8 %all-gather.11.cloned.1.call-start = ((), (), s32[]{:S(2)}) async-start(), calls=%async_computation.11 | async-start | bytes 4325376 | tf_op jit(solution)/shard_map/all_gather | solution.py:63
  34.7 254.9 %all-gather.7.cloned.1.call-start = ((), (), s32[]{:S(2)}) async-start(), calls=%async_computation.9 | async-start | bytes 4325376 | tf_op jit(solution)/shard_map/all_gather | solution.py:62
  36.4 532.3 %reduce-scatter.11.cloned.1.call-start = ((), (), s32[]{:S(2)}) async-start(), calls=%async_computation.15 | async-start | bytes 2162688 | tf_op jit(solution)/shard_map/reduce_scatter | solution.py:127
  59.2 288.9 %copy-start.49 = (f32[16,2560]{1,0:T(8,128)}, f32[16,2560]{1,0:T(8,128)S(1)}, u32[]{:S(2)}) copy-start(f32[16,2560]{1,0:T(8,128)S(1)} %subtract_convert_fusion) | copy-start | bytes 491524
  341.1 7.0 copy-start.28
  348.1 3.6 copy-start.3
  351.7 6.2 copy-start.66
  354.6 9.5 %copy-start.62 = (f32[4,16]{1,0:T(4,128)}, f32[4,16]{1,0:T(4,128)S(1)}, u32[]{:S(2)}) copy-start(f32[4,16]{1,0:T(4,128)S(1)} %get-tuple-element.65) | copy-start | bytes 772
  360.9 3.3 copy-start.34
  364.1 2.8 copy-start.53
  364.2 2.8 copy-start.77
  373.6 3.1 copy-start.25
  373.6 3.1 copy-start.50
  383.2 3.0 copy-start.23
  392.7 3.0 copy-start.22
  402.2 3.0 copy-start.20
  419.5 3.2 copy-start.64
  422.7 3.0 copy-start.60
  425.7 3.5 copy-start.51
  427.6 5.6 copy-start.5
  447.7 2.6 copy-start.18
  450.3 237.5 %reduce-scatter.9.cloned.1.call-start = ((), (), s32[]{:S(2)}) async-start(), calls=%async_computation.14 | async-start | bytes 2162688 | tf_op jit(solution)/shard_map/reduce_scatter | solution.py:124
  453.6 2.0 copy-start.36
  453.6 2.0 copy-start.67
  453.6 2.0 copy-start.84
  454.5 27.2 %copy-start = (f32[2560,4,128]{0,2,1:T(8,128)}, f32[2560,4,128]{0,2,1:T(8,128)S(1)}, u32[]{:S(2)}) copy-start(f32[2560,4,128]{0,2,1:T(8,128)S(1)} %convolution_bitcast_fusion.15) | copy-start | bytes 15728644
  454.6 2.0 copy-start.12
  454.6 2.6 copy-start.35
  454.6 2.5 copy-start.63
  454.6 2.5 copy-start.79
  456.4 22.1 %copy-start.39 = (bf16[4,16,2560]{2,1,0:T(8,128)(2,1)}, bf16[4,16,2560]{2,1,0:T(8,128)(2,1)S(1)}, u32[]{:S(2)}) copy-start(bf16[4,16,2560]{2,1,0:T(8,128)(2,1)S(1)} %fusion.73) | copy-start | bytes 983044
  456.5 1.8 copy-start.33
  457.9 17.4 %copy-start.41 = (bf16[4,16,2560]{2,1,0:T(8,128)(2,1)}, bf16[4,16,2560]{2,1,0:T(8,128)(2,1)S(1)}, u32[]{:S(2)}) copy-start(bf16[4,16,2560]{2,1,0:T(8,128)(2,1)S(1)} %fusion.72) | copy-start | bytes 983044
  459.1 13.0 %copy-start.42 = (bf16[4,16,2560]{2,1,0:T(8,128)(2,1)}, bf16[4,16,2560]{2,1,0:T(8,128)(2,1)S(1)}, u32[]{:S(2)}) copy-start(bf16[4,16,2560]{2,1,0:T(8,128)(2,1)S(1)} %fusion.71) | copy-start | bytes 983044
  460.2 8.8 copy-start.44
  461.3 3.9 copy-start.45
  462.4 1.9 copy-start.47
  463.4 1.9 copy-start.48
  463.4 1.8 copy-start.56
  464.3 17.5 %copy-start.1 = (f32[2560,4,128]{0,2,1:T(8,128)}, f32[2560,4,128]{0,2,1:T(8,128)S(1)}, u32[]{:S(2)}) copy-start(f32[2560,4,128]{0,2,1:T(8,128)S(1)} %convolution_bitcast_fusion.14) | copy-start | bytes 15728644
  464.3 4.6 copy-start.55
  465.3 16.5 %copy-start.2 = (f32[2560,4,128]{0,2,1:T(8,128)}, f32[2560,4,128]{0,2,1:T(8,128)S(1)}, u32[]{:S(2)}) copy-start(f32[2560,4,128]{0,2,1:T(8,128)S(1)} %convolution_bitcast_fusion.13) | copy-start | bytes 15728644
  465.3 6.8 copy-start.54
  468.9 6.4 copy-start.57
  472.1 6.5 copy-start.52
  493.0 318.5 %reduce-scatter.7.cloned.1.call-start = ((), (), s32[]{:S(2)}) async-start(), calls=%async_computation.13 | async-start | bytes 4325376 | tf_op jit(solution)/shard_map/reduce_scatter | solution.py:119
  507.9 2.7 copy-start.9
  522.2 413.5 %reduce-scatter.5.cloned.1.call-start = ((), (), s32[]{:S(2)}) async-start(), calls=%async_computation.12 | async-start | bytes 4325376 | tf_op jit(solution)/shard_map/reduce_scatter | solution.py:116
  536.5 3.6 copy-start.10
  536.7 3.6 copy-start.11
  540.3 4.4 copy-start.8
  540.4 5.3 copy-start.7
  544.8 3.4 copy-start.4
  544.8 3.4 copy-start.40
  549.8 3.2 copy-start.26
  551.4 3.2 copy-start.24
  554.5 4.2 copy-start.21
  555.1 5.2 copy-start.19
  555.1 5.2 copy-start.38
  568.7 119.1 %all-to-all-start.3 = ((bf16[8,8,512]{2,1,0:T(8,128)(2,1)}), bf16[8,8,512]{2,1,0:T(8,128)(2,1)S(1)}, u32[]{:S(2)}, u32[]{:S(2)}) async-start(bf16[8,8,512]{2,1,0:T(8,128)(2,1)} %bitcast.318), calls=%async_computation.7 | async-start | bytes 131072 | tf_op jit(solution)/shard_map/all_to_all | solution.py:135
  687.8 13.4 %all-to-all-start.2 = ((bf16[8,8,512]{2,1,0:T(8,128)(2,1)}), bf16[8,8,512]{2,1,0:T(8,128)(2,1)S(1)}, u32[]{:S(2)}, u32[]{:S(2)}) async-start(bf16[8,8,512]{2,1,0:T(8,128)(2,1)} %bitcast.319), calls=%async_computation.5 | async-start | bytes 131072 | tf_op jit(solution)/shard_map/all_to_all | solution.py:132
  694.8 242.2 %copy-start.76 = (bf16[8,16,512]{2,1,0:T(8,128)(2,1)}, bf16[8,16,512]{2,1,0:T(8,128)(2,1)S(1)}, u32[]{:S(2)}) copy-start(bf16[8,16,512]{2,1,0:T(8,128)(2,1)S(1)} %constant_dynamic-update-slice_fusion) | copy-start | bytes 393220
  (31 other events, 39.4 us)
Sparse Core Ops, SparseCore 0:
  21.2 64.4 all-gather.4
  87.6 64.1 all-gather.8
  154.2 66.5 all-gather.10
  223.1 66.4 all-gather.6
  450.4 118.3 reduce-scatter.10
  571.3 116.4 reduce-scatter.8
  690.9 120.6 reduce-scatter.6
  814.7 121.0 reduce-scatter.4
where the time goes:
time: 958 us; the launch traced here: 944 us
  waiting for transfers between devices  522 us (54%)
  local copies, waits for them, and re-layouts  209 us (22%)
  matrix products  114 us (12%)
  other arithmetic  43.2 us (5%)
  blocking collectives  25.7 us (3%)
  between operations  15.7 us (2%)
  starting transfers between devices  14.5 us (2%)
    reduce_scatter x1, waiting for transfers between devices, body(): lax.psum_scatter(jnp.stack(terms_k).astype(jnp.bfloat16), 'wide', scatter...  124 us
    reduce_scatter x1, waiting for transfers between devices, body(): lax.psum_scatter(prompt_terms_k.astype(jnp.bfloat16), 'wide', scatter_dim...  112 us
    reduce_scatter x1, waiting for transfers between devices, body(): lax.psum_scatter(jnp.stack(terms_v).astype(jnp.bfloat16), 'wide', scatter...  110 us
    unnamed x211, local copies, waits for them, and re-layouts  70.6 us
    all_gather x1, waiting for transfers between devices, body(): lax.all_gather(resp_v, 'wide', axis=1, tiled=True)  63.6 us
    all_gather x1, waiting for transfers between devices, body(): lax.all_gather(own_pv, 'wide', axis=0, tiled=True)  60.6 us
    dot_general x8, matrix products, backward_local(): jnp.einsum('hqk,qhd->khd', probs_b, grad_heads, preferred_element_type=jn...  26.7 us
    all_gather x1, waiting for transfers between devices, body(): lax.all_gather(own_pk, 'wide', axis=0, tiled=True)  26.5 us
  transfers between devices with their start and end apart: 10, of which 9 were waited for; matrix products, arithmetic and copies ran while one was open for 21% of the time, Pallas kernels for 0%

commit v1 on v0

v1 whole, which is shorter than its diff:
```python
import functools

import jax
import jax.numpy as jnp
from jax import lax
from jax.experimental import pallas as pl
from jax.experimental.pallas import tpu as pltpu
from jax.sharding import Mesh, PartitionSpec as P

HEADS = 32
HDIM = 128
RESPONSES = 8
RESP = 512
PROMPT = 2048
BLOCK = 16
CHUNK = 256
LOG2E = 1.4426950408889634
F32 = jnp.float32
BF16 = jnp.bfloat16

AXES = ("zh", "zl", "x", "core", "narrow")
WIDE = ("zh", "zl", "x", "core")
GROUP = ("zl", "x", "core")

VMEM = pl.BlockSpec(memory_space=pltpu.VMEM)
SMEM = pl.BlockSpec(memory_space=pltpu.SMEM)
PARAMS = pltpu.CompilerParams(vmem_limit_bytes=48 * 1024 * 1024)


def pack_prompt_kernel(k_ref, v_ref, out_ref):
    keys = k_ref[...].astype(F32)
    values = v_ref[...].astype(F32)
    for zh in range(4):
        for n in range(8):
            cols = slice((n * 4 + zh) * HDIM, (n * 4 + zh + 1) * HDIM)
            both = jnp.concatenate([keys[:, cols], values[:, cols]], axis=0)
            both = both.astype(BF16)
            out_ref[zh * 16 + n] = both
            out_ref[zh * 16 + 8 + n] = both


def pack_resp_kernel(q_ref, k_ref, v_ref, o_ref, out_ref):
    for h in range(4):
        for r in range(RESPONSES):
            for i, ref in enumerate((q_ref, k_ref, v_ref, o_ref)):
                out_ref[h * 8 + r, i * BLOCK : (i + 1) * BLOCK, :] = ref[
                    r, :, h * HDIM : (h + 1) * HDIM
                ]


def dot(a, b, ca, cb):
    return lax.dot_general(a, b, (((ca,), (cb,)), ((), ())), preferred_element_type=F32)


def attn_kernel(
    adv_ref, len_ref, resp_ref, p00_ref, p01_ref, p10_ref, p11_ref,
    mine_ref, keep_ref, send_ref,
    k_s, v_s, t_s, d_s,
):
    me = lax.axis_index(GROUP)
    core = lax.axis_index("core")
    x = lax.axis_index("x")
    parts = ((p00_ref, p01_ref), (p10_ref, p11_ref))
    head = lax.axis_index("narrow") * 4 + lax.axis_index("zh")
    factor = HDIM ** -0.5
    n_prompt = PROMPT // CHUNK
    n_chunks = (PROMPT + RESP) // CHUNK

    queries = resp_ref[:, 0:BLOCK, :].reshape(RESP, HDIM)
    k_s[PROMPT:, :] = resp_ref[:, BLOCK : 2 * BLOCK, :].reshape(RESP, HDIM)
    v_s[PROMPT:, :] = resp_ref[:, 2 * BLOCK : 3 * BLOCK, :].reshape(RESP, HDIM)
    gain = adv_ref[me]
    length = len_ref[me]
    row = lax.broadcasted_iota(jnp.int32, (RESP, HDIM), 0)
    weight = jnp.where(row < length, gain, 0.0)
    cot = resp_ref[:, 3 * BLOCK : 4 * BLOCK, :].reshape(RESP, HDIM)
    grad = (cot.astype(F32) * weight).astype(BF16)

    power = jnp.full((8, HDIM), head + 1, jnp.int32).astype(F32) * (-8.0 / HEADS)
    slope = (jnp.exp2(power) * (128.0 / (PROMPT + RESP) * LOG2E))[0:1, :]
    key_row = lax.broadcasted_iota(jnp.int32, (CHUNK, HDIM), 0)
    prompt_row = ((key_row // 64) * 256 + key_row % 64 - PROMPT).astype(F32)
    resp_row = key_row.astype(F32)

    def wide4(x):
        return jnp.concatenate([x] * 4, axis=1)

    top = jnp.full((8, RESP), -jnp.inf, F32)
    for c in range(n_chunks):
        rows = slice(c * CHUNK, (c + 1) * CHUNK)
        if c < n_prompt:
            dc, dx, half = c % 2, (c // 2) % 2, c // 4
            both = parts[dc][dx][half * 32 : (half + 1) * 32].astype(F32)
            place = half * 1024 + jnp.bitwise_xor(x, dx) * 128 + jnp.bitwise_xor(core, dc) * 64
            k_s[rows, :] = both[:, 0:8, :].reshape(CHUNK, HDIM).astype(BF16)
            v_s[rows, :] = both[:, 8:16, :].reshape(CHUNK, HDIM).astype(BF16)
            bias = slope * (prompt_row + place.astype(F32))
        else:
            bias = slope * (resp_row + float((c - n_prompt) * CHUNK))
        scores = dot(k_s[rows, :], queries, 1, 1)
        t = scores * (factor * LOG2E) + wide4(bias)
        if c >= n_prompt:
            key_pos = lax.broadcasted_iota(jnp.int32, (CHUNK, RESP), 0) + (c - n_prompt) * CHUNK
            query_pos = lax.broadcasted_iota(jnp.int32, (CHUNK, RESP), 1)
            t = jnp.where(key_pos <= query_pos, t, -jnp.inf)
        t_s[rows, :] = t
        top = jnp.maximum(top, jnp.max(t.reshape(CHUNK // 8, 8, RESP), axis=0))
    top = jnp.max(top, axis=0, keepdims=True)

    total = jnp.zeros((8, RESP), F32)
    delta = jnp.zeros((8, RESP), F32)
    for c in range(n_chunks):
        rows = slice(c * CHUNK, (c + 1) * CHUNK)
        p = jnp.exp2(t_s[rows, :] - top)
        t_s[rows, :] = p
        dp = dot(v_s[rows, :], grad, 1, 1)
        d_s[rows, :] = dp
        total = total + jnp.sum(p.reshape(CHUNK // 8, 8, RESP), axis=0)
        delta = delta + jnp.sum((p * dp).reshape(CHUNK // 8, 8, RESP), axis=0)
    inv = 1.0 / jnp.sum(total, axis=0, keepdims=True)
    delta = jnp.sum(delta, axis=0, keepdims=True) * inv

    dq = jnp.zeros((HDIM, RESP), F32)
    for c in range(n_chunks):
        rows = slice(c * CHUNK, (c + 1) * CHUNK)
        p = t_s[rows, :] * inv
        ds = (p * (d_s[rows, :] - delta)).astype(BF16)
        dv = dot(p.astype(BF16), grad, 1, 0)
        dk = dot(ds, queries, 1, 0) * factor
        dq = dq + dot(k_s[rows, :], ds, 0, 0)
        if c < n_prompt:
            both = jnp.concatenate(
                [dk.reshape(CHUNK // 8, 8, HDIM), dv.reshape(CHUNK // 8, 8, HDIM)], axis=1
            ).astype(BF16)
            out = send_ref if c % 2 else keep_ref
            half = c // 4
            out[(c // 2) % 2, half * 32 : (half + 1) * 32] = both
        else:
            part = slice((c - n_prompt) * 16, (c - n_prompt + 1) * 16)
            mine_ref[part, BLOCK : 2 * BLOCK, :] = dk.reshape(16, BLOCK, HDIM).astype(BF16)
            mine_ref[part, 2 * BLOCK : 3 * BLOCK, :] = dv.reshape(16, BLOCK, HDIM).astype(BF16)
    dq = (dq * factor).T
    mine_ref[:, 0:BLOCK, :] = dq.reshape(32, BLOCK, HDIM).astype(BF16)


def add_core_kernel(keep_ref, got_ref, next_ref, send_ref):
    next_ref[...] = (keep_ref[0].astype(F32) + got_ref[0].astype(F32)).astype(BF16)
    send_ref[...] = (keep_ref[1].astype(F32) + got_ref[1].astype(F32)).astype(BF16)


def add_x_kernel(keep_ref, got_ref, out_ref):
    out_ref[...] = (keep_ref[...].astype(F32) + got_ref[...].astype(F32)).astype(BF16)


def unpack_resp_kernel(got_ref, q_ref, k_ref, v_ref):
    for h in range(4):
        for r in range(RESPONSES):
            for i, ref in enumerate((q_ref, k_ref, v_ref)):
                ref[r, :, h * HDIM : (h + 1) * HDIM] = got_ref[
                    h * 8 + r, i * BLOCK : (i + 1) * BLOCK, :
                ]


def unpack_prompt_kernel(got_ref, k_ref, v_ref):
    for zh in range(4):
        for n in range(8):
            cols = slice((n * 4 + zh) * HDIM, (n * 4 + zh + 1) * HDIM)
            both = got_ref[zh * 2, n].astype(F32) + got_ref[zh * 2 + 1, n].astype(F32)
            k_ref[:, cols] = both[0:8].astype(BF16)
            v_ref[:, cols] = both[8:16].astype(BF16)


def call(kernel, outs, n_in, scratch=(), smem=0, flops=0, bytes_accessed=1 << 20):
    return pl.pallas_call(
        kernel,
        out_shape=[jax.ShapeDtypeStruct(s, BF16) for s in outs],
        in_specs=[SMEM] * smem + [VMEM] * n_in,
        out_specs=[VMEM] * len(outs),
        scratch_shapes=list(scratch),
        compiler_params=PARAMS,
        cost_estimate=pl.CostEstimate(
            flops=flops, bytes_accessed=bytes_accessed, transcendentals=0
        ),
    )


def body(resp_q, resp_k, resp_v, resp_dout, advantage, resp_len, prompt_k, prompt_v):
    swap = [(0, 1), (1, 0)]
    (sent_p,) = call(pack_prompt_kernel, [(64, 16, HDIM)], 2)(prompt_k, prompt_v)
    p00 = lax.all_to_all(sent_p, ("zh", "zl", "narrow"), 0, 0, tiled=True)
    p01 = lax.ppermute(p00, "x", swap)
    p10 = lax.ppermute(p00, "core", swap)
    p11 = lax.ppermute(p01, "core", swap)
    (sent_r,) = call(pack_resp_kernel, [(32, 4 * BLOCK, HDIM)], 4)(
        resp_q, resp_k, resp_v, resp_dout
    )
    got_r = lax.all_to_all(sent_r, WIDE, 0, 0, tiled=True)

    keys = PROMPT + RESP
    mine, keep, send = call(
        attn_kernel,
        [(32, 3 * BLOCK, HDIM), (2, 64, 16, HDIM), (2, 64, 16, HDIM)],
        5,
        scratch=[
            pltpu.VMEM((keys, HDIM), BF16),
            pltpu.VMEM((keys, HDIM), BF16),
            pltpu.VMEM((keys, RESP), F32),
            pltpu.VMEM((keys, RESP), F32),
        ],
        smem=2,
        flops=5 * 2 * keys * RESP * HDIM,
        bytes_accessed=3 << 20,
    )(advantage, resp_len, got_r, p00, p01, p10, p11)

    got = lax.ppermute(send, "core", swap)
    keep, send = call(add_core_kernel, [(64, 16, HDIM)] * 2, 2)(keep, got)
    got = lax.ppermute(send, "x", swap)
    mine, _ = lax.optimization_barrier((mine, send))
    back = lax.all_to_all(mine, WIDE, 0, 0, tiled=True)
    (owned,) = call(add_x_kernel, [(64, 16, HDIM)], 2)(keep, got)
    owned, _ = lax.optimization_barrier((owned, back))
    owned = lax.all_to_all(owned, ("zh", "zl", "narrow"), 0, 0, tiled=True)
    grad_q, grad_k, grad_v = call(unpack_resp_kernel, [(RESPONSES, BLOCK, 4 * HDIM)] * 3, 1)(back)
    prompt_gk, prompt_gv = call(unpack_prompt_kernel, [(8, HEADS * HDIM)] * 2, 1)(
        owned.reshape(8, 8, 16, HDIM)
    )
    return grad_q, grad_k, grad_v, prompt_gk, prompt_gv


def solution(mesh):
    fine = Mesh(mesh.devices.reshape(4, 2, 2, 2, 8), AXES)
    resp = P(None, WIDE, "narrow")
    prompt = P(AXES, None)
    return jax.shard_map(
        body,
        mesh=fine,
        in_specs=(resp, resp, resp, resp, P(), P(), prompt, prompt),
        out_specs=(resp, resp, resp, prompt, prompt),
        check_vma=False,
    )
```

time: 958 us -> 104 us (0.11); the launches traced: 944 us -> 104 us
  waiting for transfers between devices: 522 us -> 55.7 us
  local copies, waits for them, and re-layouts: 209 us -> 1.69 us
  matrix products: 114 us -> 0 us
  other arithmetic: 43.2 us -> 0 us
  blocking collectives: 25.7 us -> 0 us
  starting transfers between devices: 14.5 us -> 35.6 us
  between operations: 15.7 us -> 0.73 us
  Pallas kernels: 0 us -> 10.2 us
    reduce_scatter x4 -> x0, waiting for transfers between devices: 354 us -> none  [the longest x1 124 us: body(): lax.psum_scatter(jnp.stack(terms_k).astype(jnp.bfloat16), 'wide', scatter...]
    all_gather x4 -> x0, waiting for transfers between devices: 161 us -> none  [the longest x1 63.6 us: body(): lax.all_gather(resp_v, 'wide', axis=1, tiled=True)]
    dot_general x48 -> x0, matrix products: 114 us -> none  [the longest x8 26.7 us: backward_local(): jnp.einsum('hqk,qhd->khd', probs_b, grad_heads, preferred_element_type=jn...]
    slice x21 -> x0, local copies, waits for them, and re-layouts: 72.9 us -> none  [the longest x1 21.7 us: body(): all_values = jnp.concatenate([full_pv, full_rv[which]], axis=0)]
    unnamed x211 -> x16, local copies, waits for them, and re-layouts: 70.6 us -> 1.69 us
    concatenate x18 -> x0, local copies, waits for them, and re-layouts: 33.8 us -> none  [the longest x9 16.9 us: body(): all_keys = jnp.concatenate([full_pk, full_rk[which]], axis=0)]
    all_to_all x2 -> x0, blocking collectives: 25.7 us -> none  [the longest x1 13.9 us: body(): lax.all_to_all(prompt_k, 'narrow', split_axis=1, concat_axis=0, tiled=True)]
    all_to_all x2 -> x4, waiting for transfers between devices: 6.39 us -> 32 us  [the longest x1 12.5 us: body(): p00 = lax.all_to_all(sent_p, ('zh', 'zl', 'narrow'), 0, 0, tiled=True)]
  transfers between devices with their start and end apart: 10 -> 9, of which waited for: 9 -> 7; matrix products, arithmetic and copies ran while one was open for 21% -> 0% of each run, Pallas kernels for 0% -> 2%
where the time goes in v1:
time: 104 us
  waiting for transfers between devices  55.7 us (54%)
  starting transfers between devices  35.6 us (34%)
  Pallas kernels  10.2 us (10%)
  local copies, waits for them, and re-layouts  1.69 us (2%)
    all_to_all x1, starting transfers between devices, body(): p00 = lax.all_to_all(sent_p, ('zh', 'zl', 'narrow'), 0, 0, tiled=True)  14.7 us
    all_to_all x1, waiting for transfers between devices, body(): p00 = lax.all_to_all(sent_p, ('zh', 'zl', 'narrow'), 0, 0, tiled=True)  12.5 us
    all_to_all x1, waiting for transfers between devices, body(): owned = lax.all_to_all(owned, ('zh', 'zl', 'narrow'), 0, 0, tiled=True)  12.4 us
    ppermute x1, waiting for transfers between devices, body(): p01 = lax.ppermute(p00, 'x', swap)  11.2 us
    ppermute x1, waiting for transfers between devices, body(): got = lax.ppermute(send, 'x', swap)  10.6 us
    all_to_all x1, starting transfers between devices, body(): owned = lax.all_to_all(owned, ('zh', 'zl', 'narrow'), 0, 0, tiled=True)  8.64 us
    pallas_call x1, Pallas kernels, body(): call(attn_kernel, [(32, 3 * BLOCK, HDIM), (2, 64, 16, HDIM), (2, 64, 16,...  6.21 us
    all_to_all x1, waiting for transfers between devices, body(): got_r = lax.all_to_all(sent_r, WIDE, 0, 0, tiled=True)  5.08 us
  transfers between devices with their start and end apart: 9, of which 7 were waited for; matrix products, arithmetic and copies ran while one was open for 0% of the time, Pallas kernels for 2%

profile of v1, /device:TPU:8, one launch (start us, length us, event | category | flops | bytes accessed | tf_op | source)
XLA Modules:
  0.0 103.9 jit_solution(10754574340116320723)
XLA Ops:
  0.6 0.0 copy-start.4
  0.6 0.8 copy-done.4
  1.5 0.0 copy-start.5
  1.5 0.8 copy-done.5
  2.3 0.7 shard_map.120
  3.0 0.0 copy-start
  3.1 0.0 copy-start.1
  3.1 0.0 copy-start.2
  3.1 0.0 copy-start.3
  3.1 14.7 %all-to-all-start.1 = ((bf16[64,16,128]{2,1,0:T(8,128)(2,1)}), bf16[64,16,128]{2,1,0:T(8,128)(2,1)S(1)}, u32[]{:S(2)}, u32[]{:S(2)}) async-start(bf16[64,16,128]{2,1,0:T(8,128)(2,1)} %shard_map.120), calls=%async_computation.1 | async-start | bytes 524288 | tf_op jit(solution)/shard_map/all_to_all | solution.py:190
  17.8 0.0 copy-done
  17.8 0.0 copy-done.1
  17.8 0.0 copy-done.2
  17.8 0.0 copy-done.3
  17.8 0.9 shard_map.119
  18.7 0.0 copy-start.6
  18.7 0.0 copy-start.7
  18.7 12.5 %all-to-all-done.1.p00_ref = bf16[64,16,128]{2,1,0:T(8,128)(2,1)S(1)} async-done(((bf16[64,16,128]{2,1,0:T(8,128)(2,1)}), bf16[64,16,128]{2,1,0:T(8,128)(2,1)S(1)}, u32[]{:S(2)}, u32[]{:S(2)}) %all-to-all-start.1) | async-done | bytes 262176 | tf_op jit(solution)/shard_map/all_to_all | solution.py:190
  31.2 3.9 %all-to-all-start = ((bf16[32,64,128]{2,1,0:T(8,128)(2,1)}), bf16[32,64,128]{2,1,0:T(8,128)(2,1)S(1)}, u32[]{:S(2)}, u32[]{:S(2)}) async-start(bf16[32,64,128]{2,1,0:T(8,128)(2,1)} %shard_map.119), calls=%async_computation | async-start | bytes 1048576 | tf_op jit(solution)/shard_map/all_to_all | solution.py:197
  35.1 1.8 %collective-permute-start = (bf16[64,16,128]{2,1,0:T(8,128)(2,1)S(1)}, bf16[64,16,128]{2,1,0:T(8,128)(2,1)S(1)}, u32[]{:S(2)}, u32[]{:S(2)}) collective-permute-start(bf16[64,16,128]{2,1,0:T(8,128)(2,1)S(1)} %all-to-all-done.1.p00_ref), channel_id=1, source_target_pairs={{0,16},{16,0},{1,17},{17,1},{2,18},{18,2},{3,19},{19,3},{4,20},{20... | collective-permute-start | bytes 786440 | tf_op jit(solution)/shard_map/ppermute | solution.py:191
  36.9 0.0 collective-permute-start.1
  36.9 11.2 %collective-permute-done.p01_ref = bf16[64,16,128]{2,1,0:T(8,128)(2,1)S(1)} collective-permute-done((bf16[64,16,128]{2,1,0:T(8,128)(2,1)S(1)}, bf16[64,16,128]{2,1,0:T(8,128)(2,1)S(1)}, u32[]{:S(2)}, u32[]{:S(2)}) %collective-permute-start) | collective-permute-done | bytes 262176 | tf_op jit(solution)/shard_map/ppermute | solution.py:191
  48.1 0.0 collective-permute-start.2
  48.1 0.0 collective-permute-done.1.p10_ref
  48.1 5.1 %all-to-all-done.resp_ref = bf16[32,64,128]{2,1,0:T(8,128)(2,1)S(1)} async-done(((bf16[32,64,128]{2,1,0:T(8,128)(2,1)}), bf16[32,64,128]{2,1,0:T(8,128)(2,1)S(1)}, u32[]{:S(2)}, u32[]{:S(2)}) %all-to-all-start) | async-done | bytes 524320 | tf_op jit(solution)/shard_map/all_to_all | solution.py:197
  53.1 0.0 collective-permute-done.2.p11_ref
  53.1 0.0 copy-done.6
  53.1 0.0 copy-done.7
  53.2 6.2 %shard_map.121 = (bf16[32,48,128]{2,1,0:T(8,128)(2,1)}, bf16[2,64,16,128]{3,2,1,0:T(8,128)(2,1)S(1)}, bf16[2,64,16,128]{3,2,1,0:T(8,128)(2,1)S(1)}) custom-call(f32[8]{0:T(128)S(1)} %copy-done.6, s32[8]{0:T(128)S(1)} %copy-done.7, bf16[32,64,128]{2,1,0:T(8,128)(2,1)S(1)} %all-to-all-done.resp_ref, bf16[64,16,128]{2,1,0:T(8,128)(2,1)S(1)} %all-to-all-done.1.p00_ref, ...), custom_call_target="tpu_custom_call" | custom-call | flops 1677721600 | bytes 3145728 | tf_op jit(solution)/shard_map/pallas_call | solution.py:200
  59.4 0.0 collective-permute-start.3
  59.4 1.9 %collective-permute-done.3.got_ref = bf16[2,64,16,128]{3,2,1,0:T(8,128)(2,1)S(1)} collective-permute-done((bf16[2,64,16,128]{3,2,1,0:T(8,128)(2,1)S(1)}, bf16[2,64,16,128]{3,2,1,0:T(8,128)(2,1)S(1)}, u32[]{:S(2)}, u32[]{:S(2)}) %collective-permute-start.3) | collective-permute-done | bytes 524320 | tf_op jit(solution)/shard_map/ppermute | solution.py:215
  61.3 0.1 shard_map.122
  61.4 4.7 %all-to-all-start.2 = ((bf16[32,48,128]{2,1,0:T(8,128)(2,1)}), bf16[32,48,128]{2,1,0:T(8,128)(2,1)S(1)}, u32[]{:S(2)}, u32[]{:S(2)}) async-start(bf16[32,48,128]{2,1,0:T(8,128)(2,1)} %get-tuple-element.21), calls=%async_computation.2 | async-start | bytes 786432 | tf_op jit(solution)/shard_map/all_to_all | solution.py:219
  66.1 1.9 %collective-permute-start.4 = (bf16[64,16,128]{2,1,0:T(8,128)(2,1)S(1)}, bf16[64,16,128]{2,1,0:T(8,128)(2,1)S(1)}, u32[]{:S(2)}, u32[]{:S(2)}) collective-permute-start(bf16[64,16,128]{2,1,0:T(8,128)(2,1)S(1)} %get-tuple-element.20), channel_id=1, source_target_pairs={{0,16},{16,0},{1,17},{17,1},{2,18},{18,2},{3,19},{19,3},{4,20},{20... | collective-permute-start | bytes 786440 | tf_op jit(solution)/shard_map/ppermute | solution.py:217
  68.0 10.6 %collective-permute-done.4.got_ref = bf16[64,16,128]{2,1,0:T(8,128)(2,1)S(1)} collective-permute-done((bf16[64,16,128]{2,1,0:T(8,128)(2,1)S(1)}, bf16[64,16,128]{2,1,0:T(8,128)(2,1)S(1)}, u32[]{:S(2)}, u32[]{:S(2)}) %collective-permute-start.4) | collective-permute-done | bytes 262176 | tf_op jit(solution)/shard_map/ppermute | solution.py:217
  78.5 0.8 shard_map.124
  79.3 2.0 %all-to-all-done.2.got_ref = bf16[32,48,128]{2,1,0:T(8,128)(2,1)S(1)} async-done(((bf16[32,48,128]{2,1,0:T(8,128)(2,1)}), bf16[32,48,128]{2,1,0:T(8,128)(2,1)S(1)}, u32[]{:S(2)}, u32[]{:S(2)}) %all-to-all-start.2) | async-done | bytes 393248 | tf_op jit(solution)/shard_map/all_to_all | solution.py:219
  81.3 8.6 %all-to-all-start.3 = ((bf16[64,16,128]{2,1,0:T(8,128)(2,1)}), bf16[64,16,128]{2,1,0:T(8,128)(2,1)S(1)}, u32[]{:S(2)}, u32[]{:S(2)}) async-start(bf16[64,16,128]{2,1,0:T(8,128)(2,1)} %shard_map.124), calls=%async_computation.3 | async-start | bytes 524288 | tf_op jit(solution)/shard_map/all_to_all | solution.py:222
  90.0 0.8 shard_map.123
  90.8 12.4 %all-to-all-done.3 = bf16[64,16,128]{2,1,0:T(8,128)(2,1)S(1)} async-done(((bf16[64,16,128]{2,1,0:T(8,128)(2,1)}), bf16[64,16,128]{2,1,0:T(8,128)(2,1)S(1)}, u32[]{:S(2)}, u32[]{:S(2)}) %all-to-all-start.3) | async-done | bytes 262176 | tf_op jit(solution)/shard_map/all_to_all | solution.py:222
  103.2 0.7 shard_map.125
Async XLA Ops:
  0.6 0.8 copy-start.4
  1.5 0.8 copy-start.5
  3.0 14.7 %copy-start = (bf16[8,16,512]{2,1,0:T(8,128)(2,1)S(1)}, bf16[8,16,512]{2,1,0:T(8,128)(2,1)}, u32[]{:S(2)}) copy-start(bf16[8,16,512]{2,1,0:T(8,128)(2,1)} %q_ref.1) | copy-start | bytes 393220
  3.1 14.7 %copy-start.1 = (bf16[8,16,512]{2,1,0:T(8,128)(2,1)S(1)}, bf16[8,16,512]{2,1,0:T(8,128)(2,1)}, u32[]{:S(2)}) copy-start(bf16[8,16,512]{2,1,0:T(8,128)(2,1)} %k_ref.2) | copy-start | bytes 393220
  3.1 14.7 %copy-start.2 = (bf16[8,16,512]{2,1,0:T(8,128)(2,1)S(1)}, bf16[8,16,512]{2,1,0:T(8,128)(2,1)}, u32[]{:S(2)}) copy-start(bf16[8,16,512]{2,1,0:T(8,128)(2,1)} %v_ref.2) | copy-start | bytes 393220
  3.1 14.7 %copy-start.3 = (bf16[8,16,512]{2,1,0:T(8,128)(2,1)S(1)}, bf16[8,16,512]{2,1,0:T(8,128)(2,1)}, u32[]{:S(2)}) copy-start(bf16[8,16,512]{2,1,0:T(8,128)(2,1)} %o_ref.1) | copy-start | bytes 393220
  3.1 28.2 %all-to-all-start.1 = ((bf16[64,16,128]{2,1,0:T(8,128)(2,1)}), bf16[64,16,128]{2,1,0:T(8,128)(2,1)S(1)}, u32[]{:S(2)}, u32[]{:S(2)}) async-start(bf16[64,16,128]{2,1,0:T(8,128)(2,1)} %shard_map.120), calls=%async_computation.1 | async-start | bytes 524288 | tf_op jit(solution)/shard_map/all_to_all | solution.py:190
  18.7 34.4 %copy-start.6 = (f32[8]{0:T(128)S(1)}, f32[8]{0:T(128)}, u32[]{:S(2)}) copy-start(f32[8]{0:T(128)} %adv_ref.1) | copy-start | bytes 100
  18.7 34.4 %copy-start.7 = (s32[8]{0:T(128)S(1)}, s32[8]{0:T(128)}, u32[]{:S(2)}) copy-start(s32[8]{0:T(128)} %len_ref.1) | copy-start | bytes 100
  31.2 21.9 %all-to-all-start = ((bf16[32,64,128]{2,1,0:T(8,128)(2,1)}), bf16[32,64,128]{2,1,0:T(8,128)(2,1)S(1)}, u32[]{:S(2)}, u32[]{:S(2)}) async-start(bf16[32,64,128]{2,1,0:T(8,128)(2,1)} %shard_map.119), calls=%async_computation | async-start | bytes 1048576 | tf_op jit(solution)/shard_map/all_to_all | solution.py:197
  35.1 12.9 %collective-permute-start = (bf16[64,16,128]{2,1,0:T(8,128)(2,1)S(1)}, bf16[64,16,128]{2,1,0:T(8,128)(2,1)S(1)}, u32[]{:S(2)}, u32[]{:S(2)}) collective-permute-start(bf16[64,16,128]{2,1,0:T(8,128)(2,1)S(1)} %all-to-all-done.1.p00_ref), channel_id=1, source_target_pairs={{0,16},{16,0},{1,17},{17,1},{2,18},{18,2},{3,19},{19,3},{4,20},{20... | collective-permute-start | bytes 786440 | tf_op jit(solution)/shard_map/ppermute | solution.py:191
  36.9 11.2 %collective-permute-start.1 = (bf16[64,16,128]{2,1,0:T(8,128)(2,1)S(1)}, bf16[64,16,128]{2,1,0:T(8,128)(2,1)S(1)}, u32[]{:S(2)}, u32[]{:S(2)}) collective-permute-start(bf16[64,16,128]{2,1,0:T(8,128)(2,1)S(1)} %all-to-all-done.1.p00_ref), channel_id=1, source_target_pairs={{0,8},{8,0},{1,9},{9,1},{2,10},{10,2},{3,11},{11,3},{4,12},{12,4},... | collective-permute-start | bytes 786440 | tf_op jit(solution)/shard_map/ppermute | solution.py:192
  48.1 5.1 %collective-permute-start.2 = (bf16[64,16,128]{2,1,0:T(8,128)(2,1)S(1)}, bf16[64,16,128]{2,1,0:T(8,128)(2,1)S(1)}, u32[]{:S(2)}, u32[]{:S(2)}) collective-permute-start(bf16[64,16,128]{2,1,0:T(8,128)(2,1)S(1)} %collective-permute-done.p01_ref), channel_id=1, source_target_pairs={{0,8},{8,0},{1,9},{9,1},{2,10},{10,2},{3,11},{11,3},{4,12},{12,4},... | collective-permute-start | bytes 786440 | tf_op jit(solution)/shard_map/ppermute | solution.py:193
  59.4 1.9 %collective-permute-start.3 = (bf16[2,64,16,128]{3,2,1,0:T(8,128)(2,1)S(1)}, bf16[2,64,16,128]{3,2,1,0:T(8,128)(2,1)S(1)}, u32[]{:S(2)}, u32[]{:S(2)}) collective-permute-start(bf16[2,64,16,128]{3,2,1,0:T(8,128)(2,1)S(1)} %get-tuple-element.19), channel_id=1, source_target_pairs={{0,8},{8,0},{1,9},{9,1},{2,10},{10,2},{3,11},{11,3},{4,12},{12,4},... | collective-permute-start | bytes 1572872 | tf_op jit(solution)/shard_map/ppermute | solution.py:215
  61.4 19.9 %all-to-all-start.2 = ((bf16[32,48,128]{2,1,0:T(8,128)(2,1)}), bf16[32,48,128]{2,1,0:T(8,128)(2,1)S(1)}, u32[]{:S(2)}, u32[]{:S(2)}) async-start(bf16[32,48,128]{2,1,0:T(8,128)(2,1)} %get-tuple-element.21), calls=%async_computation.2 | async-start | bytes 786432 | tf_op jit(solution)/shard_map/all_to_all | solution.py:219
  66.1 12.4 %collective-permute-start.4 = (bf16[64,16,128]{2,1,0:T(8,128)(2,1)S(1)}, bf16[64,16,128]{2,1,0:T(8,128)(2,1)S(1)}, u32[]{:S(2)}, u32[]{:S(2)}) collective-permute-start(bf16[64,16,128]{2,1,0:T(8,128)(2,1)S(1)} %get-tuple-element.20), channel_id=1, source_target_pairs={{0,16},{16,0},{1,17},{17,1},{2,18},{18,2},{3,19},{19,3},{4,20},{20... | collective-permute-start | bytes 786440 | tf_op jit(solution)/shard_map/ppermute | solution.py:217
  81.3 21.9 %all-to-all-start.3 = ((bf16[64,16,128]{2,1,0:T(8,128)(2,1)}), bf16[64,16,128]{2,1,0:T(8,128)(2,1)S(1)}, u32[]{:S(2)}, u32[]{:S(2)}) async-start(bf16[64,16,128]{2,1,0:T(8,128)(2,1)} %shard_map.124), calls=%async_computation.3 | async-start | bytes 524288 | tf_op jit(solution)/shard_map/all_to_all | solution.py:222

commit v2 on v1

--- a/solution.py
+++ b/solution.py
@@ -215,7 +215,6 @@
     got = lax.ppermute(send, "core", swap)
     keep, send = call(add_core_kernel, [(64, 16, HDIM)] * 2, 2)(keep, got)
     got = lax.ppermute(send, "x", swap)
-    mine, _ = lax.optimization_barrier((mine, send))
     back = lax.all_to_all(mine, WIDE, 0, 0, tiled=True)
     (owned,) = call(add_x_kernel, [(64, 16, HDIM)], 2)(keep, got)
     owned, _ = lax.optimization_barrier((owned, back))

time: 104 us -> 103 us (level)
  waiting for transfers between devices: 55.7 us -> 53.7 us
    ppermute x1, waiting for transfers between devices: 1.91 us -> 0.01 us  [body(): got = lax.ppermute(send, 'core', swap)]
  transfers between devices with their start and end apart: 9 -> 9, of which waited for: 7 -> 6; matrix products, arithmetic and copies ran while one was open for 0% -> 0% of each run, Pallas kernels for 2% -> 3%
where the time goes in v2:
time: 103 us; the launch traced here: 102 us
  waiting for transfers between devices  53.7 us (52%)
  starting transfers between devices  35.9 us (35%)
  Pallas kernels  10.2 us (10%)
  local copies, waits for them, and re-layouts  1.69 us (2%)
    all_to_all x1, starting transfers between devices, body(): p00 = lax.all_to_all(sent_p, ('zh', 'zl', 'narrow'), 0, 0, tiled=True)  14.7 us
    all_to_all x1, waiting for transfers between devices, body(): owned = lax.all_to_all(owned, ('zh', 'zl', 'narrow'), 0, 0, tiled=True)  12.6 us
    all_to_all x1, waiting for transfers between devices, body(): p00 = lax.all_to_all(sent_p, ('zh', 'zl', 'narrow'), 0, 0, tiled=True)  12.5 us
    ppermute x1, waiting for transfers between devices, body(): p01 = lax.ppermute(p00, 'x', swap)  11.2 us
    ppermute x1, waiting for transfers between devices, body(): got = lax.ppermute(send, 'x', swap)  10.4 us
    all_to_all x1, starting transfers between devices, body(): owned = lax.all_to_all(owned, ('zh', 'zl', 'narrow'), 0, 0, tiled=True)  8.78 us
    pallas_call x1, Pallas kernels, body(): call(attn_kernel, [(32, 3 * BLOCK, HDIM), (2, 64, 16, HDIM), (2, 64, 16,...  6.21 us
    all_to_all x1, waiting for transfers between devices, body(): got_r = lax.all_to_all(sent_r, WIDE, 0, 0, tiled=True)  5.08 us
  transfers between devices with their start and end apart: 9, of which 6 were waited for; matrix products, arithmetic and copies ran while one was open for 0% of the time, Pallas kernels for 3%

profile of v2, /device:TPU:8, one launch (start us, length us, event | category | flops | bytes accessed | tf_op | source)
XLA Modules:
  0.0 102.3 jit_solution(5857978608419274062)
XLA Ops:
  0.6 0.0 copy-start.4
  0.6 0.8 copy-done.4
  1.5 0.0 copy-start.5
  1.5 0.8 copy-done.5
  2.3 0.7 shard_map.120
  3.0 0.0 copy-start
  3.1 0.0 copy-start.1
  3.1 0.0 copy-start.2
  3.1 0.0 copy-start.3
  3.1 14.7 %all-to-all-start.1 = ((bf16[64,16,128]{2,1,0:T(8,128)(2,1)}), bf16[64,16,128]{2,1,0:T(8,128)(2,1)S(1)}, u32[]{:S(2)}, u32[]{:S(2)}) async-start(bf16[64,16,128]{2,1,0:T(8,128)(2,1)} %shard_map.120), calls=%async_computation.1 | async-start | bytes 524288 | tf_op jit(solution)/shard_map/all_to_all | solution.py:190
  17.8 0.0 copy-done
  17.8 0.0 copy-done.1
  17.8 0.0 copy-done.2
  17.8 0.0 copy-done.3
  17.8 0.9 shard_map.119
  18.7 0.0 copy-start.6
  18.7 0.0 copy-start.7
  18.7 12.5 %all-to-all-done.1.p00_ref = bf16[64,16,128]{2,1,0:T(8,128)(2,1)S(1)} async-done(((bf16[64,16,128]{2,1,0:T(8,128)(2,1)}), bf16[64,16,128]{2,1,0:T(8,128)(2,1)S(1)}, u32[]{:S(2)}, u32[]{:S(2)}) %all-to-all-start.1) | async-done | bytes 262176 | tf_op jit(solution)/shard_map/all_to_all | solution.py:190
  31.2 3.9 %all-to-all-start = ((bf16[32,64,128]{2,1,0:T(8,128)(2,1)}), bf16[32,64,128]{2,1,0:T(8,128)(2,1)S(1)}, u32[]{:S(2)}, u32[]{:S(2)}) async-start(bf16[32,64,128]{2,1,0:T(8,128)(2,1)} %shard_map.119), calls=%async_computation | async-start | bytes 1048576 | tf_op jit(solution)/shard_map/all_to_all | solution.py:197
  35.1 1.8 %collective-permute-start = (bf16[64,16,128]{2,1,0:T(8,128)(2,1)S(1)}, bf16[64,16,128]{2,1,0:T(8,128)(2,1)S(1)}, u32[]{:S(2)}, u32[]{:S(2)}) collective-permute-start(bf16[64,16,128]{2,1,0:T(8,128)(2,1)S(1)} %all-to-all-done.1.p00_ref), channel_id=1, source_target_pairs={{0,16},{16,0},{1,17},{17,1},{2,18},{18,2},{3,19},{19,3},{4,20},{20... | collective-permute-start | bytes 786440 | tf_op jit(solution)/shard_map/ppermute | solution.py:191
  36.9 0.0 collective-permute-start.1
  36.9 11.2 %collective-permute-done.p01_ref = bf16[64,16,128]{2,1,0:T(8,128)(2,1)S(1)} collective-permute-done((bf16[64,16,128]{2,1,0:T(8,128)(2,1)S(1)}, bf16[64,16,128]{2,1,0:T(8,128)(2,1)S(1)}, u32[]{:S(2)}, u32[]{:S(2)}) %collective-permute-start) | collective-permute-done | bytes 262176 | tf_op jit(solution)/shard_map/ppermute | solution.py:191
  48.1 0.0 collective-permute-start.2
  48.1 0.0 collective-permute-done.1.p10_ref
  48.1 5.1 %all-to-all-done.resp_ref = bf16[32,64,128]{2,1,0:T(8,128)(2,1)S(1)} async-done(((bf16[32,64,128]{2,1,0:T(8,128)(2,1)}), bf16[32,64,128]{2,1,0:T(8,128)(2,1)S(1)}, u32[]{:S(2)}, u32[]{:S(2)}) %all-to-all-start) | async-done | bytes 524320 | tf_op jit(solution)/shard_map/all_to_all | solution.py:197
  53.1 0.0 collective-permute-done.2.p11_ref
  53.1 0.0 copy-done.6
  53.1 0.0 copy-done.7
  53.2 6.2 %shard_map.121 = (bf16[32,48,128]{2,1,0:T(8,128)(2,1)}, bf16[2,64,16,128]{3,2,1,0:T(8,128)(2,1)S(1)}, bf16[2,64,16,128]{3,2,1,0:T(8,128)(2,1)S(1)}) custom-call(f32[8]{0:T(128)S(1)} %copy-done.6, s32[8]{0:T(128)S(1)} %copy-done.7, bf16[32,64,128]{2,1,0:T(8,128)(2,1)S(1)} %all-to-all-done.resp_ref, bf16[64,16,128]{2,1,0:T(8,128)(2,1)S(1)} %all-to-all-done.1.p00_ref, ...), custom_call_target="tpu_custom_call" | custom-call | flops 1677721600 | bytes 3145728 | tf_op jit(solution)/shard_map/pallas_call | solution.py:200
  59.4 0.0 collective-permute-start.3
  59.4 4.8 %all-to-all-start.2 = ((bf16[32,48,128]{2,1,0:T(8,128)(2,1)}), bf16[32,48,128]{2,1,0:T(8,128)(2,1)S(1)}, u32[]{:S(2)}, u32[]{:S(2)}) async-start(bf16[32,48,128]{2,1,0:T(8,128)(2,1)} %get-tuple-element.16), calls=%async_computation.2 | async-start | bytes 786432 | tf_op jit(solution)/shard_map/all_to_all | solution.py:218
  64.2 0.0 collective-permute-done.3.got_ref
  64.2 0.1 shard_map.123
  64.3 1.9 %collective-permute-start.4 = (bf16[64,16,128]{2,1,0:T(8,128)(2,1)S(1)}, bf16[64,16,128]{2,1,0:T(8,128)(2,1)S(1)}, u32[]{:S(2)}, u32[]{:S(2)}) collective-permute-start(bf16[64,16,128]{2,1,0:T(8,128)(2,1)S(1)} %get-tuple-element.23), channel_id=1, source_target_pairs={{0,16},{16,0},{1,17},{17,1},{2,18},{18,2},{3,19},{19,3},{4,20},{20... | collective-permute-start | bytes 786440 | tf_op jit(solution)/shard_map/ppermute | solution.py:217
  66.2 10.4 %collective-permute-done.4.got_ref = bf16[64,16,128]{2,1,0:T(8,128)(2,1)S(1)} collective-permute-done((bf16[64,16,128]{2,1,0:T(8,128)(2,1)S(1)}, bf16[64,16,128]{2,1,0:T(8,128)(2,1)S(1)}, u32[]{:S(2)}, u32[]{:S(2)}) %collective-permute-start.4) | collective-permute-done | bytes 262176 | tf_op jit(solution)/shard_map/ppermute | solution.py:217
  76.6 0.8 shard_map.124
  77.4 2.0 %all-to-all-done.2.got_ref = bf16[32,48,128]{2,1,0:T(8,128)(2,1)S(1)} async-done(((bf16[32,48,128]{2,1,0:T(8,128)(2,1)}), bf16[32,48,128]{2,1,0:T(8,128)(2,1)S(1)}, u32[]{:S(2)}, u32[]{:S(2)}) %all-to-all-start.2) | async-done | bytes 393248 | tf_op jit(solution)/shard_map/all_to_all | solution.py:218
  79.4 8.8 %all-to-all-start.3 = ((bf16[64,16,128]{2,1,0:T(8,128)(2,1)}), bf16[64,16,128]{2,1,0:T(8,128)(2,1)S(1)}, u32[]{:S(2)}, u32[]{:S(2)}) async-start(bf16[64,16,128]{2,1,0:T(8,128)(2,1)} %shard_map.124), calls=%async_computation.3 | async-start | bytes 524288 | tf_op jit(solution)/shard_map/all_to_all | solution.py:221
  88.2 0.8 shard_map.122
  89.0 12.6 %all-to-all-done.3 = bf16[64,16,128]{2,1,0:T(8,128)(2,1)S(1)} async-done(((bf16[64,16,128]{2,1,0:T(8,128)(2,1)}), bf16[64,16,128]{2,1,0:T(8,128)(2,1)S(1)}, u32[]{:S(2)}, u32[]{:S(2)}) %all-to-all-start.3) | async-done | bytes 262176 | tf_op jit(solution)/shard_map/all_to_all | solution.py:221
  101.6 0.7 shard_map.125
Async XLA Ops:
  0.6 0.8 copy-start.4
  1.5 0.8 copy-start.5
  3.0 14.7 %copy-start = (bf16[8,16,512]{2,1,0:T(8,128)(2,1)S(1)}, bf16[8,16,512]{2,1,0:T(8,128)(2,1)}, u32[]{:S(2)}) copy-start(bf16[8,16,512]{2,1,0:T(8,128)(2,1)} %q_ref.1) | copy-start | bytes 393220
  3.1 14.7 %copy-start.1 = (bf16[8,16,512]{2,1,0:T(8,128)(2,1)S(1)}, bf16[8,16,512]{2,1,0:T(8,128)(2,1)}, u32[]{:S(2)}) copy-start(bf16[8,16,512]{2,1,0:T(8,128)(2,1)} %k_ref.2) | copy-start | bytes 393220
  3.1 14.7 %copy-start.2 = (bf16[8,16,512]{2,1,0:T(8,128)(2,1)S(1)}, bf16[8,16,512]{2,1,0:T(8,128)(2,1)}, u32[]{:S(2)}) copy-start(bf16[8,16,512]{2,1,0:T(8,128)(2,1)} %v_ref.2) | copy-start | bytes 393220
  3.1 14.7 %copy-start.3 = (bf16[8,16,512]{2,1,0:T(8,128)(2,1)S(1)}, bf16[8,16,512]{2,1,0:T(8,128)(2,1)}, u32[]{:S(2)}) copy-start(bf16[8,16,512]{2,1,0:T(8,128)(2,1)} %o_ref.1) | copy-start | bytes 393220
  3.1 28.2 %all-to-all-start.1 = ((bf16[64,16,128]{2,1,0:T(8,128)(2,1)}), bf16[64,16,128]{2,1,0:T(8,128)(2,1)S(1)}, u32[]{:S(2)}, u32[]{:S(2)}) async-start(bf16[64,16,128]{2,1,0:T(8,128)(2,1)} %shard_map.120), calls=%async_computation.1 | async-start | bytes 524288 | tf_op jit(solution)/shard_map/all_to_all | solution.py:190
  18.7 34.4 %copy-start.6 = (f32[8]{0:T(128)S(1)}, f32[8]{0:T(128)}, u32[]{:S(2)}) copy-start(f32[8]{0:T(128)} %adv_ref.1) | copy-start | bytes 100
  18.7 34.4 %copy-start.7 = (s32[8]{0:T(128)S(1)}, s32[8]{0:T(128)}, u32[]{:S(2)}) copy-start(s32[8]{0:T(128)} %len_ref.1) | copy-start | bytes 100
  31.2 21.9 %all-to-all-start = ((bf16[32,64,128]{2,1,0:T(8,128)(2,1)}), bf16[32,64,128]{2,1,0:T(8,128)(2,1)S(1)}, u32[]{:S(2)}, u32[]{:S(2)}) async-start(bf16[32,64,128]{2,1,0:T(8,128)(2,1)} %shard_map.119), calls=%async_computation | async-start | bytes 1048576 | tf_op jit(solution)/shard_map/all_to_all | solution.py:197
  35.1 12.9 %collective-permute-start = (bf16[64,16,128]{2,1,0:T(8,128)(2,1)S(1)}, bf16[64,16,128]{2,1,0:T(8,128)(2,1)S(1)}, u32[]{:S(2)}, u32[]{:S(2)}) collective-permute-start(bf16[64,16,128]{2,1,0:T(8,128)(2,1)S(1)} %all-to-all-done.1.p00_ref), channel_id=1, source_target_pairs={{0,16},{16,0},{1,17},{17,1},{2,18},{18,2},{3,19},{19,3},{4,20},{20... | collective-permute-start | bytes 786440 | tf_op jit(solution)/shard_map/ppermute | solution.py:191
  36.9 11.2 %collective-permute-start.1 = (bf16[64,16,128]{2,1,0:T(8,128)(2,1)S(1)}, bf16[64,16,128]{2,1,0:T(8,128)(2,1)S(1)}, u32[]{:S(2)}, u32[]{:S(2)}) collective-permute-start(bf16[64,16,128]{2,1,0:T(8,128)(2,1)S(1)} %all-to-all-done.1.p00_ref), channel_id=1, source_target_pairs={{0,8},{8,0},{1,9},{9,1},{2,10},{10,2},{3,11},{11,3},{4,12},{12,4},... | collective-permute-start | bytes 786440 | tf_op jit(solution)/shard_map/ppermute | solution.py:192
  48.1 5.1 %collective-permute-start.2 = (bf16[64,16,128]{2,1,0:T(8,128)(2,1)S(1)}, bf16[64,16,128]{2,1,0:T(8,128)(2,1)S(1)}, u32[]{:S(2)}, u32[]{:S(2)}) collective-permute-start(bf16[64,16,128]{2,1,0:T(8,128)(2,1)S(1)} %collective-permute-done.p01_ref), channel_id=1, source_target_pairs={{0,8},{8,0},{1,9},{9,1},{2,10},{10,2},{3,11},{11,3},{4,12},{12,4},... | collective-permute-start | bytes 786440 | tf_op jit(solution)/shard_map/ppermute | solution.py:193
  59.4 4.8 %collective-permute-start.3 = (bf16[2,64,16,128]{3,2,1,0:T(8,128)(2,1)S(1)}, bf16[2,64,16,128]{3,2,1,0:T(8,128)(2,1)S(1)}, u32[]{:S(2)}, u32[]{:S(2)}) collective-permute-start(bf16[2,64,16,128]{3,2,1,0:T(8,128)(2,1)S(1)} %get-tuple-element.21), channel_id=1, source_target_pairs={{0,8},{8,0},{1,9},{9,1},{2,10},{10,2},{3,11},{11,3},{4,12},{12,4},... | collective-permute-start | bytes 1572872 | tf_op jit(solution)/shard_map/ppermute | solution.py:215
  59.4 20.0 %all-to-all-start.2 = ((bf16[32,48,128]{2,1,0:T(8,128)(2,1)}), bf16[32,48,128]{2,1,0:T(8,128)(2,1)S(1)}, u32[]{:S(2)}, u32[]{:S(2)}) async-start(bf16[32,48,128]{2,1,0:T(8,128)(2,1)} %get-tuple-element.16), calls=%async_computation.2 | async-start | bytes 786432 | tf_op jit(solution)/shard_map/all_to_all | solution.py:218
  64.3 12.3 %collective-permute-start.4 = (bf16[64,16,128]{2,1,0:T(8,128)(2,1)S(1)}, bf16[64,16,128]{2,1,0:T(8,128)(2,1)S(1)}, u32[]{:S(2)}, u32[]{:S(2)}) collective-permute-start(bf16[64,16,128]{2,1,0:T(8,128)(2,1)S(1)} %get-tuple-element.23), channel_id=1, source_target_pairs={{0,16},{16,0},{1,17},{17,1},{2,18},{18,2},{3,19},{19,3},{4,20},{20... | collective-permute-start | bytes 786440 | tf_op jit(solution)/shard_map/ppermute | solution.py:217
  79.4 22.2 %all-to-all-start.3 = ((bf16[64,16,128]{2,1,0:T(8,128)(2,1)}), bf16[64,16,128]{2,1,0:T(8,128)(2,1)S(1)}, u32[]{:S(2)}, u32[]{:S(2)}) async-start(bf16[64,16,128]{2,1,0:T(8,128)(2,1)} %shard_map.124), calls=%async_computation.3 | async-start | bytes 524288 | tf_op jit(solution)/shard_map/all_to_all | solution.py:221

commit v3 on v2

--- a/solution.py
+++ b/solution.py
@@ -120,6 +120,19 @@
     inv = 1.0 / jnp.sum(total, axis=0, keepdims=True)
     delta = jnp.sum(delta, axis=0, keepdims=True) * inv
 
+    def store_blocks(z, which, rows):
+        count = rows.shape[0] // (4 * BLOCK)
+        rows = rows.astype(BF16).reshape(count, 4, BLOCK, HDIM)
+        for xt in range(2):
+            for ct in range(2):
+                mine_ref[
+                    z : z + count,
+                    jnp.bitwise_xor(x, xt),
+                    jnp.bitwise_xor(core, ct),
+                    which * BLOCK : (which + 1) * BLOCK,
+                    :,
+                ] = rows[:, xt * 2 + ct]
+
     dq = jnp.zeros((HDIM, RESP), F32)
     for c in range(n_chunks):
         rows = slice(c * CHUNK, (c + 1) * CHUNK)
@@ -136,11 +149,9 @@
             half = c // 4
             out[(c // 2) % 2, half * 32 : (half + 1) * 32] = both
         else:
-            part = slice((c - n_prompt) * 16, (c - n_prompt + 1) * 16)
-            mine_ref[part, BLOCK : 2 * BLOCK, :] = dk.reshape(16, BLOCK, HDIM).astype(BF16)
-            mine_ref[part, 2 * BLOCK : 3 * BLOCK, :] = dv.reshape(16, BLOCK, HDIM).astype(BF16)
-    dq = (dq * factor).T
-    mine_ref[:, 0:BLOCK, :] = dq.reshape(32, BLOCK, HDIM).astype(BF16)
+            store_blocks((c - n_prompt) * 4, 1, dk)
+            store_blocks((c - n_prompt) * 4, 2, dv)
+    store_blocks(0, 0, (dq * factor).T)
 
 
 def add_core_kernel(keep_ref, got_ref, next_ref, send_ref):
@@ -152,13 +163,28 @@
     out_ref[...] = (keep_ref[...].astype(F32) + got_ref[...].astype(F32)).astype(BF16)
 
 
-def unpack_resp_kernel(got_ref, q_ref, k_ref, v_ref):
-    for h in range(4):
-        for r in range(RESPONSES):
-            for i, ref in enumerate((q_ref, k_ref, v_ref)):
-                ref[r, :, h * HDIM : (h + 1) * HDIM] = got_ref[
-                    h * 8 + r, i * BLOCK : (i + 1) * BLOCK, :
-                ]
+def split_x_kernel(got_ref, out_ref):
+    out_ref[...] = got_ref[:, 1]
+
+
+def split_core_kernel(got_ref, from_x_ref, out_ref):
+    out_ref[0] = got_ref[:, 0, 1]
+    out_ref[1] = from_x_ref[:, 1]
+
+
+def unpack_resp_kernel(got_ref, from_x_ref, from_core_ref, q_ref, k_ref, v_ref):
+    x, core = lax.axis_index("x"), lax.axis_index("core")
+    for z in range(8):
+        h = z // 2
+        for dx in range(2):
+            for dc in range(2):
+                r = (z % 2) * 4 + jnp.bitwise_xor(x, dx) * 2 + jnp.bitwise_xor(core, dc)
+                if dc:
+                    rows = from_core_ref[dx, z]
+                else:
+                    rows = from_x_ref[z, 0] if dx else got_ref[z, 0, 0]
+                for i, ref in enumerate((q_ref, k_ref, v_ref)):
+                    ref[r, :, h * HDIM : (h + 1) * HDIM] = rows[i * BLOCK : (i + 1) * BLOCK]
 
 
 def unpack_prompt_kernel(got_ref, k_ref, v_ref):
@@ -170,14 +196,14 @@
             v_ref[:, cols] = both[8:16].astype(BF16)
 
 
-def call(kernel, outs, n_in, scratch=(), smem=0, flops=0, bytes_accessed=1 << 20):
+def call(kernel, outs, n_in, scratch=(), smem=0, params=PARAMS, flops=0, bytes_accessed=1 << 20):
     return pl.pallas_call(
         kernel,
         out_shape=[jax.ShapeDtypeStruct(s, BF16) for s in outs],
         in_specs=[SMEM] * smem + [VMEM] * n_in,
         out_specs=[VMEM] * len(outs),
         scratch_shapes=list(scratch),
-        compiler_params=PARAMS,
+        compiler_params=params,
         cost_estimate=pl.CostEstimate(
             flops=flops, bytes_accessed=bytes_accessed, transcendentals=0
         ),
@@ -186,7 +212,7 @@
 
 def body(resp_q, resp_k, resp_v, resp_dout, advantage, resp_len, prompt_k, prompt_v):
     swap = [(0, 1), (1, 0)]
-    (sent_p,) = call(pack_prompt_kernel, [(64, 16, HDIM)], 2)(prompt_k, prompt_v)
+    (sent_p,) = call(pack_prompt_kernel, [(64, 16, HDIM)], 2, params=None)(prompt_k, prompt_v)
     p00 = lax.all_to_all(sent_p, ("zh", "zl", "narrow"), 0, 0, tiled=True)
     p01 = lax.ppermute(p00, "x", swap)
     p10 = lax.ppermute(p00, "core", swap)
@@ -199,7 +225,7 @@
     keys = PROMPT + RESP
     mine, keep, send = call(
         attn_kernel,
-        [(32, 3 * BLOCK, HDIM), (2, 64, 16, HDIM), (2, 64, 16, HDIM)],
+        [(8, 2, 2, 3 * BLOCK, HDIM), (2, 64, 16, HDIM), (2, 64, 16, HDIM)],
         5,
         scratch=[
             pltpu.VMEM((keys, HDIM), BF16),
@@ -215,11 +241,17 @@
     got = lax.ppermute(send, "core", swap)
     keep, send = call(add_core_kernel, [(64, 16, HDIM)] * 2, 2)(keep, got)
     got = lax.ppermute(send, "x", swap)
-    back = lax.all_to_all(mine, WIDE, 0, 0, tiled=True)
+    back = lax.all_to_all(mine, ("zh", "zl"), 0, 0, tiled=True)
     (owned,) = call(add_x_kernel, [(64, 16, HDIM)], 2)(keep, got)
     owned, _ = lax.optimization_barrier((owned, back))
     owned = lax.all_to_all(owned, ("zh", "zl", "narrow"), 0, 0, tiled=True)
-    grad_q, grad_k, grad_v = call(unpack_resp_kernel, [(RESPONSES, BLOCK, 4 * HDIM)] * 3, 1)(back)
+    (part,) = call(split_x_kernel, [(8, 2, 3 * BLOCK, HDIM)], 1)(back)
+    from_x = lax.ppermute(part, "x", swap)
+    (part,) = call(split_core_kernel, [(2, 8, 3 * BLOCK, HDIM)], 2)(back, from_x)
+    from_core = lax.ppermute(part, "core", swap)
+    grad_q, grad_k, grad_v = call(unpack_resp_kernel, [(RESPONSES, BLOCK, 4 * HDIM)] * 3, 3)(
+        back, from_x, from_core
+    )
     prompt_gk, prompt_gv = call(unpack_prompt_kernel, [(8, HEADS * HDIM)] * 2, 1)(
         owned.reshape(8, 8, 16, HDIM)
     )

time: 103 us -> 99 us (0.961)
  starting transfers between devices: 35.9 us -> 32 us
  local copies, waits for them, and re-layouts: 1.69 us -> 0.02 us
    all_to_all x1, waiting for transfers between devices: 12.6 us -> 2.73 us  [body(): owned = lax.all_to_all(owned, ('zh', 'zl', 'narrow'), 0, 0, tiled=True)]
    ppermute x0 -> x2, waiting for transfers between devices: none -> 9.4 us  [the longest x1 7.98 us: body(): from_x = lax.ppermute(part, 'x', swap)]
    all_to_all x1, waiting for transfers between devices: 2 us -> 5.93 us  [body(): back = lax.all_to_all(mine, ('zh', 'zl'), 0, 0, tiled=True)]
    all_to_all x1, starting transfers between devices: 8.78 us -> 5.59 us  [body(): owned = lax.all_to_all(owned, ('zh', 'zl', 'narrow'), 0, 0, tiled=True)]
    ppermute x1, waiting for transfers between devices: 10.4 us -> 7.74 us  [body(): got = lax.ppermute(send, 'x', swap)]
    unnamed x16 -> x12, local copies, waits for them, and re-layouts: 1.69 us -> 0.02 us
    ppermute x1, starting transfers between devices: 1.88 us -> 0.64 us  [body(): got = lax.ppermute(send, 'x', swap)]
    pallas_call x3 -> x5, Pallas kernels: 7.76 us -> 8.66 us  [the longest x1 6.21 us: body(): call(attn_kernel, [(8, 2, 2, 3 * BLOCK, HDIM), (2, 64, 16, HDIM), (2, 64,...]
  transfers between devices with their start and end apart: 9 -> 11, of which waited for: 6 -> 8; matrix products, arithmetic and copies ran while one was open for 0% -> 0% of each run, Pallas kernels for 3% -> 3%
where the time goes in v3:
time: 99 us; the launch traced here: 98.5 us
  waiting for transfers between devices  54.6 us (55%)
  starting transfers between devices  32 us (32%)
  Pallas kernels  11.1 us (11%)
    all_to_all x1, starting transfers between devices, body(): p00 = lax.all_to_all(sent_p, ('zh', 'zl', 'narrow'), 0, 0, tiled=True)  14.7 us
    all_to_all x1, waiting for transfers between devices, body(): p00 = lax.all_to_all(sent_p, ('zh', 'zl', 'narrow'), 0, 0, tiled=True)  12.5 us
    ppermute x1, waiting for transfers between devices, body(): p01 = lax.ppermute(p00, 'x', swap)  11.2 us
    ppermute x1, waiting for transfers between devices, body(): from_x = lax.ppermute(part, 'x', swap)  7.98 us
    ppermute x1, waiting for transfers between devices, body(): got = lax.ppermute(send, 'x', swap)  7.74 us
    pallas_call x1, Pallas kernels, body(): call(attn_kernel, [(8, 2, 2, 3 * BLOCK, HDIM), (2, 64, 16, HDIM), (2, 64,...  6.21 us
    all_to_all x1, waiting for transfers between devices, body(): back = lax.all_to_all(mine, ('zh', 'zl'), 0, 0, tiled=True)  5.93 us
    all_to_all x1, starting transfers between devices, body(): owned = lax.all_to_all(owned, ('zh', 'zl', 'narrow'), 0, 0, tiled=True)  5.59 us
  transfers between devices with their start and end apart: 11, of which 8 were waited for; matrix products, arithmetic and copies ran while one was open for 0% of the time, Pallas kernels for 3%

profile of v3, /device:TPU:8, one launch (start us, length us, event | category | flops | bytes accessed | tf_op | source)
XLA Modules:
  0.0 98.5 jit_solution(16446933390042067496)
XLA Ops:
  0.6 1.6 %shard_map.120 = bf16[64,16,128]{2,1,0:T(8,128)(2,1)} custom-call(bf16[8,4096]{1,0:T(8,128)(2,1)} %k_ref.3, bf16[8,4096]{1,0:T(8,128)(2,1)} %v_ref.3), custom_call_target="tpu_custom_call" | custom-call | bytes 1048576 | tf_op jit(solution)/shard_map/pallas_call | solution.py:215
  2.2 0.0 copy-start
  2.2 0.0 copy-start.1
  2.2 0.0 copy-start.2
  2.2 0.0 copy-start.3
  2.3 14.7 %all-to-all-start.1 = ((bf16[64,16,128]{2,1,0:T(8,128)(2,1)}), bf16[64,16,128]{2,1,0:T(8,128)(2,1)S(1)}, u32[]{:S(2)}, u32[]{:S(2)}) async-start(bf16[64,16,128]{2,1,0:T(8,128)(2,1)} %shard_map.120), calls=%async_computation.1 | async-start | bytes 524288 | tf_op jit(solution)/shard_map/all_to_all | solution.py:216
  17.0 0.0 copy-done
  17.0 0.0 copy-done.1
  17.0 0.0 copy-done.2
  17.0 0.0 copy-done.3
  17.0 0.9 shard_map.119
  17.9 0.0 copy-start.4
  17.9 0.0 copy-start.5
  17.9 12.5 %all-to-all-done.1.p00_ref = bf16[64,16,128]{2,1,0:T(8,128)(2,1)S(1)} async-done(((bf16[64,16,128]{2,1,0:T(8,128)(2,1)}), bf16[64,16,128]{2,1,0:T(8,128)(2,1)S(1)}, u32[]{:S(2)}, u32[]{:S(2)}) %all-to-all-start.1) | async-done | bytes 262176 | tf_op jit(solution)/shard_map/all_to_all | solution.py:216
  30.4 3.9 %all-to-all-start = ((bf16[32,64,128]{2,1,0:T(8,128)(2,1)}), bf16[32,64,128]{2,1,0:T(8,128)(2,1)S(1)}, u32[]{:S(2)}, u32[]{:S(2)}) async-start(bf16[32,64,128]{2,1,0:T(8,128)(2,1)} %shard_map.119), calls=%async_computation | async-start | bytes 1048576 | tf_op jit(solution)/shard_map/all_to_all | solution.py:223
  34.3 1.8 %collective-permute-start = (bf16[64,16,128]{2,1,0:T(8,128)(2,1)S(1)}, bf16[64,16,128]{2,1,0:T(8,128)(2,1)S(1)}, u32[]{:S(2)}, u32[]{:S(2)}) collective-permute-start(bf16[64,16,128]{2,1,0:T(8,128)(2,1)S(1)} %all-to-all-done.1.p00_ref), channel_id=1, source_target_pairs={{0,16},{16,0},{1,17},{17,1},{2,18},{18,2},{3,19},{19,3},{4,20},{20... | collective-permute-start | bytes 786440 | tf_op jit(solution)/shard_map/ppermute | solution.py:217
  36.1 0.0 collective-permute-start.1
  36.1 11.2 %collective-permute-done.p01_ref = bf16[64,16,128]{2,1,0:T(8,128)(2,1)S(1)} collective-permute-done((bf16[64,16,128]{2,1,0:T(8,128)(2,1)S(1)}, bf16[64,16,128]{2,1,0:T(8,128)(2,1)S(1)}, u32[]{:S(2)}, u32[]{:S(2)}) %collective-permute-start) | collective-permute-done | bytes 262176 | tf_op jit(solution)/shard_map/ppermute | solution.py:217
  47.3 0.0 collective-permute-start.2
  47.3 0.0 collective-permute-done.1.p10_ref
  47.3 5.1 %all-to-all-done.resp_ref = bf16[32,64,128]{2,1,0:T(8,128)(2,1)S(1)} async-done(((bf16[32,64,128]{2,1,0:T(8,128)(2,1)}), bf16[32,64,128]{2,1,0:T(8,128)(2,1)S(1)}, u32[]{:S(2)}, u32[]{:S(2)}) %all-to-all-start) | async-done | bytes 524320 | tf_op jit(solution)/shard_map/all_to_all | solution.py:223
  52.3 0.0 collective-permute-done.2.p11_ref
  52.3 0.0 copy-done.4
  52.3 0.0 copy-done.5
  52.3 6.2 %shard_map.121 = (bf16[8,2,2,48,128]{4,3,2,1,0:T(8,128)(2,1)}, bf16[2,64,16,128]{3,2,1,0:T(8,128)(2,1)S(1)}, bf16[2,64,16,128]{3,2,1,0:T(8,128)(2,1)S(1)}) custom-call(f32[8]{0:T(128)S(1)} %copy-done.4, s32[8]{0:T(128)S(1)} %copy-done.5, bf16[32,64,128]{2,1,0:T(8,128)(2,1)S(1)} %all-to-all-done.resp_ref, bf16[64,16,128]{2,1,0:T(8,128)(2,1)S(1)} %all-to-all-done.1.p00_ref, ...), custom_call_target="tpu_custom_call" | custom-call | flops 1677721600 | bytes 3145728 | tf_op jit(solution)/shard_map/pallas_call | solution.py:226
  58.6 0.0 collective-permute-start.5
  58.6 4.4 %all-to-all-start.2 = ((bf16[8,2,2,48,128]{4,3,2,1,0:T(8,128)(2,1)}), bf16[8,2,2,48,128]{4,3,2,1,0:T(8,128)(2,1)S(1)}, u32[]{:S(2)}, u32[]{:S(2)}) async-start(bf16[8,2,2,48,128]{4,3,2,1,0:T(8,128)(2,1)} %get-tuple-element.16), calls=%async_computation.2 | async-start | bytes 786432 | tf_op jit(solution)/shard_map/all_to_all | solution.py:244
  63.0 0.0 collective-permute-done.5.got_ref
  63.0 0.1 shard_map.125
  63.1 0.6 collective-permute-start.6
  63.8 7.7 %collective-permute-done.6.got_ref = bf16[64,16,128]{2,1,0:T(8,128)(2,1)S(1)} collective-permute-done((bf16[64,16,128]{2,1,0:T(8,128)(2,1)S(1)}, bf16[64,16,128]{2,1,0:T(8,128)(2,1)S(1)}, u32[]{:S(2)}, u32[]{:S(2)}) %collective-permute-start.6) | collective-permute-done | bytes 262176 | tf_op jit(solution)/shard_map/ppermute | solution.py:243
  71.5 0.8 shard_map.126
  72.3 5.9 %all-to-all-done.2.got_ref = bf16[8,2,2,48,128]{4,3,2,1,0:T(8,128)(2,1)S(1)} async-done(((bf16[8,2,2,48,128]{4,3,2,1,0:T(8,128)(2,1)}), bf16[8,2,2,48,128]{4,3,2,1,0:T(8,128)(2,1)S(1)}, u32[]{:S(2)}, u32[]{:S(2)}) %all-to-all-start.2) | async-done | bytes 393248 | tf_op jit(solution)/shard_map/all_to_all | solution.py:244
  78.2 5.6 %all-to-all-start.3 = ((bf16[64,16,128]{2,1,0:T(8,128)(2,1)}), bf16[64,16,128]{2,1,0:T(8,128)(2,1)S(1)}, u32[]{:S(2)}, u32[]{:S(2)}) async-start(bf16[64,16,128]{2,1,0:T(8,128)(2,1)} %shard_map.126), calls=%async_computation.3 | async-start | bytes 524288 | tf_op jit(solution)/shard_map/all_to_all | solution.py:247
  83.8 0.9 collective-permute-start.3
  84.7 8.0 %collective-permute-done.3.from_x_ref = bf16[8,2,48,128]{3,2,1,0:T(8,128)(2,1)S(1)} collective-permute-done((bf16[8,2,48,128]{3,2,1,0:T(8,128)(2,1)S(1)}, bf16[8,2,48,128]{3,2,1,0:T(8,128)(2,1)S(1)}, u32[]{:S(2)}, u32[]{:S(2)}) %collective-permute-start.3) | collective-permute-done | bytes 196640 | tf_op jit(solution)/shard_map/ppermute | solution.py:249
  92.7 0.1 collective-permute-start.4
  92.8 1.4 %collective-permute-done.4.from_core_ref = bf16[2,8,48,128]{3,2,1,0:T(8,128)(2,1)S(1)} collective-permute-done((bf16[2,8,48,128]{3,2,1,0:T(8,128)(2,1)S(1)}, bf16[2,8,48,128]{3,2,1,0:T(8,128)(2,1)S(1)}, u32[]{:S(2)}, u32[]{:S(2)}) %collective-permute-start.4) | collective-permute-done | bytes 196640 | tf_op jit(solution)/shard_map/ppermute | solution.py:251
  94.3 0.8 shard_map.124
  95.1 2.7 %all-to-all-done.3 = bf16[64,16,128]{2,1,0:T(8,128)(2,1)S(1)} async-done(((bf16[64,16,128]{2,1,0:T(8,128)(2,1)}), bf16[64,16,128]{2,1,0:T(8,128)(2,1)S(1)}, u32[]{:S(2)}, u32[]{:S(2)}) %all-to-all-start.3) | async-done | bytes 262176 | tf_op jit(solution)/shard_map/all_to_all | solution.py:247
  97.8 0.7 shard_map.127
  (2 shorter events, 0.0 us)
Async XLA Ops:
  2.2 14.7 %copy-start = (bf16[8,16,512]{2,1,0:T(8,128)(2,1)S(1)}, bf16[8,16,512]{2,1,0:T(8,128)(2,1)}, u32[]{:S(2)}) copy-start(bf16[8,16,512]{2,1,0:T(8,128)(2,1)} %q_ref.1) | copy-start | bytes 393220
  2.2 14.7 %copy-start.1 = (bf16[8,16,512]{2,1,0:T(8,128)(2,1)S(1)}, bf16[8,16,512]{2,1,0:T(8,128)(2,1)}, u32[]{:S(2)}) copy-start(bf16[8,16,512]{2,1,0:T(8,128)(2,1)} %k_ref.2) | copy-start | bytes 393220
  2.2 14.7 %copy-start.2 = (bf16[8,16,512]{2,1,0:T(8,128)(2,1)S(1)}, bf16[8,16,512]{2,1,0:T(8,128)(2,1)}, u32[]{:S(2)}) copy-start(bf16[8,16,512]{2,1,0:T(8,128)(2,1)} %v_ref.2) | copy-start | bytes 393220
  2.2 14.8 %copy-start.3 = (bf16[8,16,512]{2,1,0:T(8,128)(2,1)S(1)}, bf16[8,16,512]{2,1,0:T(8,128)(2,1)}, u32[]{:S(2)}) copy-start(bf16[8,16,512]{2,1,0:T(8,128)(2,1)} %o_ref.1) | copy-start | bytes 393220
  2.3 28.2 %all-to-all-start.1 = ((bf16[64,16,128]{2,1,0:T(8,128)(2,1)}), bf16[64,16,128]{2,1,0:T(8,128)(2,1)S(1)}, u32[]{:S(2)}, u32[]{:S(2)}) async-start(bf16[64,16,128]{2,1,0:T(8,128)(2,1)} %shard_map.120), calls=%async_computation.1 | async-start | bytes 524288 | tf_op jit(solution)/shard_map/all_to_all | solution.py:216
  17.9 34.4 %copy-start.4 = (f32[8]{0:T(128)S(1)}, f32[8]{0:T(128)}, u32[]{:S(2)}) copy-start(f32[8]{0:T(128)} %adv_ref.1) | copy-start | bytes 100
  17.9 34.4 %copy-start.5 = (s32[8]{0:T(128)S(1)}, s32[8]{0:T(128)}, u32[]{:S(2)}) copy-start(s32[8]{0:T(128)} %len_ref.1) | copy-start | bytes 100
  30.4 21.9 %all-to-all-start = ((bf16[32,64,128]{2,1,0:T(8,128)(2,1)}), bf16[32,64,128]{2,1,0:T(8,128)(2,1)S(1)}, u32[]{:S(2)}, u32[]{:S(2)}) async-start(bf16[32,64,128]{2,1,0:T(8,128)(2,1)} %shard_map.119), calls=%async_computation | async-start | bytes 1048576 | tf_op jit(solution)/shard_map/all_to_all | solution.py:223
  34.3 12.9 %collective-permute-start = (bf16[64,16,128]{2,1,0:T(8,128)(2,1)S(1)}, bf16[64,16,128]{2,1,0:T(8,128)(2,1)S(1)}, u32[]{:S(2)}, u32[]{:S(2)}) collective-permute-start(bf16[64,16,128]{2,1,0:T(8,128)(2,1)S(1)} %all-to-all-done.1.p00_ref), channel_id=1, source_target_pairs={{0,16},{16,0},{1,17},{17,1},{2,18},{18,2},{3,19},{19,3},{4,20},{20... | collective-permute-start | bytes 786440 | tf_op jit(solution)/shard_map/ppermute | solution.py:217
  36.1 11.2 %collective-permute-start.1 = (bf16[64,16,128]{2,1,0:T(8,128)(2,1)S(1)}, bf16[64,16,128]{2,1,0:T(8,128)(2,1)S(1)}, u32[]{:S(2)}, u32[]{:S(2)}) collective-permute-start(bf16[64,16,128]{2,1,0:T(8,128)(2,1)S(1)} %all-to-all-done.1.p00_ref), channel_id=1, source_target_pairs={{0,8},{8,0},{1,9},{9,1},{2,10},{10,2},{3,11},{11,3},{4,12},{12,4},... | collective-permute-start | bytes 786440 | tf_op jit(solution)/shard_map/ppermute | solution.py:218
  47.3 5.1 %collective-permute-start.2 = (bf16[64,16,128]{2,1,0:T(8,128)(2,1)S(1)}, bf16[64,16,128]{2,1,0:T(8,128)(2,1)S(1)}, u32[]{:S(2)}, u32[]{:S(2)}) collective-permute-start(bf16[64,16,128]{2,1,0:T(8,128)(2,1)S(1)} %collective-permute-done.p01_ref), channel_id=1, source_target_pairs={{0,8},{8,0},{1,9},{9,1},{2,10},{10,2},{3,11},{11,3},{4,12},{12,4},... | collective-permute-start | bytes 786440 | tf_op jit(solution)/shard_map/ppermute | solution.py:219
  58.6 4.4 %collective-permute-start.5 = (bf16[2,64,16,128]{3,2,1,0:T(8,128)(2,1)S(1)}, bf16[2,64,16,128]{3,2,1,0:T(8,128)(2,1)S(1)}, u32[]{:S(2)}, u32[]{:S(2)}) collective-permute-start(bf16[2,64,16,128]{3,2,1,0:T(8,128)(2,1)S(1)} %get-tuple-element.21), channel_id=1, source_target_pairs={{0,8},{8,0},{1,9},{9,1},{2,10},{10,2},{3,11},{11,3},{4,12},{12,4},... | collective-permute-start | bytes 1572872 | tf_op jit(solution)/shard_map/ppermute | solution.py:241
  58.6 19.6 %all-to-all-start.2 = ((bf16[8,2,2,48,128]{4,3,2,1,0:T(8,128)(2,1)}), bf16[8,2,2,48,128]{4,3,2,1,0:T(8,128)(2,1)S(1)}, u32[]{:S(2)}, u32[]{:S(2)}) async-start(bf16[8,2,2,48,128]{4,3,2,1,0:T(8,128)(2,1)} %get-tuple-element.16), calls=%async_computation.2 | async-start | bytes 786432 | tf_op jit(solution)/shard_map/all_to_all | solution.py:244
  63.1 8.4 %collective-permute-start.6 = (bf16[64,16,128]{2,1,0:T(8,128)(2,1)S(1)}, bf16[64,16,128]{2,1,0:T(8,128)(2,1)S(1)}, u32[]{:S(2)}, u32[]{:S(2)}) collective-permute-start(bf16[64,16,128]{2,1,0:T(8,128)(2,1)S(1)} %get-tuple-element.23), channel_id=1, source_target_pairs={{0,16},{16,0},{1,17},{17,1},{2,18},{18,2},{3,19},{19,3},{4,20},{20... | collective-permute-start | bytes 786440 | tf_op jit(solution)/shard_map/ppermute | solution.py:243
  78.2 19.6 %all-to-all-start.3 = ((bf16[64,16,128]{2,1,0:T(8,128)(2,1)}), bf16[64,16,128]{2,1,0:T(8,128)(2,1)S(1)}, u32[]{:S(2)}, u32[]{:S(2)}) async-start(bf16[64,16,128]{2,1,0:T(8,128)(2,1)} %shard_map.126), calls=%async_computation.3 | async-start | bytes 524288 | tf_op jit(solution)/shard_map/all_to_all | solution.py:247
  83.8 8.9 %collective-permute-start.3 = (bf16[8,2,48,128]{3,2,1,0:T(8,128)(2,1)S(1)}, bf16[8,2,48,128]{3,2,1,0:T(8,128)(2,1)S(1)}, u32[]{:S(2)}, u32[]{:S(2)}) collective-permute-start(bf16[8,2,48,128]{3,2,1,0:T(8,128)(2,1)S(1)} %shard_map.122), channel_id=1, source_target_pairs={{0,16},{16,0},{1,17},{17,1},{2,18},{18,2},{3,19},{19,3},{4,20},{20... | collective-permute-start | bytes 589832 | tf_op jit(solution)/shard_map/ppermute | solution.py:249
  92.7 1.5 %collective-permute-start.4 = (bf16[2,8,48,128]{3,2,1,0:T(8,128)(2,1)S(1)}, bf16[2,8,48,128]{3,2,1,0:T(8,128)(2,1)S(1)}, u32[]{:S(2)}, u32[]{:S(2)}) collective-permute-start(bf16[2,8,48,128]{3,2,1,0:T(8,128)(2,1)S(1)} %shard_map.123), channel_id=1, source_target_pairs={{0,8},{8,0},{1,9},{9,1},{2,10},{10,2},{3,11},{11,3},{4,12},{12,4},... | collective-permute-start | bytes 589832 | tf_op jit(solution)/shard_map/ppermute | solution.py:251

commit v4 on v3

--- a/solution.py
+++ b/solution.py
@@ -127,8 +127,8 @@
             for ct in range(2):
                 mine_ref[
                     z : z + count,
+                    ct,
                     jnp.bitwise_xor(x, xt),
-                    jnp.bitwise_xor(core, ct),
                     which * BLOCK : (which + 1) * BLOCK,
                     :,
                 ] = rows[:, xt * 2 + ct]
@@ -164,25 +164,17 @@
 
 
 def split_x_kernel(got_ref, out_ref):
-    out_ref[...] = got_ref[:, 1]
-
-
-def split_core_kernel(got_ref, from_x_ref, out_ref):
-    out_ref[0] = got_ref[:, 0, 1]
-    out_ref[1] = from_x_ref[:, 1]
-
-
-def unpack_resp_kernel(got_ref, from_x_ref, from_core_ref, q_ref, k_ref, v_ref):
-    x, core = lax.axis_index("x"), lax.axis_index("core")
+    out_ref[...] = got_ref[:, :, 1]
+
+
+def unpack_resp_kernel(got_ref, from_x_ref, q_ref, k_ref, v_ref):
+    x = lax.axis_index("x")
     for z in range(8):
         h = z // 2
         for dx in range(2):
-            for dc in range(2):
-                r = (z % 2) * 4 + jnp.bitwise_xor(x, dx) * 2 + jnp.bitwise_xor(core, dc)
-                if dc:
-                    rows = from_core_ref[dx, z]
-                else:
-                    rows = from_x_ref[z, 0] if dx else got_ref[z, 0, 0]
+            for c in range(2):
+                r = (z % 2) * 4 + jnp.bitwise_xor(x, dx) * 2 + c
+                rows = from_x_ref[z, c] if dx else got_ref[z, c, 0]
                 for i, ref in enumerate((q_ref, k_ref, v_ref)):
                     ref[r, :, h * HDIM : (h + 1) * HDIM] = rows[i * BLOCK : (i + 1) * BLOCK]
 
@@ -241,16 +233,16 @@
     got = lax.ppermute(send, "core", swap)
     keep, send = call(add_core_kernel, [(64, 16, HDIM)] * 2, 2)(keep, got)
     got = lax.ppermute(send, "x", swap)
-    back = lax.all_to_all(mine, ("zh", "zl"), 0, 0, tiled=True)
+    back = lax.all_to_all(
+        mine.reshape(16, 2, 3 * BLOCK, HDIM), ("zh", "zl", "core"), 0, 0, tiled=True
+    ).reshape(8, 2, 2, 3 * BLOCK, HDIM)
     (owned,) = call(add_x_kernel, [(64, 16, HDIM)], 2)(keep, got)
     owned, _ = lax.optimization_barrier((owned, back))
     owned = lax.all_to_all(owned, ("zh", "zl", "narrow"), 0, 0, tiled=True)
     (part,) = call(split_x_kernel, [(8, 2, 3 * BLOCK, HDIM)], 1)(back)
     from_x = lax.ppermute(part, "x", swap)
-    (part,) = call(split_core_kernel, [(2, 8, 3 * BLOCK, HDIM)], 2)(back, from_x)
-    from_core = lax.ppermute(part, "core", swap)
-    grad_q, grad_k, grad_v = call(unpack_resp_kernel, [(RESPONSES, BLOCK, 4 * HDIM)] * 3, 3)(
-        back, from_x, from_core
+    grad_q, grad_k, grad_v = call(unpack_resp_kernel, [(RESPONSES, BLOCK, 4 * HDIM)] * 3, 2)(
+        back, from_x
     )
     prompt_gk, prompt_gv = call(unpack_prompt_kernel, [(8, HEADS * HDIM)] * 2, 1)(
         owned.reshape(8, 8, 16, HDIM)

time: 99 us -> 99 us (level)
  starting transfers between devices: 32 us -> 33 us
  waiting for transfers between devices: 54.6 us -> 53.6 us
    all_to_all x1, waiting for transfers between devices: 5.93 us -> 4.04 us  [body(): lax.all_to_all(mine.reshape(16, 2, 3 * BLOCK, HDIM), ('zh', 'zl', 'core')...]
    all_to_all x1, starting transfers between devices: 5.59 us -> 7.33 us  [body(): owned = lax.all_to_all(owned, ('zh', 'zl', 'narrow'), 0, 0, tiled=True)]
    all_to_all x1, waiting for transfers between devices: 2.73 us -> 4.2 us  [body(): owned = lax.all_to_all(owned, ('zh', 'zl', 'narrow'), 0, 0, tiled=True)]
    ppermute x1 -> x0, waiting for transfers between devices: 1.43 us -> none  [body(): from_core = lax.ppermute(part, 'core', swap)]
  transfers between devices with their start and end apart: 11 -> 10, of which waited for: 8 -> 7; matrix products, arithmetic and copies ran while one was open for 0% -> 0% of each run, Pallas kernels for 3% -> 3%
where the time goes in v4:
time: 99 us; the launch traced here: 98.5 us
  waiting for transfers between devices  53.6 us (54%)
  starting transfers between devices  33 us (33%)
  Pallas kernels  11.1 us (11%)
    all_to_all x1, starting transfers between devices, body(): p00 = lax.all_to_all(sent_p, ('zh', 'zl', 'narrow'), 0, 0, tiled=True)  14.7 us
    all_to_all x1, waiting for transfers between devices, body(): p00 = lax.all_to_all(sent_p, ('zh', 'zl', 'narrow'), 0, 0, tiled=True)  12.5 us
    ppermute x1, waiting for transfers between devices, body(): p01 = lax.ppermute(p00, 'x', swap)  11.2 us
    ppermute x1, waiting for transfers between devices, body(): from_x = lax.ppermute(part, 'x', swap)  8.54 us
    ppermute x1, waiting for transfers between devices, body(): got = lax.ppermute(send, 'x', swap)  8.09 us
    all_to_all x1, starting transfers between devices, body(): owned = lax.all_to_all(owned, ('zh', 'zl', 'narrow'), 0, 0, tiled=True)  7.33 us
    pallas_call x1, Pallas kernels, body(): call(attn_kernel, [(8, 2, 2, 3 * BLOCK, HDIM), (2, 64, 16, HDIM), (2, 64,...  6.21 us
    all_to_all x1, waiting for transfers between devices, body(): got_r = lax.all_to_all(sent_r, WIDE, 0, 0, tiled=True)  5.08 us
  transfers between devices with their start and end apart: 10, of which 7 were waited for; matrix products, arithmetic and copies ran while one was open for 0% of the time, Pallas kernels for 3%

profile of v4, /device:TPU:8, one launch (start us, length us, event | category | flops | bytes accessed | tf_op | source)
XLA Modules:
  0.0 98.5 jit_solution(15621818971077866265)
XLA Ops:
  0.6 1.6 %shard_map.120 = bf16[64,16,128]{2,1,0:T(8,128)(2,1)} custom-call(bf16[8,4096]{1,0:T(8,128)(2,1)} %k_ref.3, bf16[8,4096]{1,0:T(8,128)(2,1)} %v_ref.3), custom_call_target="tpu_custom_call" | custom-call | bytes 1048576 | tf_op jit(solution)/shard_map/pallas_call | solution.py:207
  2.2 0.0 copy-start
  2.2 0.0 copy-start.1
  2.2 0.0 copy-start.2
  2.2 0.0 copy-start.3
  2.2 14.7 %all-to-all-start.1 = ((bf16[64,16,128]{2,1,0:T(8,128)(2,1)}), bf16[64,16,128]{2,1,0:T(8,128)(2,1)S(1)}, u32[]{:S(2)}, u32[]{:S(2)}) async-start(bf16[64,16,128]{2,1,0:T(8,128)(2,1)} %shard_map.120), calls=%async_computation.1 | async-start | bytes 524288 | tf_op jit(solution)/shard_map/all_to_all | solution.py:208
  17.0 0.0 copy-done
  17.0 0.0 copy-done.1
  17.0 0.0 copy-done.2
  17.0 0.0 copy-done.3
  17.0 0.9 shard_map.119
  17.9 0.0 copy-start.4
  17.9 0.0 copy-start.5
  17.9 12.5 %all-to-all-done.1.p00_ref = bf16[64,16,128]{2,1,0:T(8,128)(2,1)S(1)} async-done(((bf16[64,16,128]{2,1,0:T(8,128)(2,1)}), bf16[64,16,128]{2,1,0:T(8,128)(2,1)S(1)}, u32[]{:S(2)}, u32[]{:S(2)}) %all-to-all-start.1) | async-done | bytes 262176 | tf_op jit(solution)/shard_map/all_to_all | solution.py:208
  30.4 3.9 %all-to-all-start = ((bf16[32,64,128]{2,1,0:T(8,128)(2,1)}), bf16[32,64,128]{2,1,0:T(8,128)(2,1)S(1)}, u32[]{:S(2)}, u32[]{:S(2)}) async-start(bf16[32,64,128]{2,1,0:T(8,128)(2,1)} %shard_map.119), calls=%async_computation | async-start | bytes 1048576 | tf_op jit(solution)/shard_map/all_to_all | solution.py:215
  34.3 1.8 %collective-permute-start = (bf16[64,16,128]{2,1,0:T(8,128)(2,1)S(1)}, bf16[64,16,128]{2,1,0:T(8,128)(2,1)S(1)}, u32[]{:S(2)}, u32[]{:S(2)}) collective-permute-start(bf16[64,16,128]{2,1,0:T(8,128)(2,1)S(1)} %all-to-all-done.1.p00_ref), channel_id=1, source_target_pairs={{0,16},{16,0},{1,17},{17,1},{2,18},{18,2},{3,19},{19,3},{4,20},{20... | collective-permute-start | bytes 786440 | tf_op jit(solution)/shard_map/ppermute | solution.py:209
  36.1 0.0 collective-permute-start.1
  36.1 11.2 %collective-permute-done.p01_ref = bf16[64,16,128]{2,1,0:T(8,128)(2,1)S(1)} collective-permute-done((bf16[64,16,128]{2,1,0:T(8,128)(2,1)S(1)}, bf16[64,16,128]{2,1,0:T(8,128)(2,1)S(1)}, u32[]{:S(2)}, u32[]{:S(2)}) %collective-permute-start) | collective-permute-done | bytes 262176 | tf_op jit(solution)/shard_map/ppermute | solution.py:209
  47.2 0.0 collective-permute-start.2
  47.2 0.0 collective-permute-done.1.p10_ref
  47.3 5.1 %all-to-all-done.resp_ref = bf16[32,64,128]{2,1,0:T(8,128)(2,1)S(1)} async-done(((bf16[32,64,128]{2,1,0:T(8,128)(2,1)}), bf16[32,64,128]{2,1,0:T(8,128)(2,1)S(1)}, u32[]{:S(2)}, u32[]{:S(2)}) %all-to-all-start) | async-done | bytes 524320 | tf_op jit(solution)/shard_map/all_to_all | solution.py:215
  52.3 0.0 collective-permute-done.2.p11_ref
  52.3 0.0 copy-done.4
  52.3 0.0 copy-done.5
  52.3 6.2 %shard_map.121 = (bf16[8,2,2,48,128]{4,3,2,1,0:T(8,128)(2,1)}, bf16[2,64,16,128]{3,2,1,0:T(8,128)(2,1)S(1)}, bf16[2,64,16,128]{3,2,1,0:T(8,128)(2,1)S(1)}) custom-call(f32[8]{0:T(128)S(1)} %copy-done.4, s32[8]{0:T(128)S(1)} %copy-done.5, bf16[32,64,128]{2,1,0:T(8,128)(2,1)S(1)} %all-to-all-done.resp_ref, bf16[64,16,128]{2,1,0:T(8,128)(2,1)S(1)} %all-to-all-done.1.p00_ref, ...), custom_call_target="tpu_custom_call" | custom-call | flops 1677721600 | bytes 3145728 | tf_op jit(solution)/shard_map/pallas_call | solution.py:218
  58.6 0.0 collective-permute-start.4
  58.6 4.5 %all-to-all-start.2 = ((bf16[16,2,48,128]{3,2,1,0:T(8,128)(2,1)}), bf16[16,2,48,128]{3,2,1,0:T(8,128)(2,1)S(1)}, u32[]{:S(2)}, u32[]{:S(2)}) async-start(bf16[16,2,48,128]{3,2,1,0:T(8,128)(2,1)} %bitcast), calls=%async_computation.2 | async-start | bytes 786432 | tf_op jit(solution)/shard_map/all_to_all | solution.py:236
  63.1 0.0 collective-permute-done.4.got_ref
  63.1 0.1 shard_map.124
  63.2 0.6 collective-permute-start.5
  63.9 8.1 %collective-permute-done.5.got_ref = bf16[64,16,128]{2,1,0:T(8,128)(2,1)S(1)} collective-permute-done((bf16[64,16,128]{2,1,0:T(8,128)(2,1)S(1)}, bf16[64,16,128]{2,1,0:T(8,128)(2,1)S(1)}, u32[]{:S(2)}, u32[]{:S(2)}) %collective-permute-start.5) | collective-permute-done | bytes 262176 | tf_op jit(solution)/shard_map/ppermute | solution.py:235
  72.0 0.8 shard_map.125
  72.7 4.0 %all-to-all-done.2 = bf16[16,2,48,128]{3,2,1,0:T(8,128)(2,1)S(1)} async-done(((bf16[16,2,48,128]{3,2,1,0:T(8,128)(2,1)}), bf16[16,2,48,128]{3,2,1,0:T(8,128)(2,1)S(1)}, u32[]{:S(2)}, u32[]{:S(2)}) %all-to-all-start.2) | async-done | bytes 393248 | tf_op jit(solution)/shard_map/all_to_all | solution.py:236
  76.8 7.3 %all-to-all-start.3 = ((bf16[64,16,128]{2,1,0:T(8,128)(2,1)}), bf16[64,16,128]{2,1,0:T(8,128)(2,1)S(1)}, u32[]{:S(2)}, u32[]{:S(2)}) async-start(bf16[64,16,128]{2,1,0:T(8,128)(2,1)} %shard_map.125), calls=%async_computation.3 | async-start | bytes 524288 | tf_op jit(solution)/shard_map/all_to_all | solution.py:241
  84.1 0.1 collective-permute-start.3
  84.2 8.5 %collective-permute-done.3.from_x_ref = bf16[8,2,48,128]{3,2,1,0:T(8,128)(2,1)S(1)} collective-permute-done((bf16[8,2,48,128]{3,2,1,0:T(8,128)(2,1)S(1)}, bf16[8,2,48,128]{3,2,1,0:T(8,128)(2,1)S(1)}, u32[]{:S(2)}, u32[]{:S(2)}) %collective-permute-start.3) | collective-permute-done | bytes 196640 | tf_op jit(solution)/shard_map/ppermute | solution.py:243
  92.8 0.8 shard_map.123
  93.6 4.2 %all-to-all-done.3 = bf16[64,16,128]{2,1,0:T(8,128)(2,1)S(1)} async-done(((bf16[64,16,128]{2,1,0:T(8,128)(2,1)}), bf16[64,16,128]{2,1,0:T(8,128)(2,1)S(1)}, u32[]{:S(2)}, u32[]{:S(2)}) %all-to-all-start.3) | async-done | bytes 262176 | tf_op jit(solution)/shard_map/all_to_all | solution.py:241
  97.8 0.7 shard_map.126
  (1 shorter events, 0.0 us)
Async XLA Ops:
  2.2 14.7 %copy-start = (bf16[8,16,512]{2,1,0:T(8,128)(2,1)S(1)}, bf16[8,16,512]{2,1,0:T(8,128)(2,1)}, u32[]{:S(2)}) copy-start(bf16[8,16,512]{2,1,0:T(8,128)(2,1)} %q_ref.1) | copy-start | bytes 393220
  2.2 14.7 %copy-start.1 = (bf16[8,16,512]{2,1,0:T(8,128)(2,1)S(1)}, bf16[8,16,512]{2,1,0:T(8,128)(2,1)}, u32[]{:S(2)}) copy-start(bf16[8,16,512]{2,1,0:T(8,128)(2,1)} %k_ref.2) | copy-start | bytes 393220
  2.2 14.7 %copy-start.2 = (bf16[8,16,512]{2,1,0:T(8,128)(2,1)S(1)}, bf16[8,16,512]{2,1,0:T(8,128)(2,1)}, u32[]{:S(2)}) copy-start(bf16[8,16,512]{2,1,0:T(8,128)(2,1)} %v_ref.2) | copy-start | bytes 393220
  2.2 14.8 %copy-start.3 = (bf16[8,16,512]{2,1,0:T(8,128)(2,1)S(1)}, bf16[8,16,512]{2,1,0:T(8,128)(2,1)}, u32[]{:S(2)}) copy-start(bf16[8,16,512]{2,1,0:T(8,128)(2,1)} %o_ref.1) | copy-start | bytes 393220
  2.2 28.2 %all-to-all-start.1 = ((bf16[64,16,128]{2,1,0:T(8,128)(2,1)}), bf16[64,16,128]{2,1,0:T(8,128)(2,1)S(1)}, u32[]{:S(2)}, u32[]{:S(2)}) async-start(bf16[64,16,128]{2,1,0:T(8,128)(2,1)} %shard_map.120), calls=%async_computation.1 | async-start | bytes 524288 | tf_op jit(solution)/shard_map/all_to_all | solution.py:208
  17.9 34.4 %copy-start.4 = (f32[8]{0:T(128)S(1)}, f32[8]{0:T(128)}, u32[]{:S(2)}) copy-start(f32[8]{0:T(128)} %adv_ref.1) | copy-start | bytes 100
  17.9 34.4 %copy-start.5 = (s32[8]{0:T(128)S(1)}, s32[8]{0:T(128)}, u32[]{:S(2)}) copy-start(s32[8]{0:T(128)} %len_ref.1) | copy-start | bytes 100
  30.4 21.9 %all-to-all-start = ((bf16[32,64,128]{2,1,0:T(8,128)(2,1)}), bf16[32,64,128]{2,1,0:T(8,128)(2,1)S(1)}, u32[]{:S(2)}, u32[]{:S(2)}) async-start(bf16[32,64,128]{2,1,0:T(8,128)(2,1)} %shard_map.119), calls=%async_computation | async-start | bytes 1048576 | tf_op jit(solution)/shard_map/all_to_all | solution.py:215
  34.3 12.9 %collective-permute-start = (bf16[64,16,128]{2,1,0:T(8,128)(2,1)S(1)}, bf16[64,16,128]{2,1,0:T(8,128)(2,1)S(1)}, u32[]{:S(2)}, u32[]{:S(2)}) collective-permute-start(bf16[64,16,128]{2,1,0:T(8,128)(2,1)S(1)} %all-to-all-done.1.p00_ref), channel_id=1, source_target_pairs={{0,16},{16,0},{1,17},{17,1},{2,18},{18,2},{3,19},{19,3},{4,20},{20... | collective-permute-start | bytes 786440 | tf_op jit(solution)/shard_map/ppermute | solution.py:209
  36.1 11.2 %collective-permute-start.1 = (bf16[64,16,128]{2,1,0:T(8,128)(2,1)S(1)}, bf16[64,16,128]{2,1,0:T(8,128)(2,1)S(1)}, u32[]{:S(2)}, u32[]{:S(2)}) collective-permute-start(bf16[64,16,128]{2,1,0:T(8,128)(2,1)S(1)} %all-to-all-done.1.p00_ref), channel_id=1, source_target_pairs={{0,8},{8,0},{1,9},{9,1},{2,10},{10,2},{3,11},{11,3},{4,12},{12,4},... | collective-permute-start | bytes 786440 | tf_op jit(solution)/shard_map/ppermute | solution.py:210
  47.2 5.1 %collective-permute-start.2 = (bf16[64,16,128]{2,1,0:T(8,128)(2,1)S(1)}, bf16[64,16,128]{2,1,0:T(8,128)(2,1)S(1)}, u32[]{:S(2)}, u32[]{:S(2)}) collective-permute-start(bf16[64,16,128]{2,1,0:T(8,128)(2,1)S(1)} %collective-permute-done.p01_ref), channel_id=1, source_target_pairs={{0,8},{8,0},{1,9},{9,1},{2,10},{10,2},{3,11},{11,3},{4,12},{12,4},... | collective-permute-start | bytes 786440 | tf_op jit(solution)/shard_map/ppermute | solution.py:211
  58.6 4.5 %collective-permute-start.4 = (bf16[2,64,16,128]{3,2,1,0:T(8,128)(2,1)S(1)}, bf16[2,64,16,128]{3,2,1,0:T(8,128)(2,1)S(1)}, u32[]{:S(2)}, u32[]{:S(2)}) collective-permute-start(bf16[2,64,16,128]{3,2,1,0:T(8,128)(2,1)S(1)} %get-tuple-element.21), channel_id=1, source_target_pairs={{0,8},{8,0},{1,9},{9,1},{2,10},{10,2},{3,11},{11,3},{4,12},{12,4},... | collective-permute-start | bytes 1572872 | tf_op jit(solution)/shard_map/ppermute | solution.py:233
  58.6 18.2 %all-to-all-start.2 = ((bf16[16,2,48,128]{3,2,1,0:T(8,128)(2,1)}), bf16[16,2,48,128]{3,2,1,0:T(8,128)(2,1)S(1)}, u32[]{:S(2)}, u32[]{:S(2)}) async-start(bf16[16,2,48,128]{3,2,1,0:T(8,128)(2,1)} %bitcast), calls=%async_computation.2 | async-start | bytes 786432 | tf_op jit(solution)/shard_map/all_to_all | solution.py:236
  63.2 8.7 %collective-permute-start.5 = (bf16[64,16,128]{2,1,0:T(8,128)(2,1)S(1)}, bf16[64,16,128]{2,1,0:T(8,128)(2,1)S(1)}, u32[]{:S(2)}, u32[]{:S(2)}) collective-permute-start(bf16[64,16,128]{2,1,0:T(8,128)(2,1)S(1)} %get-tuple-element.23), channel_id=1, source_target_pairs={{0,16},{16,0},{1,17},{17,1},{2,18},{18,2},{3,19},{19,3},{4,20},{20... | collective-permute-start | bytes 786440 | tf_op jit(solution)/shard_map/ppermute | solution.py:235
  76.8 21.0 %all-to-all-start.3 = ((bf16[64,16,128]{2,1,0:T(8,128)(2,1)}), bf16[64,16,128]{2,1,0:T(8,128)(2,1)S(1)}, u32[]{:S(2)}, u32[]{:S(2)}) async-start(bf16[64,16,128]{2,1,0:T(8,128)(2,1)} %shard_map.125), calls=%async_computation.3 | async-start | bytes 524288 | tf_op jit(solution)/shard_map/all_to_all | solution.py:241
  84.1 8.6 %collective-permute-start.3 = (bf16[8,2,48,128]{3,2,1,0:T(8,128)(2,1)S(1)}, bf16[8,2,48,128]{3,2,1,0:T(8,128)(2,1)S(1)}, u32[]{:S(2)}, u32[]{:S(2)}) collective-permute-start(bf16[8,2,48,128]{3,2,1,0:T(8,128)(2,1)S(1)} %shard_map.122), channel_id=1, source_target_pairs={{0,16},{16,0},{1,17},{17,1},{2,18},{18,2},{3,19},{19,3},{4,20},{20... | collective-permute-start | bytes 589832 | tf_op jit(solution)/shard_map/ppermute | solution.py:243

commit v5 on v4

--- a/solution.py
+++ b/solution.py
@@ -1,7 +1,9 @@
 import functools
+import math
 
 import jax
 import jax.numpy as jnp
+import numpy as np
 from jax import lax
 from jax.experimental import pallas as pl
 from jax.experimental.pallas import tpu as pltpu
@@ -14,6 +16,7 @@
 PROMPT = 2048
 BLOCK = 16
 CHUNK = 256
+FLIP_IN, FLIP_RESP, FLIP_BACK, FLIP_OUT = 32, 16, 8, 32
 LOG2E = 1.4426950408889634
 F32 = jnp.float32
 BF16 = jnp.bfloat16
@@ -35,15 +38,15 @@
             cols = slice((n * 4 + zh) * HDIM, (n * 4 + zh + 1) * HDIM)
             both = jnp.concatenate([keys[:, cols], values[:, cols]], axis=0)
             both = both.astype(BF16)
-            out_ref[zh * 16 + n] = both
-            out_ref[zh * 16 + 8 + n] = both
+            out_ref[(zh * 16 + n) ^ FLIP_IN] = both
+            out_ref[(zh * 16 + 8 + n) ^ FLIP_IN] = both
 
 
 def pack_resp_kernel(q_ref, k_ref, v_ref, o_ref, out_ref):
     for h in range(4):
         for r in range(RESPONSES):
             for i, ref in enumerate((q_ref, k_ref, v_ref, o_ref)):
-                out_ref[h * 8 + r, i * BLOCK : (i + 1) * BLOCK, :] = ref[
+                out_ref[(h * 8 + r) ^ FLIP_RESP, i * BLOCK : (i + 1) * BLOCK, :] = ref[
                     r, :, h * HDIM : (h + 1) * HDIM
                 ]
 
@@ -66,20 +69,26 @@
     n_prompt = PROMPT // CHUNK
     n_chunks = (PROMPT + RESP) // CHUNK
 
-    queries = resp_ref[:, 0:BLOCK, :].reshape(RESP, HDIM)
-    k_s[PROMPT:, :] = resp_ref[:, BLOCK : 2 * BLOCK, :].reshape(RESP, HDIM)
-    v_s[PROMPT:, :] = resp_ref[:, 2 * BLOCK : 3 * BLOCK, :].reshape(RESP, HDIM)
+    def take(which):
+        cols = slice(which * BLOCK, (which + 1) * BLOCK)
+        low, high = (resp_ref[i : i + 16, cols, :].reshape(RESP // 2, HDIM) for i in (0, 16))
+        return jnp.concatenate([high, low] if FLIP_RESP else [low, high], axis=0)
+
+    queries = take(0)
+    k_s[PROMPT:, :] = take(1)
+    v_s[PROMPT:, :] = take(2)
     gain = adv_ref[me]
     length = len_ref[me]
     row = lax.broadcasted_iota(jnp.int32, (RESP, HDIM), 0)
     weight = jnp.where(row < length, gain, 0.0)
-    cot = resp_ref[:, 3 * BLOCK : 4 * BLOCK, :].reshape(RESP, HDIM)
+    cot = take(3)
     grad = (cot.astype(F32) * weight).astype(BF16)
 
     power = jnp.full((8, HDIM), head + 1, jnp.int32).astype(F32) * (-8.0 / HEADS)
     slope = (jnp.exp2(power) * (128.0 / (PROMPT + RESP) * LOG2E))[0:1, :]
     key_row = lax.broadcasted_iota(jnp.int32, (CHUNK, HDIM), 0)
-    prompt_row = ((key_row // 64) * 256 + key_row % 64 - PROMPT).astype(F32)
+    block = jnp.bitwise_xor(key_row // 8, FLIP_IN % 32)
+    prompt_row = ((block // 8) * 256 + (block % 8) * 8 + key_row % 8 - PROMPT).astype(F32)
     resp_row = key_row.astype(F32)
 
     def wide4(x):
@@ -91,7 +100,7 @@
         if c < n_prompt:
             dc, dx, half = c % 2, (c // 2) % 2, c // 4
             both = parts[dc][dx][half * 32 : (half + 1) * 32].astype(F32)
-            place = half * 1024 + jnp.bitwise_xor(x, dx) * 128 + jnp.bitwise_xor(core, dc) * 64
+            place = (half ^ (FLIP_IN // 32)) * 1024 + jnp.bitwise_xor(x, dx) * 128 + jnp.bitwise_xor(core, dc) * 64
             k_s[rows, :] = both[:, 0:8, :].reshape(CHUNK, HDIM).astype(BF16)
             v_s[rows, :] = both[:, 8:16, :].reshape(CHUNK, HDIM).astype(BF16)
             bias = slope * (prompt_row + place.astype(F32))
@@ -125,13 +134,15 @@
         rows = rows.astype(BF16).reshape(count, 4, BLOCK, HDIM)
         for xt in range(2):
             for ct in range(2):
-                mine_ref[
-                    z : z + count,
-                    ct,
-                    jnp.bitwise_xor(x, xt),
-                    which * BLOCK : (which + 1) * BLOCK,
-                    :,
-                ] = rows[:, xt * 2 + ct]
+                for i in range(0, count, 4):
+                    at = (z + i) ^ (FLIP_BACK // 2)
+                    mine_ref[
+                        at : at + 4,
+                        ct,
+                        jnp.bitwise_xor(x, xt),
+                        which * BLOCK : (which + 1) * BLOCK,
+                        :,
+                    ] = rows[i : i + 4, xt * 2 + ct]
 
     dq = jnp.zeros((HDIM, RESP), F32)
     for c in range(n_chunks):
@@ -174,7 +185,8 @@
         for dx in range(2):
             for c in range(2):
                 r = (z % 2) * 4 + jnp.bitwise_xor(x, dx) * 2 + c
-                rows = from_x_ref[z, c] if dx else got_ref[z, c, 0]
+                at = z ^ (FLIP_BACK // 2)
+                rows = from_x_ref[at, c] if dx else got_ref[at, c, 0]
                 for i, ref in enumerate((q_ref, k_ref, v_ref)):
                     ref[r, :, h * HDIM : (h + 1) * HDIM] = rows[i * BLOCK : (i + 1) * BLOCK]
 
@@ -183,9 +195,27 @@
     for zh in range(4):
         for n in range(8):
             cols = slice((n * 4 + zh) * HDIM, (n * 4 + zh + 1) * HDIM)
-            both = got_ref[zh * 2, n].astype(F32) + got_ref[zh * 2 + 1, n].astype(F32)
+            both = (
+                got_ref[(zh * 16 + n) ^ FLIP_OUT].astype(F32)
+                + got_ref[(zh * 16 + 8 + n) ^ FLIP_OUT].astype(F32)
+            )
             k_ref[:, cols] = both[0:8].astype(BF16)
             v_ref[:, cols] = both[8:16].astype(BF16)
+
+
+def groups_of(axes, flip):
+    sizes = dict(zip(AXES, (4, 2, 2, 2, 8)))
+    ids = np.arange(256).reshape([sizes[a] for a in AXES])
+    rest = [a for a in AXES if a not in axes]
+    ids = ids.transpose([AXES.index(a) for a in rest + list(axes)])
+    ids = ids.reshape(-1, math.prod(sizes[a] for a in axes))
+    return ids[:, np.arange(ids.shape[1]) ^ flip].tolist()
+
+
+def exchange(x, axes, flip):
+    return lax.all_to_all(
+        x, AXES, 0, 0, axis_index_groups=groups_of(axes, flip), tiled=True
+    )
 
 
 def call(kernel, outs, n_in, scratch=(), smem=0, params=PARAMS, flops=0, bytes_accessed=1 << 20):
@@ -205,14 +235,14 @@
 def body(resp_q, resp_k, resp_v, resp_dout, advantage, resp_len, prompt_k, prompt_v):
     swap = [(0, 1), (1, 0)]
     (sent_p,) = call(pack_prompt_kernel, [(64, 16, HDIM)], 2, params=None)(prompt_k, prompt_v)
-    p00 = lax.all_to_all(sent_p, ("zh", "zl", "narrow"), 0, 0, tiled=True)
+    p00 = exchange(sent_p, ("zh", "zl", "narrow"), FLIP_IN)
     p01 = lax.ppermute(p00, "x", swap)
     p10 = lax.ppermute(p00, "core", swap)
     p11 = lax.ppermute(p01, "core", swap)
     (sent_r,) = call(pack_resp_kernel, [(32, 4 * BLOCK, HDIM)], 4)(
         resp_q, resp_k, resp_v, resp_dout
     )
-    got_r = lax.all_to_all(sent_r, WIDE, 0, 0, tiled=True)
+    got_r = exchange(sent_r, WIDE, FLIP_RESP)
 
     keys = PROMPT + RESP
     mine, keep, send = call(
@@ -233,19 +263,18 @@
     got = lax.ppermute(send, "core", swap)
     keep, send = call(add_core_kernel, [(64, 16, HDIM)] * 2, 2)(keep, got)
     got = lax.ppermute(send, "x", swap)
-    back = lax.all_to_all(
-        mine.reshape(16, 2, 3 * BLOCK, HDIM), ("zh", "zl", "core"), 0, 0, tiled=True
-    ).reshape(8, 2, 2, 3 * BLOCK, HDIM)
+    back = exchange(mine.reshape(16, 2, 3 * BLOCK, HDIM), ("zh", "zl", "core"), FLIP_BACK)
+    back = back.reshape(8, 2, 2, 3 * BLOCK, HDIM)
     (owned,) = call(add_x_kernel, [(64, 16, HDIM)], 2)(keep, got)
     owned, _ = lax.optimization_barrier((owned, back))
-    owned = lax.all_to_all(owned, ("zh", "zl", "narrow"), 0, 0, tiled=True)
+    owned = exchange(owned, ("zh", "zl", "narrow"), FLIP_OUT)
     (part,) = call(split_x_kernel, [(8, 2, 3 * BLOCK, HDIM)], 1)(back)
     from_x = lax.ppermute(part, "x", swap)
     grad_q, grad_k, grad_v = call(unpack_resp_kernel, [(RESPONSES, BLOCK, 4 * HDIM)] * 3, 2)(
         back, from_x
     )
     prompt_gk, prompt_gv = call(unpack_prompt_kernel, [(8, HEADS * HDIM)] * 2, 1)(
-        owned.reshape(8, 8, 16, HDIM)
+        owned
     )
     return grad_q, grad_k, grad_v, prompt_gk, prompt_gv
 

time: 99 us -> 98.1 us (level); the launches traced: 98.5 us -> 96.3 us
  waiting for transfers between devices: 53.6 us -> 40.3 us
  starting transfers between devices: 33 us -> 44.2 us
    all_to_all x4, waiting for transfers between devices: 25.8 us -> 10.8 us  [exchange(): lax.all_to_all(x, AXES, 0, 0, axis_index_groups=groups_of(axes, flip), ti...]
    all_to_all x4, starting transfers between devices: 30.5 us -> 41.7 us  [exchange(): lax.all_to_all(x, AXES, 0, 0, axis_index_groups=groups_of(axes, flip), ti...]
    ppermute x1, waiting for transfers between devices: 0.01 us -> 1.52 us  [body(): p11 = lax.ppermute(p01, 'core', swap)]
    ppermute x1, waiting for transfers between devices: 11.2 us -> 12.2 us  [body(): p01 = lax.ppermute(p00, 'x', swap)]
where the time goes in v5:
time: 98.1 us; the launch traced here: 96.3 us
  starting transfers between devices  44.2 us (45%)
  waiting for transfers between devices  40.3 us (41%)
  Pallas kernels  11.1 us (11%)
    all_to_all x4, starting transfers between devices, exchange(): lax.all_to_all(x, AXES, 0, 0, axis_index_groups=groups_of(axes, flip), ti...  41.7 us
    ppermute x1, waiting for transfers between devices, body(): p01 = lax.ppermute(p00, 'x', swap)  12.2 us
    all_to_all x4, waiting for transfers between devices, exchange(): lax.all_to_all(x, AXES, 0, 0, axis_index_groups=groups_of(axes, flip), ti...  10.8 us
    ppermute x1, waiting for transfers between devices, body(): from_x = lax.ppermute(part, 'x', swap)  7.83 us
    ppermute x1, waiting for transfers between devices, body(): got = lax.ppermute(send, 'x', swap)  7.81 us
    pallas_call x1, Pallas kernels, body(): call(attn_kernel, [(8, 2, 2, 3 * BLOCK, HDIM), (2, 64, 16, HDIM), (2, 64,...  6.21 us
  transfers between devices with their start and end apart: 10, of which 7 were waited for; matrix products, arithmetic and copies ran while one was open for 0% of the time, Pallas kernels for 3%

profile of v5, /device:TPU:8, one launch (start us, length us, event | category | flops | bytes accessed | tf_op | source)
XLA Modules:
  0.0 96.3 jit_solution(9235661003194571473)
XLA Ops:
  0.6 1.6 %shard_map.120 = bf16[64,16,128]{2,1,0:T(8,128)(2,1)} custom-call(bf16[8,4096]{1,0:T(8,128)(2,1)} %k_ref.3, bf16[8,4096]{1,0:T(8,128)(2,1)} %v_ref.3), custom_call_target="tpu_custom_call" | custom-call | bytes 1048576 | tf_op jit(solution)/shard_map/pallas_call | solution.py:237
  2.2 0.0 copy-start
  2.2 0.0 copy-start.1
  2.2 0.0 copy-start.2
  2.2 0.0 copy-start.3
  2.2 16.2 %all-to-all-start.1 = ((bf16[64,16,128]{2,1,0:T(8,128)(2,1)}), bf16[64,16,128]{2,1,0:T(8,128)(2,1)S(1)}, u32[]{:S(2)}, u32[]{:S(2)}) async-start(bf16[64,16,128]{2,1,0:T(8,128)(2,1)} %shard_map.120), calls=%async_computation.1 | async-start | bytes 524288 | tf_op jit(solution)/shard_map/all_to_all | solution.py:216
  18.4 0.0 copy-done
  18.4 0.0 copy-done.1
  18.5 0.0 copy-done.2
  18.5 0.0 copy-done.3
  18.5 0.9 shard_map.119
  19.4 0.0 copy-start.4
  19.4 0.0 copy-start.5
  19.4 8.8 %all-to-all-done.1.p00_ref = bf16[64,16,128]{2,1,0:T(8,128)(2,1)S(1)} async-done(((bf16[64,16,128]{2,1,0:T(8,128)(2,1)}), bf16[64,16,128]{2,1,0:T(8,128)(2,1)S(1)}, u32[]{:S(2)}, u32[]{:S(2)}) %all-to-all-start.1) | async-done | bytes 262176 | tf_op jit(solution)/shard_map/all_to_all | solution.py:216
  28.2 7.8 %all-to-all-start = ((bf16[32,64,128]{2,1,0:T(8,128)(2,1)}), bf16[32,64,128]{2,1,0:T(8,128)(2,1)S(1)}, u32[]{:S(2)}, u32[]{:S(2)}) async-start(bf16[32,64,128]{2,1,0:T(8,128)(2,1)} %shard_map.119), calls=%async_computation | async-start | bytes 1048576 | tf_op jit(solution)/shard_map/all_to_all | solution.py:216
  36.0 1.6 %collective-permute-start = (bf16[64,16,128]{2,1,0:T(8,128)(2,1)S(1)}, bf16[64,16,128]{2,1,0:T(8,128)(2,1)S(1)}, u32[]{:S(2)}, u32[]{:S(2)}) collective-permute-start(bf16[64,16,128]{2,1,0:T(8,128)(2,1)S(1)} %all-to-all-done.1.p00_ref), channel_id=1, source_target_pairs={{0,16},{16,0},{1,17},{17,1},{2,18},{18,2},{3,19},{19,3},{4,20},{20... | collective-permute-start | bytes 786440 | tf_op jit(solution)/shard_map/ppermute | solution.py:239
  37.6 0.0 collective-permute-start.1
  37.6 12.2 %collective-permute-done.p01_ref = bf16[64,16,128]{2,1,0:T(8,128)(2,1)S(1)} collective-permute-done((bf16[64,16,128]{2,1,0:T(8,128)(2,1)S(1)}, bf16[64,16,128]{2,1,0:T(8,128)(2,1)S(1)}, u32[]{:S(2)}, u32[]{:S(2)}) %collective-permute-start) | collective-permute-done | bytes 262176 | tf_op jit(solution)/shard_map/ppermute | solution.py:239
  49.8 0.0 collective-permute-start.2
  49.8 0.0 collective-permute-done.1.p10_ref
  49.8 0.0 all-to-all-done.resp_ref
  49.8 1.5 %collective-permute-done.2.p11_ref = bf16[64,16,128]{2,1,0:T(8,128)(2,1)S(1)} collective-permute-done((bf16[64,16,128]{2,1,0:T(8,128)(2,1)S(1)}, bf16[64,16,128]{2,1,0:T(8,128)(2,1)S(1)}, u32[]{:S(2)}, u32[]{:S(2)}) %collective-permute-start.2) | collective-permute-done | bytes 262176 | tf_op jit(solution)/shard_map/ppermute | solution.py:241
  51.3 0.0 copy-done.4
  51.3 0.0 copy-done.5
  51.3 6.2 %shard_map.121 = (bf16[8,2,2,48,128]{4,3,2,1,0:T(8,128)(2,1)}, bf16[2,64,16,128]{3,2,1,0:T(8,128)(2,1)S(1)}, bf16[2,64,16,128]{3,2,1,0:T(8,128)(2,1)S(1)}) custom-call(f32[8]{0:T(128)S(1)} %copy-done.4, s32[8]{0:T(128)S(1)} %copy-done.5, bf16[32,64,128]{2,1,0:T(8,128)(2,1)S(1)} %all-to-all-done.resp_ref, bf16[64,16,128]{2,1,0:T(8,128)(2,1)S(1)} %all-to-all-done.1.p00_ref, ...), custom_call_target="tpu_custom_call" | custom-call | flops 1677721600 | bytes 3145728 | tf_op jit(solution)/shard_map/pallas_call | solution.py:248
  57.6 0.1 collective-permute-start.4
  57.7 7.2 %all-to-all-start.2 = ((bf16[16,2,48,128]{3,2,1,0:T(8,128)(2,1)}), bf16[16,2,48,128]{3,2,1,0:T(8,128)(2,1)S(1)}, u32[]{:S(2)}, u32[]{:S(2)}) async-start(bf16[16,2,48,128]{3,2,1,0:T(8,128)(2,1)} %bitcast), calls=%async_computation.2 | async-start | bytes 786432 | tf_op jit(solution)/shard_map/all_to_all | solution.py:216
  64.9 0.0 collective-permute-done.4.got_ref
  64.9 0.1 shard_map.124
  65.1 0.6 collective-permute-start.5
  65.7 7.8 %collective-permute-done.5.got_ref = bf16[64,16,128]{2,1,0:T(8,128)(2,1)S(1)} collective-permute-done((bf16[64,16,128]{2,1,0:T(8,128)(2,1)S(1)}, bf16[64,16,128]{2,1,0:T(8,128)(2,1)S(1)}, u32[]{:S(2)}, u32[]{:S(2)}) %collective-permute-start.5) | collective-permute-done | bytes 262176 | tf_op jit(solution)/shard_map/ppermute | solution.py:265
  73.5 0.8 shard_map.125
  74.3 0.8 all-to-all-done.2
  75.1 10.5 %all-to-all-start.3 = ((bf16[64,16,128]{2,1,0:T(8,128)(2,1)}), bf16[64,16,128]{2,1,0:T(8,128)(2,1)S(1)}, u32[]{:S(2)}, u32[]{:S(2)}) async-start(bf16[64,16,128]{2,1,0:T(8,128)(2,1)} %shard_map.125), calls=%async_computation.3 | async-start | bytes 524288 | tf_op jit(solution)/shard_map/all_to_all | solution.py:216
  85.6 0.1 collective-permute-start.3
  85.7 7.8 %collective-permute-done.3.from_x_ref = bf16[8,2,48,128]{3,2,1,0:T(8,128)(2,1)S(1)} collective-permute-done((bf16[8,2,48,128]{3,2,1,0:T(8,128)(2,1)S(1)}, bf16[8,2,48,128]{3,2,1,0:T(8,128)(2,1)S(1)}, u32[]{:S(2)}, u32[]{:S(2)}) %collective-permute-start.3) | collective-permute-done | bytes 196640 | tf_op jit(solution)/shard_map/ppermute | solution.py:272
  93.6 0.8 shard_map.123
  94.4 1.2 %all-to-all-done.3.got_ref = bf16[64,16,128]{2,1,0:T(8,128)(2,1)S(1)} async-done(((bf16[64,16,128]{2,1,0:T(8,128)(2,1)}), bf16[64,16,128]{2,1,0:T(8,128)(2,1)S(1)}, u32[]{:S(2)}, u32[]{:S(2)}) %all-to-all-start.3) | async-done | bytes 262176 | tf_op jit(solution)/shard_map/all_to_all | solution.py:216
  95.6 0.7 shard_map.126
  (1 shorter events, 0.0 us)
Async XLA Ops:
  2.2 16.2 %copy-start = (bf16[8,16,512]{2,1,0:T(8,128)(2,1)S(1)}, bf16[8,16,512]{2,1,0:T(8,128)(2,1)}, u32[]{:S(2)}) copy-start(bf16[8,16,512]{2,1,0:T(8,128)(2,1)} %q_ref.1) | copy-start | bytes 393220
  2.2 16.2 %copy-start.1 = (bf16[8,16,512]{2,1,0:T(8,128)(2,1)S(1)}, bf16[8,16,512]{2,1,0:T(8,128)(2,1)}, u32[]{:S(2)}) copy-start(bf16[8,16,512]{2,1,0:T(8,128)(2,1)} %k_ref.2) | copy-start | bytes 393220
  2.2 16.2 %copy-start.2 = (bf16[8,16,512]{2,1,0:T(8,128)(2,1)S(1)}, bf16[8,16,512]{2,1,0:T(8,128)(2,1)}, u32[]{:S(2)}) copy-start(bf16[8,16,512]{2,1,0:T(8,128)(2,1)} %v_ref.2) | copy-start | bytes 393220
  2.2 16.2 %copy-start.3 = (bf16[8,16,512]{2,1,0:T(8,128)(2,1)S(1)}, bf16[8,16,512]{2,1,0:T(8,128)(2,1)}, u32[]{:S(2)}) copy-start(bf16[8,16,512]{2,1,0:T(8,128)(2,1)} %o_ref.1) | copy-start | bytes 393220
  2.2 25.9 %all-to-all-start.1 = ((bf16[64,16,128]{2,1,0:T(8,128)(2,1)}), bf16[64,16,128]{2,1,0:T(8,128)(2,1)S(1)}, u32[]{:S(2)}, u32[]{:S(2)}) async-start(bf16[64,16,128]{2,1,0:T(8,128)(2,1)} %shard_map.120), calls=%async_computation.1 | async-start | bytes 524288 | tf_op jit(solution)/shard_map/all_to_all | solution.py:216
  19.4 32.0 %copy-start.4 = (f32[8]{0:T(128)S(1)}, f32[8]{0:T(128)}, u32[]{:S(2)}) copy-start(f32[8]{0:T(128)} %adv_ref.1) | copy-start | bytes 100
  19.4 32.0 %copy-start.5 = (s32[8]{0:T(128)S(1)}, s32[8]{0:T(128)}, u32[]{:S(2)}) copy-start(s32[8]{0:T(128)} %len_ref.1) | copy-start | bytes 100
  28.2 21.6 %all-to-all-start = ((bf16[32,64,128]{2,1,0:T(8,128)(2,1)}), bf16[32,64,128]{2,1,0:T(8,128)(2,1)S(1)}, u32[]{:S(2)}, u32[]{:S(2)}) async-start(bf16[32,64,128]{2,1,0:T(8,128)(2,1)} %shard_map.119), calls=%async_computation | async-start | bytes 1048576 | tf_op jit(solution)/shard_map/all_to_all | solution.py:216
  36.0 13.8 %collective-permute-start = (bf16[64,16,128]{2,1,0:T(8,128)(2,1)S(1)}, bf16[64,16,128]{2,1,0:T(8,128)(2,1)S(1)}, u32[]{:S(2)}, u32[]{:S(2)}) collective-permute-start(bf16[64,16,128]{2,1,0:T(8,128)(2,1)S(1)} %all-to-all-done.1.p00_ref), channel_id=1, source_target_pairs={{0,16},{16,0},{1,17},{17,1},{2,18},{18,2},{3,19},{19,3},{4,20},{20... | collective-permute-start | bytes 786440 | tf_op jit(solution)/shard_map/ppermute | solution.py:239
  37.6 12.2 %collective-permute-start.1 = (bf16[64,16,128]{2,1,0:T(8,128)(2,1)S(1)}, bf16[64,16,128]{2,1,0:T(8,128)(2,1)S(1)}, u32[]{:S(2)}, u32[]{:S(2)}) collective-permute-start(bf16[64,16,128]{2,1,0:T(8,128)(2,1)S(1)} %all-to-all-done.1.p00_ref), channel_id=1, source_target_pairs={{0,8},{8,0},{1,9},{9,1},{2,10},{10,2},{3,11},{11,3},{4,12},{12,4},... | collective-permute-start | bytes 786440 | tf_op jit(solution)/shard_map/ppermute | solution.py:240
  49.8 1.5 %collective-permute-start.2 = (bf16[64,16,128]{2,1,0:T(8,128)(2,1)S(1)}, bf16[64,16,128]{2,1,0:T(8,128)(2,1)S(1)}, u32[]{:S(2)}, u32[]{:S(2)}) collective-permute-start(bf16[64,16,128]{2,1,0:T(8,128)(2,1)S(1)} %collective-permute-done.p01_ref), channel_id=1, source_target_pairs={{0,8},{8,0},{1,9},{9,1},{2,10},{10,2},{3,11},{11,3},{4,12},{12,4},... | collective-permute-start | bytes 786440 | tf_op jit(solution)/shard_map/ppermute | solution.py:241
  57.6 7.4 %collective-permute-start.4 = (bf16[2,64,16,128]{3,2,1,0:T(8,128)(2,1)S(1)}, bf16[2,64,16,128]{3,2,1,0:T(8,128)(2,1)S(1)}, u32[]{:S(2)}, u32[]{:S(2)}) collective-permute-start(bf16[2,64,16,128]{3,2,1,0:T(8,128)(2,1)S(1)} %get-tuple-element.21), channel_id=1, source_target_pairs={{0,8},{8,0},{1,9},{9,1},{2,10},{10,2},{3,11},{11,3},{4,12},{12,4},... | collective-permute-start | bytes 1572872 | tf_op jit(solution)/shard_map/ppermute | solution.py:263
  57.7 17.4 %all-to-all-start.2 = ((bf16[16,2,48,128]{3,2,1,0:T(8,128)(2,1)}), bf16[16,2,48,128]{3,2,1,0:T(8,128)(2,1)S(1)}, u32[]{:S(2)}, u32[]{:S(2)}) async-start(bf16[16,2,48,128]{3,2,1,0:T(8,128)(2,1)} %bitcast), calls=%async_computation.2 | async-start | bytes 786432 | tf_op jit(solution)/shard_map/all_to_all | solution.py:216
  65.1 8.4 %collective-permute-start.5 = (bf16[64,16,128]{2,1,0:T(8,128)(2,1)S(1)}, bf16[64,16,128]{2,1,0:T(8,128)(2,1)S(1)}, u32[]{:S(2)}, u32[]{:S(2)}) collective-permute-start(bf16[64,16,128]{2,1,0:T(8,128)(2,1)S(1)} %get-tuple-element.23), channel_id=1, source_target_pairs={{0,16},{16,0},{1,17},{17,1},{2,18},{18,2},{3,19},{19,3},{4,20},{20... | collective-permute-start | bytes 786440 | tf_op jit(solution)/shard_map/ppermute | solution.py:265
  75.1 20.5 %all-to-all-start.3 = ((bf16[64,16,128]{2,1,0:T(8,128)(2,1)}), bf16[64,16,128]{2,1,0:T(8,128)(2,1)S(1)}, u32[]{:S(2)}, u32[]{:S(2)}) async-start(bf16[64,16,128]{2,1,0:T(8,128)(2,1)} %shard_map.125), calls=%async_computation.3 | async-start | bytes 524288 | tf_op jit(solution)/shard_map/all_to_all | solution.py:216
  85.6 7.9 %collective-permute-start.3 = (bf16[8,2,48,128]{3,2,1,0:T(8,128)(2,1)S(1)}, bf16[8,2,48,128]{3,2,1,0:T(8,128)(2,1)S(1)}, u32[]{:S(2)}, u32[]{:S(2)}) collective-permute-start(bf16[8,2,48,128]{3,2,1,0:T(8,128)(2,1)S(1)} %shard_map.122), channel_id=1, source_target_pairs={{0,16},{16,0},{1,17},{17,1},{2,18},{18,2},{3,19},{19,3},{4,20},{20... | collective-permute-start | bytes 589832 | tf_op jit(solution)/shard_map/ppermute | solution.py:272

commit v6 on v5

--- a/solution.py
+++ b/solution.py
@@ -16,7 +16,7 @@
 PROMPT = 2048
 BLOCK = 16
 CHUNK = 256
-FLIP_IN, FLIP_RESP, FLIP_BACK, FLIP_OUT = 32, 16, 8, 32
+FLIP_IN, FLIP_RESP, FLIP_BACK, FLIP_OUT = 36, 16, 8, 36
 LOG2E = 1.4426950408889634
 F32 = jnp.float32
 BF16 = jnp.bfloat16

time: 98.1 us -> 96.9 us (0.988)
  no operation moved by 1% of the time
where the time goes in v6:
time: 96.9 us; the launch traced here: 96 us
  starting transfers between devices  43.3 us (45%)
  waiting for transfers between devices  40.9 us (42%)
  Pallas kernels  11.1 us (11%)
    all_to_all x4, starting transfers between devices, exchange(): lax.all_to_all(x, AXES, 0, 0, axis_index_groups=groups_of(axes, flip), ti...  40.8 us
    ppermute x1, waiting for transfers between devices, body(): p01 = lax.ppermute(p00, 'x', swap)  12.2 us
    all_to_all x4, waiting for transfers between devices, exchange(): lax.all_to_all(x, AXES, 0, 0, axis_index_groups=groups_of(axes, flip), ti...  11.4 us
    ppermute x1, waiting for transfers between devices, body(): from_x = lax.ppermute(part, 'x', swap)  7.97 us
    ppermute x1, waiting for transfers between devices, body(): got = lax.ppermute(send, 'x', swap)  7.79 us
    pallas_call x1, Pallas kernels, body(): call(attn_kernel, [(8, 2, 2, 3 * BLOCK, HDIM), (2, 64, 16, HDIM), (2, 64,...  6.23 us
  transfers between devices with their start and end apart: 10, of which 7 were waited for; matrix products, arithmetic and copies ran while one was open for 0% of the time, Pallas kernels for 3%

profile of v6, /device:TPU:8, one launch (start us, length us, event | category | flops | bytes accessed | tf_op | source)
XLA Modules:
  0.0 96.0 jit_solution(11788209364864889283)
XLA Ops:
  0.6 1.6 %shard_map.120 = bf16[64,16,128]{2,1,0:T(8,128)(2,1)} custom-call(bf16[8,4096]{1,0:T(8,128)(2,1)} %k_ref.3, bf16[8,4096]{1,0:T(8,128)(2,1)} %v_ref.3), custom_call_target="tpu_custom_call" | custom-call | bytes 1048576 | tf_op jit(solution)/shard_map/pallas_call | solution.py:237
  2.2 0.0 copy-start
  2.2 0.0 copy-start.1
  2.2 0.0 copy-start.2
  2.2 0.0 copy-start.3
  2.2 15.4 %all-to-all-start.1 = ((bf16[64,16,128]{2,1,0:T(8,128)(2,1)}), bf16[64,16,128]{2,1,0:T(8,128)(2,1)S(1)}, u32[]{:S(2)}, u32[]{:S(2)}) async-start(bf16[64,16,128]{2,1,0:T(8,128)(2,1)} %shard_map.120), calls=%async_computation.1 | async-start | bytes 524288 | tf_op jit(solution)/shard_map/all_to_all | solution.py:216
  17.7 0.0 copy-done
  17.7 0.0 copy-done.1
  17.7 0.0 copy-done.2
  17.7 0.0 copy-done.3
  17.7 0.9 shard_map.119
  18.6 0.0 copy-start.4
  18.6 0.0 copy-start.5
  18.6 9.1 %all-to-all-done.1.p00_ref = bf16[64,16,128]{2,1,0:T(8,128)(2,1)S(1)} async-done(((bf16[64,16,128]{2,1,0:T(8,128)(2,1)}), bf16[64,16,128]{2,1,0:T(8,128)(2,1)S(1)}, u32[]{:S(2)}, u32[]{:S(2)}) %all-to-all-start.1) | async-done | bytes 262176 | tf_op jit(solution)/shard_map/all_to_all | solution.py:216
  27.7 7.4 %all-to-all-start = ((bf16[32,64,128]{2,1,0:T(8,128)(2,1)}), bf16[32,64,128]{2,1,0:T(8,128)(2,1)S(1)}, u32[]{:S(2)}, u32[]{:S(2)}) async-start(bf16[32,64,128]{2,1,0:T(8,128)(2,1)} %shard_map.119), calls=%async_computation | async-start | bytes 1048576 | tf_op jit(solution)/shard_map/all_to_all | solution.py:216
  35.1 1.6 %collective-permute-start = (bf16[64,16,128]{2,1,0:T(8,128)(2,1)S(1)}, bf16[64,16,128]{2,1,0:T(8,128)(2,1)S(1)}, u32[]{:S(2)}, u32[]{:S(2)}) collective-permute-start(bf16[64,16,128]{2,1,0:T(8,128)(2,1)S(1)} %all-to-all-done.1.p00_ref), channel_id=1, source_target_pairs={{0,16},{16,0},{1,17},{17,1},{2,18},{18,2},{3,19},{19,3},{4,20},{20... | collective-permute-start | bytes 786440 | tf_op jit(solution)/shard_map/ppermute | solution.py:239
  36.7 0.0 collective-permute-start.1
  36.7 12.2 %collective-permute-done.p01_ref = bf16[64,16,128]{2,1,0:T(8,128)(2,1)S(1)} collective-permute-done((bf16[64,16,128]{2,1,0:T(8,128)(2,1)S(1)}, bf16[64,16,128]{2,1,0:T(8,128)(2,1)S(1)}, u32[]{:S(2)}, u32[]{:S(2)}) %collective-permute-start) | collective-permute-done | bytes 262176 | tf_op jit(solution)/shard_map/ppermute | solution.py:239
  48.9 0.0 collective-permute-start.2
  48.9 0.0 collective-permute-done.1.p10_ref
  48.9 0.0 all-to-all-done.resp_ref
  48.9 1.5 %collective-permute-done.2.p11_ref = bf16[64,16,128]{2,1,0:T(8,128)(2,1)S(1)} collective-permute-done((bf16[64,16,128]{2,1,0:T(8,128)(2,1)S(1)}, bf16[64,16,128]{2,1,0:T(8,128)(2,1)S(1)}, u32[]{:S(2)}, u32[]{:S(2)}) %collective-permute-start.2) | collective-permute-done | bytes 262176 | tf_op jit(solution)/shard_map/ppermute | solution.py:241
  50.5 0.0 copy-done.4
  50.5 0.0 copy-done.5
  50.5 6.2 %shard_map.121 = (bf16[8,2,2,48,128]{4,3,2,1,0:T(8,128)(2,1)}, bf16[2,64,16,128]{3,2,1,0:T(8,128)(2,1)S(1)}, bf16[2,64,16,128]{3,2,1,0:T(8,128)(2,1)S(1)}) custom-call(f32[8]{0:T(128)S(1)} %copy-done.4, s32[8]{0:T(128)S(1)} %copy-done.5, bf16[32,64,128]{2,1,0:T(8,128)(2,1)S(1)} %all-to-all-done.resp_ref, bf16[64,16,128]{2,1,0:T(8,128)(2,1)S(1)} %all-to-all-done.1.p00_ref, ...), custom_call_target="tpu_custom_call" | custom-call | flops 1677721600 | bytes 3145728 | tf_op jit(solution)/shard_map/pallas_call | solution.py:248
  56.7 0.1 collective-permute-start.4
  56.8 7.2 %all-to-all-start.2 = ((bf16[16,2,48,128]{3,2,1,0:T(8,128)(2,1)}), bf16[16,2,48,128]{3,2,1,0:T(8,128)(2,1)S(1)}, u32[]{:S(2)}, u32[]{:S(2)}) async-start(bf16[16,2,48,128]{3,2,1,0:T(8,128)(2,1)} %bitcast), calls=%async_computation.2 | async-start | bytes 786432 | tf_op jit(solution)/shard_map/all_to_all | solution.py:216
  64.1 0.0 collective-permute-done.4.got_ref
  64.1 0.1 shard_map.124
  64.2 0.7 collective-permute-start.5
  64.9 7.8 %collective-permute-done.5.got_ref = bf16[64,16,128]{2,1,0:T(8,128)(2,1)S(1)} collective-permute-done((bf16[64,16,128]{2,1,0:T(8,128)(2,1)S(1)}, bf16[64,16,128]{2,1,0:T(8,128)(2,1)S(1)}, u32[]{:S(2)}, u32[]{:S(2)}) %collective-permute-start.5) | collective-permute-done | bytes 262176 | tf_op jit(solution)/shard_map/ppermute | solution.py:265
  72.7 0.8 shard_map.125
  73.4 0.8 all-to-all-done.2
  74.3 10.7 %all-to-all-start.3 = ((bf16[64,16,128]{2,1,0:T(8,128)(2,1)}), bf16[64,16,128]{2,1,0:T(8,128)(2,1)S(1)}, u32[]{:S(2)}, u32[]{:S(2)}) async-start(bf16[64,16,128]{2,1,0:T(8,128)(2,1)} %shard_map.125), calls=%async_computation.3 | async-start | bytes 524288 | tf_op jit(solution)/shard_map/all_to_all | solution.py:216
  85.0 0.1 collective-permute-start.3
  85.1 8.0 %collective-permute-done.3.from_x_ref = bf16[8,2,48,128]{3,2,1,0:T(8,128)(2,1)S(1)} collective-permute-done((bf16[8,2,48,128]{3,2,1,0:T(8,128)(2,1)S(1)}, bf16[8,2,48,128]{3,2,1,0:T(8,128)(2,1)S(1)}, u32[]{:S(2)}, u32[]{:S(2)}) %collective-permute-start.3) | collective-permute-done | bytes 196640 | tf_op jit(solution)/shard_map/ppermute | solution.py:272
  93.1 0.8 shard_map.123
  93.9 1.4 %all-to-all-done.3.got_ref = bf16[64,16,128]{2,1,0:T(8,128)(2,1)S(1)} async-done(((bf16[64,16,128]{2,1,0:T(8,128)(2,1)}), bf16[64,16,128]{2,1,0:T(8,128)(2,1)S(1)}, u32[]{:S(2)}, u32[]{:S(2)}) %all-to-all-start.3) | async-done | bytes 262176 | tf_op jit(solution)/shard_map/all_to_all | solution.py:216
  95.4 0.7 shard_map.126
  (1 shorter events, 0.0 us)
Async XLA Ops:
  2.2 15.4 %copy-start = (bf16[8,16,512]{2,1,0:T(8,128)(2,1)S(1)}, bf16[8,16,512]{2,1,0:T(8,128)(2,1)}, u32[]{:S(2)}) copy-start(bf16[8,16,512]{2,1,0:T(8,128)(2,1)} %q_ref.1) | copy-start | bytes 393220
  2.2 15.5 %copy-start.1 = (bf16[8,16,512]{2,1,0:T(8,128)(2,1)S(1)}, bf16[8,16,512]{2,1,0:T(8,128)(2,1)}, u32[]{:S(2)}) copy-start(bf16[8,16,512]{2,1,0:T(8,128)(2,1)} %k_ref.2) | copy-start | bytes 393220
  2.2 15.5 %copy-start.2 = (bf16[8,16,512]{2,1,0:T(8,128)(2,1)S(1)}, bf16[8,16,512]{2,1,0:T(8,128)(2,1)}, u32[]{:S(2)}) copy-start(bf16[8,16,512]{2,1,0:T(8,128)(2,1)} %v_ref.2) | copy-start | bytes 393220
  2.2 15.5 %copy-start.3 = (bf16[8,16,512]{2,1,0:T(8,128)(2,1)S(1)}, bf16[8,16,512]{2,1,0:T(8,128)(2,1)}, u32[]{:S(2)}) copy-start(bf16[8,16,512]{2,1,0:T(8,128)(2,1)} %o_ref.1) | copy-start | bytes 393220
  2.2 25.5 %all-to-all-start.1 = ((bf16[64,16,128]{2,1,0:T(8,128)(2,1)}), bf16[64,16,128]{2,1,0:T(8,128)(2,1)S(1)}, u32[]{:S(2)}, u32[]{:S(2)}) async-start(bf16[64,16,128]{2,1,0:T(8,128)(2,1)} %shard_map.120), calls=%async_computation.1 | async-start | bytes 524288 | tf_op jit(solution)/shard_map/all_to_all | solution.py:216
  18.6 31.9 %copy-start.4 = (f32[8]{0:T(128)S(1)}, f32[8]{0:T(128)}, u32[]{:S(2)}) copy-start(f32[8]{0:T(128)} %adv_ref.1) | copy-start | bytes 100
  18.6 31.9 %copy-start.5 = (s32[8]{0:T(128)S(1)}, s32[8]{0:T(128)}, u32[]{:S(2)}) copy-start(s32[8]{0:T(128)} %len_ref.1) | copy-start | bytes 100
  27.7 21.2 %all-to-all-start = ((bf16[32,64,128]{2,1,0:T(8,128)(2,1)}), bf16[32,64,128]{2,1,0:T(8,128)(2,1)S(1)}, u32[]{:S(2)}, u32[]{:S(2)}) async-start(bf16[32,64,128]{2,1,0:T(8,128)(2,1)} %shard_map.119), calls=%async_computation | async-start | bytes 1048576 | tf_op jit(solution)/shard_map/all_to_all | solution.py:216
  35.1 13.8 %collective-permute-start = (bf16[64,16,128]{2,1,0:T(8,128)(2,1)S(1)}, bf16[64,16,128]{2,1,0:T(8,128)(2,1)S(1)}, u32[]{:S(2)}, u32[]{:S(2)}) collective-permute-start(bf16[64,16,128]{2,1,0:T(8,128)(2,1)S(1)} %all-to-all-done.1.p00_ref), channel_id=1, source_target_pairs={{0,16},{16,0},{1,17},{17,1},{2,18},{18,2},{3,19},{19,3},{4,20},{20... | collective-permute-start | bytes 786440 | tf_op jit(solution)/shard_map/ppermute | solution.py:239
  36.7 12.2 %collective-permute-start.1 = (bf16[64,16,128]{2,1,0:T(8,128)(2,1)S(1)}, bf16[64,16,128]{2,1,0:T(8,128)(2,1)S(1)}, u32[]{:S(2)}, u32[]{:S(2)}) collective-permute-start(bf16[64,16,128]{2,1,0:T(8,128)(2,1)S(1)} %all-to-all-done.1.p00_ref), channel_id=1, source_target_pairs={{0,8},{8,0},{1,9},{9,1},{2,10},{10,2},{3,11},{11,3},{4,12},{12,4},... | collective-permute-start | bytes 786440 | tf_op jit(solution)/shard_map/ppermute | solution.py:240
  48.9 1.5 %collective-permute-start.2 = (bf16[64,16,128]{2,1,0:T(8,128)(2,1)S(1)}, bf16[64,16,128]{2,1,0:T(8,128)(2,1)S(1)}, u32[]{:S(2)}, u32[]{:S(2)}) collective-permute-start(bf16[64,16,128]{2,1,0:T(8,128)(2,1)S(1)} %collective-permute-done.p01_ref), channel_id=1, source_target_pairs={{0,8},{8,0},{1,9},{9,1},{2,10},{10,2},{3,11},{11,3},{4,12},{12,4},... | collective-permute-start | bytes 786440 | tf_op jit(solution)/shard_map/ppermute | solution.py:241
  56.7 7.4 %collective-permute-start.4 = (bf16[2,64,16,128]{3,2,1,0:T(8,128)(2,1)S(1)}, bf16[2,64,16,128]{3,2,1,0:T(8,128)(2,1)S(1)}, u32[]{:S(2)}, u32[]{:S(2)}) collective-permute-start(bf16[2,64,16,128]{3,2,1,0:T(8,128)(2,1)S(1)} %get-tuple-element.21), channel_id=1, source_target_pairs={{0,8},{8,0},{1,9},{9,1},{2,10},{10,2},{3,11},{11,3},{4,12},{12,4},... | collective-permute-start | bytes 1572872 | tf_op jit(solution)/shard_map/ppermute | solution.py:263
  56.8 17.4 %all-to-all-start.2 = ((bf16[16,2,48,128]{3,2,1,0:T(8,128)(2,1)}), bf16[16,2,48,128]{3,2,1,0:T(8,128)(2,1)S(1)}, u32[]{:S(2)}, u32[]{:S(2)}) async-start(bf16[16,2,48,128]{3,2,1,0:T(8,128)(2,1)} %bitcast), calls=%async_computation.2 | async-start | bytes 786432 | tf_op jit(solution)/shard_map/all_to_all | solution.py:216
  64.2 8.4 %collective-permute-start.5 = (bf16[64,16,128]{2,1,0:T(8,128)(2,1)S(1)}, bf16[64,16,128]{2,1,0:T(8,128)(2,1)S(1)}, u32[]{:S(2)}, u32[]{:S(2)}) collective-permute-start(bf16[64,16,128]{2,1,0:T(8,128)(2,1)S(1)} %get-tuple-element.23), channel_id=1, source_target_pairs={{0,16},{16,0},{1,17},{17,1},{2,18},{18,2},{3,19},{19,3},{4,20},{20... | collective-permute-start | bytes 786440 | tf_op jit(solution)/shard_map/ppermute | solution.py:265
  74.3 21.1 %all-to-all-start.3 = ((bf16[64,16,128]{2,1,0:T(8,128)(2,1)}), bf16[64,16,128]{2,1,0:T(8,128)(2,1)S(1)}, u32[]{:S(2)}, u32[]{:S(2)}) async-start(bf16[64,16,128]{2,1,0:T(8,128)(2,1)} %shard_map.125), calls=%async_computation.3 | async-start | bytes 524288 | tf_op jit(solution)/shard_map/all_to_all | solution.py:216
  85.0 8.1 %collective-permute-start.3 = (bf16[8,2,48,128]{3,2,1,0:T(8,128)(2,1)S(1)}, bf16[8,2,48,128]{3,2,1,0:T(8,128)(2,1)S(1)}, u32[]{:S(2)}, u32[]{:S(2)}) collective-permute-start(bf16[8,2,48,128]{3,2,1,0:T(8,128)(2,1)S(1)} %shard_map.122), channel_id=1, source_target_pairs={{0,16},{16,0},{1,17},{17,1},{2,18},{18,2},{3,19},{19,3},{4,20},{20... | collective-permute-start | bytes 589832 | tf_op jit(solution)/shard_map/ppermute | solution.py:272

commit v7 on v6

--- a/solution.py
+++ b/solution.py
@@ -16,7 +16,7 @@
 PROMPT = 2048
 BLOCK = 16
 CHUNK = 256
-FLIP_IN, FLIP_RESP, FLIP_BACK, FLIP_OUT = 36, 16, 8, 36
+FLIP_IN, FLIP_RESP, FLIP_BACK, FLIP_OUT = 37, 16, 8, 36
 LOG2E = 1.4426950408889634
 F32 = jnp.float32
 BF16 = jnp.bfloat16
@@ -157,8 +157,8 @@
                 [dk.reshape(CHUNK // 8, 8, HDIM), dv.reshape(CHUNK // 8, 8, HDIM)], axis=1
             ).astype(BF16)
             out = send_ref if c % 2 else keep_ref
-            half = c // 4
-            out[(c // 2) % 2, half * 32 : (half + 1) * 32] = both
+            for i in range(32):
+                out[(c // 2) % 2, (c // 4 * 32 + i) ^ FLIP_IN ^ FLIP_OUT] = both[i]
         else:
             store_blocks((c - n_prompt) * 4, 1, dk)
             store_blocks((c - n_prompt) * 4, 2, dv)

time: 96.9 us -> 96.6 us (level)
  waiting for transfers between devices: 40.9 us -> 38.3 us
  starting transfers between devices: 43.3 us -> 45.6 us
    all_to_all x4, waiting for transfers between devices: 11.4 us -> 8.94 us  [exchange(): lax.all_to_all(x, AXES, 0, 0, axis_index_groups=groups_of(axes, flip), ti...]
    all_to_all x4, starting transfers between devices: 40.8 us -> 43.1 us  [exchange(): lax.all_to_all(x, AXES, 0, 0, axis_index_groups=groups_of(axes, flip), ti...]
where the time goes in v7:
time: 96.6 us; the launch traced here: 95.8 us
  starting transfers between devices  45.6 us (47%)
  waiting for transfers between devices  38.3 us (40%)
  Pallas kernels  11.1 us (11%)
    all_to_all x4, starting transfers between devices, exchange(): lax.all_to_all(x, AXES, 0, 0, axis_index_groups=groups_of(axes, flip), ti...  43.1 us
    ppermute x1, waiting for transfers between devices, body(): p01 = lax.ppermute(p00, 'x', swap)  12.2 us
    all_to_all x4, waiting for transfers between devices, exchange(): lax.all_to_all(x, AXES, 0, 0, axis_index_groups=groups_of(axes, flip), ti...  8.94 us
    ppermute x1, waiting for transfers between devices, body(): from_x = lax.ppermute(part, 'x', swap)  7.84 us
    ppermute x1, waiting for transfers between devices, body(): got = lax.ppermute(send, 'x', swap)  7.79 us
    pallas_call x1, Pallas kernels, body(): call(attn_kernel, [(8, 2, 2, 3 * BLOCK, HDIM), (2, 64, 16, HDIM), (2, 64,...  6.21 us
  transfers between devices with their start and end apart: 10, of which 7 were waited for; matrix products, arithmetic and copies ran while one was open for 0% of the time, Pallas kernels for 3%

profile of v7, /device:TPU:8, one launch (start us, length us, event | category | flops | bytes accessed | tf_op | source)
XLA Modules:
  0.0 95.8 jit_solution(728104657806216581)
XLA Ops:
  0.6 1.6 %shard_map.120 = bf16[64,16,128]{2,1,0:T(8,128)(2,1)} custom-call(bf16[8,4096]{1,0:T(8,128)(2,1)} %k_ref.3, bf16[8,4096]{1,0:T(8,128)(2,1)} %v_ref.3), custom_call_target="tpu_custom_call" | custom-call | bytes 1048576 | tf_op jit(solution)/shard_map/pallas_call | solution.py:237
  2.2 0.0 copy-start
  2.2 0.0 copy-start.1
  2.2 0.0 copy-start.2
  2.2 0.0 copy-start.3
  2.2 15.4 %all-to-all-start.1 = ((bf16[64,16,128]{2,1,0:T(8,128)(2,1)}), bf16[64,16,128]{2,1,0:T(8,128)(2,1)S(1)}, u32[]{:S(2)}, u32[]{:S(2)}) async-start(bf16[64,16,128]{2,1,0:T(8,128)(2,1)} %shard_map.120), calls=%async_computation.1 | async-start | bytes 524288 | tf_op jit(solution)/shard_map/all_to_all | solution.py:216
  17.7 0.0 copy-done
  17.7 0.0 copy-done.1
  17.7 0.0 copy-done.2
  17.7 0.0 copy-done.3
  17.7 0.9 shard_map.119
  18.6 0.0 copy-start.4
  18.6 0.0 copy-start.5
  18.6 6.5 %all-to-all-done.1.p00_ref = bf16[64,16,128]{2,1,0:T(8,128)(2,1)S(1)} async-done(((bf16[64,16,128]{2,1,0:T(8,128)(2,1)}), bf16[64,16,128]{2,1,0:T(8,128)(2,1)S(1)}, u32[]{:S(2)}, u32[]{:S(2)}) %all-to-all-start.1) | async-done | bytes 262176 | tf_op jit(solution)/shard_map/all_to_all | solution.py:216
  25.2 8.3 %all-to-all-start = ((bf16[32,64,128]{2,1,0:T(8,128)(2,1)}), bf16[32,64,128]{2,1,0:T(8,128)(2,1)S(1)}, u32[]{:S(2)}, u32[]{:S(2)}) async-start(bf16[32,64,128]{2,1,0:T(8,128)(2,1)} %shard_map.119), calls=%async_computation | async-start | bytes 1048576 | tf_op jit(solution)/shard_map/all_to_all | solution.py:216
  33.5 1.6 %collective-permute-start = (bf16[64,16,128]{2,1,0:T(8,128)(2,1)S(1)}, bf16[64,16,128]{2,1,0:T(8,128)(2,1)S(1)}, u32[]{:S(2)}, u32[]{:S(2)}) collective-permute-start(bf16[64,16,128]{2,1,0:T(8,128)(2,1)S(1)} %all-to-all-done.1.p00_ref), channel_id=1, source_target_pairs={{0,16},{16,0},{1,17},{17,1},{2,18},{18,2},{3,19},{19,3},{4,20},{20... | collective-permute-start | bytes 786440 | tf_op jit(solution)/shard_map/ppermute | solution.py:239
  35.1 0.0 collective-permute-start.1
  35.1 12.2 %collective-permute-done.p01_ref = bf16[64,16,128]{2,1,0:T(8,128)(2,1)S(1)} collective-permute-done((bf16[64,16,128]{2,1,0:T(8,128)(2,1)S(1)}, bf16[64,16,128]{2,1,0:T(8,128)(2,1)S(1)}, u32[]{:S(2)}, u32[]{:S(2)}) %collective-permute-start) | collective-permute-done | bytes 262176 | tf_op jit(solution)/shard_map/ppermute | solution.py:239
  47.3 0.0 collective-permute-start.2
  47.3 0.0 collective-permute-done.1.p10_ref
  47.3 0.0 all-to-all-done.resp_ref
  47.3 1.5 %collective-permute-done.2.p11_ref = bf16[64,16,128]{2,1,0:T(8,128)(2,1)S(1)} collective-permute-done((bf16[64,16,128]{2,1,0:T(8,128)(2,1)S(1)}, bf16[64,16,128]{2,1,0:T(8,128)(2,1)S(1)}, u32[]{:S(2)}, u32[]{:S(2)}) %collective-permute-start.2) | collective-permute-done | bytes 262176 | tf_op jit(solution)/shard_map/ppermute | solution.py:241
  48.8 0.0 copy-done.4
  48.8 0.0 copy-done.5
  48.8 6.2 %shard_map.121 = (bf16[8,2,2,48,128]{4,3,2,1,0:T(8,128)(2,1)}, bf16[2,64,16,128]{3,2,1,0:T(8,128)(2,1)S(1)}, bf16[2,64,16,128]{3,2,1,0:T(8,128)(2,1)S(1)}) custom-call(f32[8]{0:T(128)S(1)} %copy-done.4, s32[8]{0:T(128)S(1)} %copy-done.5, bf16[32,64,128]{2,1,0:T(8,128)(2,1)S(1)} %all-to-all-done.resp_ref, bf16[64,16,128]{2,1,0:T(8,128)(2,1)S(1)} %all-to-all-done.1.p00_ref, ...), custom_call_target="tpu_custom_call" | custom-call | flops 1677721600 | bytes 3145728 | tf_op jit(solution)/shard_map/pallas_call | solution.py:248
  55.0 0.1 collective-permute-start.4
  55.2 7.2 %all-to-all-start.2 = ((bf16[16,2,48,128]{3,2,1,0:T(8,128)(2,1)}), bf16[16,2,48,128]{3,2,1,0:T(8,128)(2,1)S(1)}, u32[]{:S(2)}, u32[]{:S(2)}) async-start(bf16[16,2,48,128]{3,2,1,0:T(8,128)(2,1)} %bitcast), calls=%async_computation.2 | async-start | bytes 786432 | tf_op jit(solution)/shard_map/all_to_all | solution.py:216
  62.4 0.0 collective-permute-done.4.got_ref
  62.4 0.1 shard_map.124
  62.6 0.7 collective-permute-start.5
  63.2 7.8 %collective-permute-done.5.got_ref = bf16[64,16,128]{2,1,0:T(8,128)(2,1)S(1)} collective-permute-done((bf16[64,16,128]{2,1,0:T(8,128)(2,1)S(1)}, bf16[64,16,128]{2,1,0:T(8,128)(2,1)S(1)}, u32[]{:S(2)}, u32[]{:S(2)}) %collective-permute-start.5) | collective-permute-done | bytes 262176 | tf_op jit(solution)/shard_map/ppermute | solution.py:265
  71.0 0.8 shard_map.125
  71.8 0.8 all-to-all-done.2
  72.6 12.1 %all-to-all-start.3 = ((bf16[64,16,128]{2,1,0:T(8,128)(2,1)}), bf16[64,16,128]{2,1,0:T(8,128)(2,1)S(1)}, u32[]{:S(2)}, u32[]{:S(2)}) async-start(bf16[64,16,128]{2,1,0:T(8,128)(2,1)} %shard_map.125), calls=%async_computation.3 | async-start | bytes 524288 | tf_op jit(solution)/shard_map/all_to_all | solution.py:216
  84.8 0.1 collective-permute-start.3
  84.9 7.8 %collective-permute-done.3.from_x_ref = bf16[8,2,48,128]{3,2,1,0:T(8,128)(2,1)S(1)} collective-permute-done((bf16[8,2,48,128]{3,2,1,0:T(8,128)(2,1)S(1)}, bf16[8,2,48,128]{3,2,1,0:T(8,128)(2,1)S(1)}, u32[]{:S(2)}, u32[]{:S(2)}) %collective-permute-start.3) | collective-permute-done | bytes 196640 | tf_op jit(solution)/shard_map/ppermute | solution.py:272
  92.7 0.8 shard_map.123
  93.5 1.6 %all-to-all-done.3.got_ref = bf16[64,16,128]{2,1,0:T(8,128)(2,1)S(1)} async-done(((bf16[64,16,128]{2,1,0:T(8,128)(2,1)}), bf16[64,16,128]{2,1,0:T(8,128)(2,1)S(1)}, u32[]{:S(2)}, u32[]{:S(2)}) %all-to-all-start.3) | async-done | bytes 262176 | tf_op jit(solution)/shard_map/all_to_all | solution.py:216
  95.1 0.7 shard_map.126
  (1 shorter events, 0.0 us)
Async XLA Ops:
  2.2 15.5 %copy-start = (bf16[8,16,512]{2,1,0:T(8,128)(2,1)S(1)}, bf16[8,16,512]{2,1,0:T(8,128)(2,1)}, u32[]{:S(2)}) copy-start(bf16[8,16,512]{2,1,0:T(8,128)(2,1)} %q_ref.1) | copy-start | bytes 393220
  2.2 15.5 %copy-start.1 = (bf16[8,16,512]{2,1,0:T(8,128)(2,1)S(1)}, bf16[8,16,512]{2,1,0:T(8,128)(2,1)}, u32[]{:S(2)}) copy-start(bf16[8,16,512]{2,1,0:T(8,128)(2,1)} %k_ref.2) | copy-start | bytes 393220
  2.2 15.5 %copy-start.2 = (bf16[8,16,512]{2,1,0:T(8,128)(2,1)S(1)}, bf16[8,16,512]{2,1,0:T(8,128)(2,1)}, u32[]{:S(2)}) copy-start(bf16[8,16,512]{2,1,0:T(8,128)(2,1)} %v_ref.2) | copy-start | bytes 393220
  2.2 15.5 %copy-start.3 = (bf16[8,16,512]{2,1,0:T(8,128)(2,1)S(1)}, bf16[8,16,512]{2,1,0:T(8,128)(2,1)}, u32[]{:S(2)}) copy-start(bf16[8,16,512]{2,1,0:T(8,128)(2,1)} %o_ref.1) | copy-start | bytes 393220
  2.2 22.9 %all-to-all-start.1 = ((bf16[64,16,128]{2,1,0:T(8,128)(2,1)}), bf16[64,16,128]{2,1,0:T(8,128)(2,1)S(1)}, u32[]{:S(2)}, u32[]{:S(2)}) async-start(bf16[64,16,128]{2,1,0:T(8,128)(2,1)} %shard_map.120), calls=%async_computation.1 | async-start | bytes 524288 | tf_op jit(solution)/shard_map/all_to_all | solution.py:216
  18.6 30.2 %copy-start.4 = (f32[8]{0:T(128)S(1)}, f32[8]{0:T(128)}, u32[]{:S(2)}) copy-start(f32[8]{0:T(128)} %adv_ref.1) | copy-start | bytes 100
  18.6 30.2 %copy-start.5 = (s32[8]{0:T(128)S(1)}, s32[8]{0:T(128)}, u32[]{:S(2)}) copy-start(s32[8]{0:T(128)} %len_ref.1) | copy-start | bytes 100
  25.2 22.1 %all-to-all-start = ((bf16[32,64,128]{2,1,0:T(8,128)(2,1)}), bf16[32,64,128]{2,1,0:T(8,128)(2,1)S(1)}, u32[]{:S(2)}, u32[]{:S(2)}) async-start(bf16[32,64,128]{2,1,0:T(8,128)(2,1)} %shard_map.119), calls=%async_computation | async-start | bytes 1048576 | tf_op jit(solution)/shard_map/all_to_all | solution.py:216
  33.5 13.8 %collective-permute-start = (bf16[64,16,128]{2,1,0:T(8,128)(2,1)S(1)}, bf16[64,16,128]{2,1,0:T(8,128)(2,1)S(1)}, u32[]{:S(2)}, u32[]{:S(2)}) collective-permute-start(bf16[64,16,128]{2,1,0:T(8,128)(2,1)S(1)} %all-to-all-done.1.p00_ref), channel_id=1, source_target_pairs={{0,16},{16,0},{1,17},{17,1},{2,18},{18,2},{3,19},{19,3},{4,20},{20... | collective-permute-start | bytes 786440 | tf_op jit(solution)/shard_map/ppermute | solution.py:239
  35.1 12.2 %collective-permute-start.1 = (bf16[64,16,128]{2,1,0:T(8,128)(2,1)S(1)}, bf16[64,16,128]{2,1,0:T(8,128)(2,1)S(1)}, u32[]{:S(2)}, u32[]{:S(2)}) collective-permute-start(bf16[64,16,128]{2,1,0:T(8,128)(2,1)S(1)} %all-to-all-done.1.p00_ref), channel_id=1, source_target_pairs={{0,8},{8,0},{1,9},{9,1},{2,10},{10,2},{3,11},{11,3},{4,12},{12,4},... | collective-permute-start | bytes 786440 | tf_op jit(solution)/shard_map/ppermute | solution.py:240
  47.3 1.5 %collective-permute-start.2 = (bf16[64,16,128]{2,1,0:T(8,128)(2,1)S(1)}, bf16[64,16,128]{2,1,0:T(8,128)(2,1)S(1)}, u32[]{:S(2)}, u32[]{:S(2)}) collective-permute-start(bf16[64,16,128]{2,1,0:T(8,128)(2,1)S(1)} %collective-permute-done.p01_ref), channel_id=1, source_target_pairs={{0,8},{8,0},{1,9},{9,1},{2,10},{10,2},{3,11},{11,3},{4,12},{12,4},... | collective-permute-start | bytes 786440 | tf_op jit(solution)/shard_map/ppermute | solution.py:241
  55.0 7.4 %collective-permute-start.4 = (bf16[2,64,16,128]{3,2,1,0:T(8,128)(2,1)S(1)}, bf16[2,64,16,128]{3,2,1,0:T(8,128)(2,1)S(1)}, u32[]{:S(2)}, u32[]{:S(2)}) collective-permute-start(bf16[2,64,16,128]{3,2,1,0:T(8,128)(2,1)S(1)} %get-tuple-element.21), channel_id=1, source_target_pairs={{0,8},{8,0},{1,9},{9,1},{2,10},{10,2},{3,11},{11,3},{4,12},{12,4},... | collective-permute-start | bytes 1572872 | tf_op jit(solution)/shard_map/ppermute | solution.py:263
  55.2 17.4 %all-to-all-start.2 = ((bf16[16,2,48,128]{3,2,1,0:T(8,128)(2,1)}), bf16[16,2,48,128]{3,2,1,0:T(8,128)(2,1)S(1)}, u32[]{:S(2)}, u32[]{:S(2)}) async-start(bf16[16,2,48,128]{3,2,1,0:T(8,128)(2,1)} %bitcast), calls=%async_computation.2 | async-start | bytes 786432 | tf_op jit(solution)/shard_map/all_to_all | solution.py:216
  62.6 8.4 %collective-permute-start.5 = (bf16[64,16,128]{2,1,0:T(8,128)(2,1)S(1)}, bf16[64,16,128]{2,1,0:T(8,128)(2,1)S(1)}, u32[]{:S(2)}, u32[]{:S(2)}) collective-permute-start(bf16[64,16,128]{2,1,0:T(8,128)(2,1)S(1)} %get-tuple-element.23), channel_id=1, source_target_pairs={{0,16},{16,0},{1,17},{17,1},{2,18},{18,2},{3,19},{19,3},{4,20},{20... | collective-permute-start | bytes 786440 | tf_op jit(solution)/shard_map/ppermute | solution.py:265
  72.6 22.5 %all-to-all-start.3 = ((bf16[64,16,128]{2,1,0:T(8,128)(2,1)}), bf16[64,16,128]{2,1,0:T(8,128)(2,1)S(1)}, u32[]{:S(2)}, u32[]{:S(2)}) async-start(bf16[64,16,128]{2,1,0:T(8,128)(2,1)} %shard_map.125), calls=%async_computation.3 | async-start | bytes 524288 | tf_op jit(solution)/shard_map/all_to_all | solution.py:216
  84.8 7.9 %collective-permute-start.3 = (bf16[8,2,48,128]{3,2,1,0:T(8,128)(2,1)S(1)}, bf16[8,2,48,128]{3,2,1,0:T(8,128)(2,1)S(1)}, u32[]{:S(2)}, u32[]{:S(2)}) collective-permute-start(bf16[8,2,48,128]{3,2,1,0:T(8,128)(2,1)S(1)} %shard_map.122), channel_id=1, source_target_pairs={{0,16},{16,0},{1,17},{17,1},{2,18},{18,2},{3,19},{19,3},{4,20},{20... | collective-permute-start | bytes 589832 | tf_op jit(solution)/shard_map/ppermute | solution.py:272

commit v8 on v7

--- a/solution.py
+++ b/solution.py
@@ -16,7 +16,7 @@
 PROMPT = 2048
 BLOCK = 16
 CHUNK = 256
-FLIP_IN, FLIP_RESP, FLIP_BACK, FLIP_OUT = 37, 16, 8, 36
+FLIP_IN, FLIP_RESP, FLIP_BACK, FLIP_OUT = 37, 16, 8, 32
 LOG2E = 1.4426950408889634
 F32 = jnp.float32
 BF16 = jnp.bfloat16

time: 96.6 us -> 98.4 us (1.019)
  starting transfers between devices: 45.6 us -> 46.8 us
    all_to_all x4, starting transfers between devices: 43.1 us -> 44.3 us  [exchange(): lax.all_to_all(x, AXES, 0, 0, axis_index_groups=groups_of(axes, flip), ti...]
where the time goes in v8:
time: 98.4 us; the launch traced here: 96.6 us
  starting transfers between devices  46.8 us (48%)
  waiting for transfers between devices  38 us (39%)
  Pallas kernels  11.1 us (11%)
    all_to_all x4, starting transfers between devices, exchange(): lax.all_to_all(x, AXES, 0, 0, axis_index_groups=groups_of(axes, flip), ti...  44.3 us
    ppermute x1, waiting for transfers between devices, body(): p01 = lax.ppermute(p00, 'x', swap)  12.2 us
    all_to_all x4, waiting for transfers between devices, exchange(): lax.all_to_all(x, AXES, 0, 0, axis_index_groups=groups_of(axes, flip), ti...  8.62 us
    ppermute x1, waiting for transfers between devices, body(): from_x = lax.ppermute(part, 'x', swap)  7.83 us
    ppermute x1, waiting for transfers between devices, body(): got = lax.ppermute(send, 'x', swap)  7.79 us
    pallas_call x1, Pallas kernels, body(): call(attn_kernel, [(8, 2, 2, 3 * BLOCK, HDIM), (2, 64, 16, HDIM), (2, 64,...  6.21 us
  transfers between devices with their start and end apart: 10, of which 7 were waited for; matrix products, arithmetic and copies ran while one was open for 0% of the time, Pallas kernels for 3%

profile of v8, /device:TPU:8, one launch (start us, length us, event | category | flops | bytes accessed | tf_op | source)
XLA Modules:
  0.0 96.6 jit_solution(2656267561335592889)
XLA Ops:
  0.6 1.6 %shard_map.120 = bf16[64,16,128]{2,1,0:T(8,128)(2,1)} custom-call(bf16[8,4096]{1,0:T(8,128)(2,1)} %k_ref.3, bf16[8,4096]{1,0:T(8,128)(2,1)} %v_ref.3), custom_call_target="tpu_custom_call" | custom-call | bytes 1048576 | tf_op jit(solution)/shard_map/pallas_call | solution.py:237
  2.2 0.0 copy-start
  2.2 0.0 copy-start.1
  2.2 0.0 copy-start.2
  2.2 0.0 copy-start.3
  2.2 15.4 %all-to-all-start.1 = ((bf16[64,16,128]{2,1,0:T(8,128)(2,1)}), bf16[64,16,128]{2,1,0:T(8,128)(2,1)S(1)}, u32[]{:S(2)}, u32[]{:S(2)}) async-start(bf16[64,16,128]{2,1,0:T(8,128)(2,1)} %shard_map.120), calls=%async_computation.1 | async-start | bytes 524288 | tf_op jit(solution)/shard_map/all_to_all | solution.py:216
  17.7 0.0 copy-done
  17.7 0.0 copy-done.1
  17.7 0.0 copy-done.2
  17.7 0.0 copy-done.3
  17.7 0.9 shard_map.119
  18.6 0.0 copy-start.4
  18.6 0.0 copy-start.5
  18.6 6.5 %all-to-all-done.1.p00_ref = bf16[64,16,128]{2,1,0:T(8,128)(2,1)S(1)} async-done(((bf16[64,16,128]{2,1,0:T(8,128)(2,1)}), bf16[64,16,128]{2,1,0:T(8,128)(2,1)S(1)}, u32[]{:S(2)}, u32[]{:S(2)}) %all-to-all-start.1) | async-done | bytes 262176 | tf_op jit(solution)/shard_map/all_to_all | solution.py:216
  25.2 8.3 %all-to-all-start = ((bf16[32,64,128]{2,1,0:T(8,128)(2,1)}), bf16[32,64,128]{2,1,0:T(8,128)(2,1)S(1)}, u32[]{:S(2)}, u32[]{:S(2)}) async-start(bf16[32,64,128]{2,1,0:T(8,128)(2,1)} %shard_map.119), calls=%async_computation | async-start | bytes 1048576 | tf_op jit(solution)/shard_map/all_to_all | solution.py:216
  33.5 1.6 %collective-permute-start = (bf16[64,16,128]{2,1,0:T(8,128)(2,1)S(1)}, bf16[64,16,128]{2,1,0:T(8,128)(2,1)S(1)}, u32[]{:S(2)}, u32[]{:S(2)}) collective-permute-start(bf16[64,16,128]{2,1,0:T(8,128)(2,1)S(1)} %all-to-all-done.1.p00_ref), channel_id=1, source_target_pairs={{0,16},{16,0},{1,17},{17,1},{2,18},{18,2},{3,19},{19,3},{4,20},{20... | collective-permute-start | bytes 786440 | tf_op jit(solution)/shard_map/ppermute | solution.py:239
  35.1 0.0 collective-permute-start.1
  35.1 12.2 %collective-permute-done.p01_ref = bf16[64,16,128]{2,1,0:T(8,128)(2,1)S(1)} collective-permute-done((bf16[64,16,128]{2,1,0:T(8,128)(2,1)S(1)}, bf16[64,16,128]{2,1,0:T(8,128)(2,1)S(1)}, u32[]{:S(2)}, u32[]{:S(2)}) %collective-permute-start) | collective-permute-done | bytes 262176 | tf_op jit(solution)/shard_map/ppermute | solution.py:239
  47.3 0.0 collective-permute-start.2
  47.3 0.0 collective-permute-done.1.p10_ref
  47.3 0.0 all-to-all-done.resp_ref
  47.3 1.5 %collective-permute-done.2.p11_ref = bf16[64,16,128]{2,1,0:T(8,128)(2,1)S(1)} collective-permute-done((bf16[64,16,128]{2,1,0:T(8,128)(2,1)S(1)}, bf16[64,16,128]{2,1,0:T(8,128)(2,1)S(1)}, u32[]{:S(2)}, u32[]{:S(2)}) %collective-permute-start.2) | collective-permute-done | bytes 262176 | tf_op jit(solution)/shard_map/ppermute | solution.py:241
  48.8 0.0 copy-done.4
  48.8 0.0 copy-done.5
  48.8 6.2 %shard_map.121 = (bf16[8,2,2,48,128]{4,3,2,1,0:T(8,128)(2,1)}, bf16[2,64,16,128]{3,2,1,0:T(8,128)(2,1)S(1)}, bf16[2,64,16,128]{3,2,1,0:T(8,128)(2,1)S(1)}) custom-call(f32[8]{0:T(128)S(1)} %copy-done.4, s32[8]{0:T(128)S(1)} %copy-done.5, bf16[32,64,128]{2,1,0:T(8,128)(2,1)S(1)} %all-to-all-done.resp_ref, bf16[64,16,128]{2,1,0:T(8,128)(2,1)S(1)} %all-to-all-done.1.p00_ref, ...), custom_call_target="tpu_custom_call" | custom-call | flops 1677721600 | bytes 3145728 | tf_op jit(solution)/shard_map/pallas_call | solution.py:248
  55.0 0.1 collective-permute-start.4
  55.2 7.2 %all-to-all-start.2 = ((bf16[16,2,48,128]{3,2,1,0:T(8,128)(2,1)}), bf16[16,2,48,128]{3,2,1,0:T(8,128)(2,1)S(1)}, u32[]{:S(2)}, u32[]{:S(2)}) async-start(bf16[16,2,48,128]{3,2,1,0:T(8,128)(2,1)} %bitcast), calls=%async_computation.2 | async-start | bytes 786432 | tf_op jit(solution)/shard_map/all_to_all | solution.py:216
  62.4 0.0 collective-permute-done.4.got_ref
  62.4 0.1 shard_map.124
  62.6 0.7 collective-permute-start.5
  63.2 7.8 %collective-permute-done.5.got_ref = bf16[64,16,128]{2,1,0:T(8,128)(2,1)S(1)} collective-permute-done((bf16[64,16,128]{2,1,0:T(8,128)(2,1)S(1)}, bf16[64,16,128]{2,1,0:T(8,128)(2,1)S(1)}, u32[]{:S(2)}, u32[]{:S(2)}) %collective-permute-start.5) | collective-permute-done | bytes 262176 | tf_op jit(solution)/shard_map/ppermute | solution.py:265
  71.0 0.8 shard_map.125
  71.8 0.8 all-to-all-done.2
  72.6 13.3 %all-to-all-start.3 = ((bf16[64,16,128]{2,1,0:T(8,128)(2,1)}), bf16[64,16,128]{2,1,0:T(8,128)(2,1)S(1)}, u32[]{:S(2)}, u32[]{:S(2)}) async-start(bf16[64,16,128]{2,1,0:T(8,128)(2,1)} %shard_map.125), calls=%async_computation.3 | async-start | bytes 524288 | tf_op jit(solution)/shard_map/all_to_all | solution.py:216
  85.9 0.1 collective-permute-start.3
  86.0 7.8 %collective-permute-done.3.from_x_ref = bf16[8,2,48,128]{3,2,1,0:T(8,128)(2,1)S(1)} collective-permute-done((bf16[8,2,48,128]{3,2,1,0:T(8,128)(2,1)S(1)}, bf16[8,2,48,128]{3,2,1,0:T(8,128)(2,1)S(1)}, u32[]{:S(2)}, u32[]{:S(2)}) %collective-permute-start.3) | collective-permute-done | bytes 196640 | tf_op jit(solution)/shard_map/ppermute | solution.py:272
  93.9 0.8 shard_map.123
  94.7 1.2 %all-to-all-done.3.got_ref = bf16[64,16,128]{2,1,0:T(8,128)(2,1)S(1)} async-done(((bf16[64,16,128]{2,1,0:T(8,128)(2,1)}), bf16[64,16,128]{2,1,0:T(8,128)(2,1)S(1)}, u32[]{:S(2)}, u32[]{:S(2)}) %all-to-all-start.3) | async-done | bytes 262176 | tf_op jit(solution)/shard_map/all_to_all | solution.py:216
  95.9 0.7 shard_map.126
  (1 shorter events, 0.0 us)
Async XLA Ops:
  2.2 15.5 %copy-start = (bf16[8,16,512]{2,1,0:T(8,128)(2,1)S(1)}, bf16[8,16,512]{2,1,0:T(8,128)(2,1)}, u32[]{:S(2)}) copy-start(bf16[8,16,512]{2,1,0:T(8,128)(2,1)} %q_ref.1) | copy-start | bytes 393220
  2.2 15.5 %copy-start.1 = (bf16[8,16,512]{2,1,0:T(8,128)(2,1)S(1)}, bf16[8,16,512]{2,1,0:T(8,128)(2,1)}, u32[]{:S(2)}) copy-start(bf16[8,16,512]{2,1,0:T(8,128)(2,1)} %k_ref.2) | copy-start | bytes 393220
  2.2 15.5 %copy-start.2 = (bf16[8,16,512]{2,1,0:T(8,128)(2,1)S(1)}, bf16[8,16,512]{2,1,0:T(8,128)(2,1)}, u32[]{:S(2)}) copy-start(bf16[8,16,512]{2,1,0:T(8,128)(2,1)} %v_ref.2) | copy-start | bytes 393220
  2.2 15.5 %copy-start.3 = (bf16[8,16,512]{2,1,0:T(8,128)(2,1)S(1)}, bf16[8,16,512]{2,1,0:T(8,128)(2,1)}, u32[]{:S(2)}) copy-start(bf16[8,16,512]{2,1,0:T(8,128)(2,1)} %o_ref.1) | copy-start | bytes 393220
  2.2 22.9 %all-to-all-start.1 = ((bf16[64,16,128]{2,1,0:T(8,128)(2,1)}), bf16[64,16,128]{2,1,0:T(8,128)(2,1)S(1)}, u32[]{:S(2)}, u32[]{:S(2)}) async-start(bf16[64,16,128]{2,1,0:T(8,128)(2,1)} %shard_map.120), calls=%async_computation.1 | async-start | bytes 524288 | tf_op jit(solution)/shard_map/all_to_all | solution.py:216
  18.6 30.2 %copy-start.4 = (f32[8]{0:T(128)S(1)}, f32[8]{0:T(128)}, u32[]{:S(2)}) copy-start(f32[8]{0:T(128)} %adv_ref.1) | copy-start | bytes 100
  18.6 30.2 %copy-start.5 = (s32[8]{0:T(128)S(1)}, s32[8]{0:T(128)}, u32[]{:S(2)}) copy-start(s32[8]{0:T(128)} %len_ref.1) | copy-start | bytes 100
  25.2 22.1 %all-to-all-start = ((bf16[32,64,128]{2,1,0:T(8,128)(2,1)}), bf16[32,64,128]{2,1,0:T(8,128)(2,1)S(1)}, u32[]{:S(2)}, u32[]{:S(2)}) async-start(bf16[32,64,128]{2,1,0:T(8,128)(2,1)} %shard_map.119), calls=%async_computation | async-start | bytes 1048576 | tf_op jit(solution)/shard_map/all_to_all | solution.py:216
  33.5 13.8 %collective-permute-start = (bf16[64,16,128]{2,1,0:T(8,128)(2,1)S(1)}, bf16[64,16,128]{2,1,0:T(8,128)(2,1)S(1)}, u32[]{:S(2)}, u32[]{:S(2)}) collective-permute-start(bf16[64,16,128]{2,1,0:T(8,128)(2,1)S(1)} %all-to-all-done.1.p00_ref), channel_id=1, source_target_pairs={{0,16},{16,0},{1,17},{17,1},{2,18},{18,2},{3,19},{19,3},{4,20},{20... | collective-permute-start | bytes 786440 | tf_op jit(solution)/shard_map/ppermute | solution.py:239
  35.1 12.2 %collective-permute-start.1 = (bf16[64,16,128]{2,1,0:T(8,128)(2,1)S(1)}, bf16[64,16,128]{2,1,0:T(8,128)(2,1)S(1)}, u32[]{:S(2)}, u32[]{:S(2)}) collective-permute-start(bf16[64,16,128]{2,1,0:T(8,128)(2,1)S(1)} %all-to-all-done.1.p00_ref), channel_id=1, source_target_pairs={{0,8},{8,0},{1,9},{9,1},{2,10},{10,2},{3,11},{11,3},{4,12},{12,4},... | collective-permute-start | bytes 786440 | tf_op jit(solution)/shard_map/ppermute | solution.py:240
  47.3 1.5 %collective-permute-start.2 = (bf16[64,16,128]{2,1,0:T(8,128)(2,1)S(1)}, bf16[64,16,128]{2,1,0:T(8,128)(2,1)S(1)}, u32[]{:S(2)}, u32[]{:S(2)}) collective-permute-start(bf16[64,16,128]{2,1,0:T(8,128)(2,1)S(1)} %collective-permute-done.p01_ref), channel_id=1, source_target_pairs={{0,8},{8,0},{1,9},{9,1},{2,10},{10,2},{3,11},{11,3},{4,12},{12,4},... | collective-permute-start | bytes 786440 | tf_op jit(solution)/shard_map/ppermute | solution.py:241
  55.0 7.4 %collective-permute-start.4 = (bf16[2,64,16,128]{3,2,1,0:T(8,128)(2,1)S(1)}, bf16[2,64,16,128]{3,2,1,0:T(8,128)(2,1)S(1)}, u32[]{:S(2)}, u32[]{:S(2)}) collective-permute-start(bf16[2,64,16,128]{3,2,1,0:T(8,128)(2,1)S(1)} %get-tuple-element.21), channel_id=1, source_target_pairs={{0,8},{8,0},{1,9},{9,1},{2,10},{10,2},{3,11},{11,3},{4,12},{12,4},... | collective-permute-start | bytes 1572872 | tf_op jit(solution)/shard_map/ppermute | solution.py:263
  55.2 17.4 %all-to-all-start.2 = ((bf16[16,2,48,128]{3,2,1,0:T(8,128)(2,1)}), bf16[16,2,48,128]{3,2,1,0:T(8,128)(2,1)S(1)}, u32[]{:S(2)}, u32[]{:S(2)}) async-start(bf16[16,2,48,128]{3,2,1,0:T(8,128)(2,1)} %bitcast), calls=%async_computation.2 | async-start | bytes 786432 | tf_op jit(solution)/shard_map/all_to_all | solution.py:216
  62.6 8.4 %collective-permute-start.5 = (bf16[64,16,128]{2,1,0:T(8,128)(2,1)S(1)}, bf16[64,16,128]{2,1,0:T(8,128)(2,1)S(1)}, u32[]{:S(2)}, u32[]{:S(2)}) collective-permute-start(bf16[64,16,128]{2,1,0:T(8,128)(2,1)S(1)} %get-tuple-element.23), channel_id=1, source_target_pairs={{0,16},{16,0},{1,17},{17,1},{2,18},{18,2},{3,19},{19,3},{4,20},{20... | collective-permute-start | bytes 786440 | tf_op jit(solution)/shard_map/ppermute | solution.py:265
  72.6 23.3 %all-to-all-start.3 = ((bf16[64,16,128]{2,1,0:T(8,128)(2,1)}), bf16[64,16,128]{2,1,0:T(8,128)(2,1)S(1)}, u32[]{:S(2)}, u32[]{:S(2)}) async-start(bf16[64,16,128]{2,1,0:T(8,128)(2,1)} %shard_map.125), calls=%async_computation.3 | async-start | bytes 524288 | tf_op jit(solution)/shard_map/all_to_all | solution.py:216
  85.9 7.9 %collective-permute-start.3 = (bf16[8,2,48,128]{3,2,1,0:T(8,128)(2,1)S(1)}, bf16[8,2,48,128]{3,2,1,0:T(8,128)(2,1)S(1)}, u32[]{:S(2)}, u32[]{:S(2)}) collective-permute-start(bf16[8,2,48,128]{3,2,1,0:T(8,128)(2,1)S(1)} %shard_map.122), channel_id=1, source_target_pairs={{0,16},{16,0},{1,17},{17,1},{2,18},{18,2},{3,19},{19,3},{4,20},{20... | collective-permute-start | bytes 589832 | tf_op jit(solution)/shard_map/ppermute | solution.py:272
